TPU v7x, 256 devices: a whole 4x4x8 slice. The times are simulated.
256 devices in a mesh: pt: 8 (over x, z_hi), pan: 32 (over y, z_lo, core).
Axes of the slice: x: 4, y: 4, z: 8 (z_hi: 2, z_lo: 4; z = z_hi * 4 + z_lo), core: 2. Of those that a mesh axis runs over, the one named last changes fastest.
Arguments:
- potential: bfloat16 [8, 6144, 6144], P('pt', 'pan'), may hold values from -6 to 6
- basis: bfloat16 [6144, 1280], P(None, 'pan'), may hold values from -0.078125 to 0.078125
- weights: float32 [8], replicated, may hold values from 0.05 to 0.3
- coupling: float32 [8, 8], replicated, may hold values from -0.03 to 0.03
Outputs:
- exponent: float32 [1280, 1280], P('pan', 'pt')
All inputs are finite; a program needn't handle non-finite values.
Results may differ from a plain program's by a relative error of at most 0.02.
Values may be sent and summed in bfloat16 or wider, within the bound.
No kernel may reach another device: no remote copies, remote signals or barrier semaphores. Data moves between devices by JAX's collectives and lax.ppermute only.
A program may use at most 64 MiB of HBM per device.

v0:
```python
import jax
import jax.numpy as jnp
from jax import lax
from jax.sharding import PartitionSpec as P


def shards(potential, basis, weights, coupling):
    row_count = potential.shape[1]
    point_idx = lax.axis_index("pt")
    block_idx = lax.axis_index("pan")
    row_start = block_idx * row_count
    local_rows = potential[0]
    segment = lax.all_gather(basis, "pan", axis=1, tiled=True)
    partial_value = jnp.dot(local_rows, segment, preferred_element_type=jnp.float32)
    own_rows = lax.dynamic_slice_in_dim(segment, row_start, row_count, 0).astype(jnp.float32)
    joined = jnp.concatenate([partial_value, own_rows], axis=0)
    projected = joined[:row_count].astype(jnp.bfloat16)
    own_basis = joined[row_count:].astype(jnp.bfloat16)
    channel_rows = lax.psum_scatter(
        jnp.dot(projected.T, own_basis, preferred_element_type=jnp.float32),
        "pan",
        scatter_dimension=0,
        tiled=True,
    ).astype(jnp.bfloat16)
    antisym = coupling - coupling.T
    gathered = lax.all_gather(channel_rows[None], "pt", axis=0, tiled=True)
    coeffs = lax.dynamic_index_in_dim(antisym, point_idx, 0, keepdims=False)
    mixed_rows = jnp.einsum("r,rij->ij", coeffs, gathered.astype(jnp.float32))
    mixed_rows = mixed_rows.astype(jnp.bfloat16)
    product = jnp.dot(
        mixed_rows,
        lax.all_gather(channel_rows, "pan", axis=0, tiled=True),
        preferred_element_type=jnp.float32,
    )
    weight_own = lax.dynamic_index_in_dim(weights, point_idx, 0, keepdims=False)
    contribution = weight_own * channel_rows.astype(jnp.float32) + product
    return lax.psum_scatter(
        contribution.astype(jnp.bfloat16), "pt", scatter_dimension=1, tiled=True
    ).astype(jnp.float32)


def solution(mesh):
    in_specs = (P("pt", "pan", None), P(None, "pan"), P(), P())
    out_specs = P("pan", "pt")
    return jax.shard_map(shards, mesh=mesh, in_specs=in_specs, out_specs=out_specs, check_vma=False)
```

profile of v0, /device:TPU:1, one launch (start us, length us, event | category | flops | bytes accessed | tf_op | source)
XLA Modules:
  0.0 442.8 jit_solution(13575291728012141183)
XLA Ops:
  6.5 0.0 copy-start
  6.5 0.0 all-gather.4.cloned.1.call-start
  6.5 0.7 all-gather.4.cloned.1.call-update
  7.3 0.0 reduce-scatter.5.cloned.1.call-start
  7.3 100.6 %all-gather.4.cloned.1.call-done = bf16[6144,1280]{0,1:T(8,128)(2,1)} async-done(((bf16[6144,40]{0,1:T(8,128)(2,1)}), bf16[6144,1280]{0,1:T(8,128)(2,1)}) %all-gather.4.cloned.1.call-update) | async-done | bytes 15728656 | tf_op jit(solution)/shard_map/all_gather | solution.py:13
  107.9 0.0 copy-done
  107.9 16.0 %fusion.3 = f32[1280,1280]{1,0:T(8,128)} fusion(bf16[6144,1280]{0,1:T(8,128)(2,1)} %all-gather.4.cloned.1.call-done, bf16[1,192,6144]{2,1,0:T(8,128)(2,1)S(1)} %copy-done, s32[]{:T(128)S(6)} %select_n.10), kind=kOutput, calls=%fused_computation.4 | convolution fusion | flops 3649290240 | bytes 25296900 | tf_op jit(solution)/shard_map/dot_general | solution.py:20
  124.0 0.0 reduce-scatter.5.cloned.1.call-update
  124.0 0.0 all-gather.6.cloned.1.call-start
  124.1 154.6 %reduce-scatter.5.cloned.1.call-done = f32[40,1280]{1,0:T(8,128)} async-done(((f32[1280,1280]{1,0:T(8,128)}), f32[40,1280]{1,0:T(8,128)}) %reduce-scatter.5.cloned.1.call-update) | async-done | bytes 204816 | tf_op jit(solution)/shard_map/reduce_scatter | solution.py:19
  278.7 1.6 convert_element_type.22
  280.3 0.0 all-gather.6.cloned.1.call-update
  280.3 0.0 reduce-scatter.7.cloned.1.call-start
  280.4 0.1 copy.6
  280.4 0.6 dynamic_slice.11
  281.0 49.6 %all-gather = bf16[320,1280]{1,0:T(8,128)(2,1)S(1)} all-gather(bf16[40,1280]{1,0:T(8,128)(2,1)} %convert_element_type.22), channel_id=2, replica_groups=mesh['pt'=8,'pan'=32] {'pt'}, dimensions={0}, use_global_device_ids=true | all-gather | bytes 921600 | tf_op jit(solution)/shard_map/all_gather | solution.py:26
  330.6 0.4 fusion.5
  331.0 17.2 %all-gather.6.cloned.1.call-done = bf16[1280,1280]{1,0:T(8,128)(2,1)} async-done(((bf16[40,1280]{1,0:T(8,128)(2,1)}), bf16[1280,1280]{1,0:T(8,128)(2,1)}) %all-gather.6.cloned.1.call-update) | async-done | bytes 3276816 | tf_op jit(solution)/shard_map/all_gather | solution.py:32
  348.2 3.3 fusion.1
  351.4 0.9 copy.9
  352.3 0.0 reduce-scatter.7.cloned.1.call-update
  352.4 82.4 %reduce-scatter.7.cloned.1.call-done = bf16[160,40]{1,0:T(8,128)(2,1)} async-done(((bf16[1280,40]{1,0:T(8,128)(2,1)}), bf16[160,40]{1,0:T(8,128)(2,1)}) %reduce-scatter.7.cloned.1.call-update) | async-done | bytes 12816
  434.8 0.8 copy.10
  435.6 0.6 convert_element_type.26
  (5 shorter events, 0.0 us)
Async XLA Ops:
  6.5 101.4 %copy-start = (bf16[1,192,6144]{2,1,0:T(8,128)(2,1)S(1)}, bf16[1,192,6144]{2,1,0:T(8,128)(2,1)}, u32[]{:S(2)}) copy-start(bf16[1,192,6144]{2,1,0:T(8,128)(2,1)} %param.4) | copy-start | bytes 7077892
  6.5 101.4 %all-gather.4.cloned.1.call-start = ((), (), s32[]{:S(2)}) async-start(), calls=%async_computation.2 | async-start | bytes 16220160 | tf_op jit(solution)/shard_map/all_gather | solution.py:13
  7.3 271.4 %reduce-scatter.5.cloned.1.call-start = ((), (), s32[]{:S(2)}) async-start(), calls=%async_computation.3 | async-start | bytes 6758400 | tf_op jit(solution)/shard_map/reduce_scatter | solution.py:19
  124.0 156.4 %copy-start.1 = (f32[8,8]{1,0:T(8,128)S(1)}, f32[8,8]{1,0:T(8,128)}, u32[]{:S(2)}) copy-start(f32[8,8]{1,0:T(8,128)} %param.7) | copy-start | bytes 772
  124.0 156.5 %copy-start.2 = (f32[8]{0:T(128)S(1)}, f32[8]{0:T(128)}, u32[]{:S(2)}) copy-start(f32[8]{0:T(128)} %param.6) | copy-start | bytes 100
  124.0 224.2 %all-gather.6.cloned.1.call-start = ((), (), s32[]{:S(2)}) async-start(), calls=%async_computation.4 | async-start | bytes 3379200 | tf_op jit(solution)/shard_map/all_gather | solution.py:32
  280.3 154.5 %reduce-scatter.7.cloned.1.call-start = ((), (), s32[]{:S(2)}) async-start(), calls=%async_computation.5 | async-start | bytes 368640
Sparse Core Ops, SparseCore 0:
  9.2 98.6 all-gather.3
  124.1 154.4 reduce-scatter.4
  280.5 67.6 all-gather.5
  352.5 82.2 reduce-scatter.6
where the time goes:
time: 444 us; the launch traced here: 443 us
  waiting for transfers between devices  356 us (80%)
  blocking collectives  49.6 us (11%)
  matrix products  19.7 us (4%)
  between operations  13.2 us (3%)
    reduce_scatter x1, waiting for transfers between devices, shards(): lax.psum_scatter(jnp.dot(projected.T, own_basis, preferred_element_type=j...  155 us
    all_gather x1, waiting for transfers between devices, shards(): segment = lax.all_gather(basis, 'pan', axis=1, tiled=True)  101 us
    unnamed x5, waiting for transfers between devices  83.2 us
    all_gather x1, blocking collectives, shards(): gathered = lax.all_gather(channel_rows[None], 'pt', axis=0, tiled=True)  49.6 us
    all_gather x1, waiting for transfers between devices, shards(): lax.all_gather(channel_rows, 'pan', axis=0, tiled=True)  17.2 us
    dot_general x1, matrix products, shards(): jnp.dot(projected.T, own_basis, preferred_element_type=jnp.float32)  16 us
  transfers between devices with their start and end apart: 4, of which 4 were waited for; matrix products, arithmetic and copies ran while one was open for 0% of the time, Pallas kernels for 0%

commit v1 on v0

v1 whole, which is shorter than its diff:
```python
import jax
import jax.numpy as jnp
from jax import lax
from jax.sharding import PartitionSpec as P

BF = jnp.bfloat16
F32 = jnp.float32
AXES = ("pt", "pan")


def place(x, y, z, c):
    return ((x % 4) * 2 + (z % 8) // 4) * 32 + (y % 4) * 8 + (z % 4) * 2 + c


def pairs(move):
    return [
        (place(x, y, z, c), place(*move(x, y, z, c)))
        for x in range(4) for y in range(4) for z in range(8) for c in range(2)
    ]


def along(first, ring):
    def z_move(z, step):
        return z + step if ring else z // 4 * 4 + (z + step) % 4

    def perm(step):
        return pairs(
            lambda x, y, z, c: (x, y, z_move(z, step(z)), c) if (c == 0) == first else (x, y + step(y), z, c)
        )

    return perm


UP = lambda v: 1
DOWN = lambda v: -1
TWO = lambda v: 2 if v % 2 == 0 else -2
CORE = pairs(lambda x, y, z, c: (x, y, z, 1 - c))
CHIPS = [[2 * chip + core for chip in range(16)] for core in range(2)]


def send(value, perm):
    return lax.ppermute(value, AXES, perm)


def gather_line(value, axis):
    up = send(value, axis(UP))
    down = send(value, axis(DOWN))
    two = send(value, axis(TWO))
    return value, down, two, up


def nt(a, b):
    return lax.dot_general(a, b, (((1,), (1,)), ((), ())), preferred_element_type=F32)


def unroll(blocks, start):
    return lax.dynamic_slice_in_dim(jnp.concatenate([blocks, blocks], 0), (4 - start) % 4, 4, 0)


def shards(potential, basis, weights, coupling):
    point = lax.axis_index("pt")
    pan = lax.axis_index("pan")
    core = pan % 2
    chip = pan // 2
    y, z = chip // 4, chip % 4
    second = jnp.where(core == 0, y, z)
    first = jnp.where(core == 0, z, y)
    rows = potential[0]
    panel = basis.T
    width, depth = panel.shape

    with jax.named_scope("basis_line"):
        line = jnp.concatenate(gather_line(panel, along(True, True)), 0)
    with jax.named_scope("rows_pair"):
        other_rows = send(rows, CORE)
        chip_rows = jnp.where(
            core == 0, jnp.concatenate([rows, other_rows], 0), jnp.concatenate([other_rows, rows], 0)
        )
    with jax.named_scope("basis_plane"):
        units = gather_line(line, along(False, True))
    with jax.named_scope("projected"):
        parts = [unroll(nt(u, chip_rows).astype(BF).reshape(4, width, -1), first) for u in units]
        blocks = unroll(jnp.stack(parts), second)
        blocks = jnp.where(core == 0, blocks, blocks.transpose(1, 0, 2, 3)).reshape(16, width, -1)
    with jax.named_scope("projected_exchange"):
        got = lax.all_to_all(blocks, "pan", 0, 0, axis_index_groups=CHIPS, tiled=True)
        own = got.transpose(1, 0, 2).reshape(width, depth)
        both = jnp.concatenate([own, send(own, CORE)], 0)
    with jax.named_scope("channel"):
        channel = jnp.concatenate([nt(both, u).astype(BF) for u in units], 1)
    with jax.named_scope("points"):
        every = lax.all_to_all(jnp.broadcast_to(channel, (8,) + channel.shape), "pt", 0, 0, tiled=True)
        every = every.reshape(8, 2 * width, 16 * width)
        every_other = send(every, CORE)
    with jax.named_scope("select"):
        lane = jnp.arange(2 * width)
        want = 2 * point + lane // width
        dy, dz = (want // 4 - y) % 4, (want % 4 - z) % 4
        spot = (jnp.where(core == 0, dy * 4 + dz, dz * 4 + dy)) * width + lane % width
        pick = (jnp.arange(16 * width)[:, None] == spot[None, :]).astype(BF)
        chosen = jnp.dot(every.reshape(-1, 16 * width), pick, preferred_element_type=F32)
        chosen = chosen.reshape(8, 2 * width, 2 * width)
        antisym = coupling - coupling.T
        mixed = jnp.einsum("qr,qin->irn", antisym, chosen, precision=lax.Precision.HIGHEST)
        mixed = mixed.astype(BF).reshape(2 * width, -1)
        linear = jnp.einsum("q,qin->in", weights, chosen, precision=lax.Precision.HIGHEST)
    with jax.named_scope("mixed_gather"):
        mline = jnp.concatenate(gather_line(mixed, along(True, False)), 0)
        mplane = jnp.stack(gather_line(mline, along(False, False)))
    with jax.named_scope("product"):
        right = mplane.reshape(4, 4, 2, width, 8, 2 * width)
        right_own = right[:, :, 0].transpose(3, 0, 1, 2, 4).reshape(8, 16 * width, 2 * width)
        right_other = right[:, :, 1].transpose(3, 1, 0, 2, 4).reshape(8, 16 * width, 2 * width)
        total, crossed = linear, 0.0
        for r in range(8):
            total = total + jnp.dot(every[r], right_own[r], preferred_element_type=F32)
            crossed = crossed + jnp.dot(every_other[r], right_other[r], preferred_element_type=F32)
        total = total + jnp.concatenate([crossed[width:], crossed[:width]], 0)
    with jax.named_scope("output"):
        mine = total[:width].reshape(width, 2, 1, width)
        theirs = send(total[width:], CORE).reshape(width, 2, 1, width)
        out = jnp.where(
            core == 0, jnp.concatenate([mine, theirs], 2), jnp.concatenate([theirs, mine], 2)
        )
        return out.reshape(width, 4 * width)


def solution(mesh):
    in_specs = (P("pt", "pan", None), P(None, "pan"), P(), P())
    return jax.shard_map(shards, mesh=mesh, in_specs=in_specs, out_specs=P("pan", "pt"), check_vma=False)
```

time: 444 us -> 200 us (0.45)
  waiting for transfers between devices: 356 us -> 75.5 us
  starting transfers between devices: 0.12 us -> 41.2 us
  blocking collectives: 49.6 us -> 14.6 us
  local copies, waits for them, and re-layouts: 2.4 us -> 25.9 us
  matrix products: 19.7 us -> 36 us
  between operations: 13.2 us -> 0.51 us
    reduce_scatter x1 -> x0, waiting for transfers between devices: 155 us -> none  [shards(): lax.psum_scatter(jnp.dot(projected.T, own_basis, preferred_element_type=j...]
    all_gather x2 -> x0, waiting for transfers between devices: 118 us -> none  [the longest x1 101 us: shards(): segment = lax.all_gather(basis, 'pan', axis=1, tiled=True)]
    unnamed x5 -> x0, waiting for transfers between devices: 83.2 us -> none
    ppermute x0 -> x16, waiting for transfers between devices: none -> 54.2 us  [send(): return lax.ppermute(value, AXES, perm)]
    all_gather x1 -> x0, blocking collectives: 49.6 us -> none  [shards(): gathered = lax.all_gather(channel_rows[None], 'pt', axis=0, tiled=True)]
    ppermute x0 -> x16, starting transfers between devices: none -> 33.1 us  [send(): return lax.ppermute(value, AXES, perm)]
    all_to_all x0 -> x1, waiting for transfers between devices: none -> 21.3 us  [shards(): lax.all_to_all(jnp.broadcast_to(channel, (8,) + channel.shape), 'pt', 0,...]
    dot_general x3 -> x27, matrix products: 19.7 us -> 36 us  [the longest x8 24.6 us: nt(): lax.dot_general(a, b, (((1,), (1,)), ((), ())), preferred_element_type=F32)]
  transfers between devices with their start and end apart: 4 -> 17, of which waited for: 4 -> 8; matrix products, arithmetic and copies ran while one was open for 0% -> 21% of each run, Pallas kernels for 0% -> 0%
where the time goes in v1:
time: 200 us; the launch traced here: 196 us
  waiting for transfers between devices  75.5 us (38%)
  starting transfers between devices  41.2 us (21%)
  matrix products  36 us (18%)
  local copies, waits for them, and re-layouts  25.9 us (13%)
  blocking collectives  14.6 us (7%)
  other arithmetic  2.03 us (1%)
    ppermute x16, waiting for transfers between devices, send(): return lax.ppermute(value, AXES, perm)  54.2 us
    ppermute x16, starting transfers between devices, send(): return lax.ppermute(value, AXES, perm)  33.1 us
    dot_general x8, matrix products, nt(): lax.dot_general(a, b, (((1,), (1,)), ((), ())), preferred_element_type=F32)  24.6 us
    all_to_all x1, waiting for transfers between devices, shards(): lax.all_to_all(jnp.broadcast_to(channel, (8,) + channel.shape), 'pt', 0,...  21.3 us
    all_to_all x1, blocking collectives, shards(): lax.all_to_all(blocks, 'pan', 0, 0, axis_index_groups=CHIPS, tiled=True)  14.6 us
    another operation x5, local copies, waits for them, and re-layouts, shards(): mplane = jnp.stack(gather_line(mline, along(False, False)))  11.3 us
    dot_general x8, matrix products, shards(): jnp.dot(every_other[r], right_other[r], preferred_element_type=F32)  8.55 us
    all_to_all x1, starting transfers between devices, shards(): lax.all_to_all(jnp.broadcast_to(channel, (8,) + channel.shape), 'pt', 0,...  8.06 us
  transfers between devices with their start and end apart: 17, of which 8 were waited for; matrix products, arithmetic and copies ran while one was open for 21% of the time, Pallas kernels for 0%

profile of v1, /device:TPU:1, one launch (start us, length us, event | category | flops | bytes accessed | tf_op | source)
XLA Modules:
  0.0 195.7 jit_solution(9579265416876993732)
XLA Ops:
  0.0 3.2 %collective-permute-start.3 = (bf16[192,6144]{1,0:T(8,128)(2,1)}, bf16[192,6144]{1,0:T(8,128)(2,1)}, u32[]{:S(2)}, u32[]{:S(2)}) collective-permute-start(bf16[192,6144]{1,0:T(8,128)(2,1)} %bitcast.188), channel_id=1, source_target_pairs={{0,1},{1,0},{2,3},{3,2},{4,5},{5,4},{6,7},{7,6},{32,33},{33,32},{3... | collective-permute-start | bytes 7077896 | tf_op jit(solution)/shard_map/rows_pair/ppermute | solution.py:42
  6.5 11.4 %collective-permute-done.2 = bf16[40,6144]{1,0:T(8,128)(2,1)S(1)} collective-permute-done((bf16[40,6144]{1,0:T(8,128)(2,1)}, bf16[40,6144]{1,0:T(8,128)(2,1)S(1)}, u32[]{:S(2)}, u32[]{:S(2)}) %collective-permute-start.2) | collective-permute-done | bytes 491552 | tf_op jit(solution)/shard_map/basis_line/ppermute | solution.py:42
  19.7 4.2 %collective-permute-start.4 = (bf16[160,6144]{1,0:T(8,128)(2,1)S(1)}, bf16[160,6144]{1,0:T(8,128)(2,1)}, u32[]{:S(2)}, u32[]{:S(2)}) collective-permute-start(bf16[160,6144]{1,0:T(8,128)(2,1)S(1)} %pad_maximum_fusion), channel_id=1, source_target_pairs={{0,24},{1,39},{2,26},{3,1},{4,28},{5,3},{6,30},{7,5},{32,56},{33,7... | collective-permute-start | bytes 5898248 | tf_op jit(solution)/shard_map/basis_plane/ppermute | solution.py:42
  25.9 4.9 %convolution_convert_fusion.4 = bf16[160,384]{1,0:T(8,128)(2,1)S(1)} fusion(bf16[160,6144]{1,0:T(8,128)(2,1)S(1)} %pad_maximum_fusion, bf16[192,6144]{1,0:T(8,128)(2,1)} %collective-permute-done.3, bf16[192,6144]{1,0:T(8,128)(2,1)} %bitcast.189, pred[]{:T(512)S(6)} %eq.34), kind=kOutput, calls=%fused_computation.8 | convolution fusion | flops 776269824 | bytes 6807553 | tf_op jit(solution)/shard_map/projected/dot_general | solution.py:53
  30.8 35.8 %collective-permute-done.4 = bf16[160,6144]{1,0:T(8,128)(2,1)} collective-permute-done((bf16[160,6144]{1,0:T(8,128)(2,1)S(1)}, bf16[160,6144]{1,0:T(8,128)(2,1)}, u32[]{:S(2)}, u32[]{:S(2)}) %collective-permute-start.4) | collective-permute-done | bytes 1966112 | tf_op jit(solution)/shard_map/basis_plane/ppermute | solution.py:42
  66.6 4.7 %convolution_convert_fusion.3 = bf16[160,384]{1,0:T(8,128)(2,1)S(1)} fusion(bf16[160,6144]{1,0:T(8,128)(2,1)} %collective-permute-done.4, bf16[192,6144]{1,0:T(8,128)(2,1)} %collective-permute-done.3, bf16[192,6144]{1,0:T(8,128)(2,1)S(1)} %bitcast.190, pred[]{:T(512)S(6)} %eq.34), kind=kOutput, calls=%fused_computation.7 | convolution fusion | flops 776269824 | bytes 6807553 | tf_op jit(solution)/shard_map/projected/dot_general | solution.py:53
  71.3 4.7 %convolution_convert_fusion.2 = bf16[160,384]{1,0:T(8,128)(2,1)S(1)} fusion(bf16[160,6144]{1,0:T(8,128)(2,1)} %collective-permute-done.5, bf16[192,6144]{1,0:T(8,128)(2,1)} %collective-permute-done.3, bf16[192,6144]{1,0:T(8,128)(2,1)S(1)} %bitcast.191, pred[]{:T(512)S(6)} %eq.34), kind=kOutput, calls=%fused_computation.6 | convolution fusion | flops 776269824 | bytes 6807553 | tf_op jit(solution)/shard_map/projected/dot_general | solution.py:53
  76.1 4.2 %convolution_convert_fusion.1 = bf16[160,384]{1,0:T(8,128)(2,1)S(1)} fusion(bf16[160,6144]{1,0:T(8,128)(2,1)S(1)} %collective-permute-done.6, bf16[192,6144]{1,0:T(8,128)(2,1)} %collective-permute-done.3, bf16[192,6144]{1,0:T(8,128)(2,1)S(1)} %bitcast.192, pred[]{:T(512)S(6)} %eq.34), kind=kOutput, calls=%fused_computation.5 | convolution fusion | flops 776269824 | bytes 6807553 | tf_op jit(solution)/shard_map/projected/dot_general | solution.py:53
  80.8 14.6 %all_to_all.10 = bf16[16,40,384]{2,1,0:T(8,128)(2,1)S(1)} all-to-all(bf16[16,40,384]{2,1,0:T(8,128)(2,1)S(1)} %bitcast.155), channel_id=1, replica_groups={{0,2,4,6,8,10,12,14,16,18,20,22,24,26,28,30},{1,3,5,7,9,11,13,15,17,19,..., dimensions={0} | all-to-all | bytes 983040 | tf_op jit(solution)/shard_map/projected_exchange/all_to_all | solution.py:86
  95.4 7.8 %collective-permute-start.7 = (bf16[40,6144]{1,0:T(8,128)(2,1)S(1)}, bf16[40,6144]{1,0:T(8,128)(2,1)S(1)}, u32[]{:S(2)}, u32[]{:S(2)}) collective-permute-start(bf16[40,6144]{1,0:T(8,128)(2,1)S(1)} %bitcast.156), channel_id=1, source_target_pairs={{0,1},{1,0},{2,3},{3,2},{4,5},{5,4},{6,7},{7,6},{32,33},{33,32},{3... | collective-permute-start | bytes 1474568 | tf_op jit(solution)/shard_map/projected_exchange/ppermute | solution.py:42
  106.3 2.3 %convolution_convert_fusion.6 = bf16[80,160]{1,0:T(8,128)(2,1)S(1)} fusion(bf16[80,6144]{1,0:T(8,128)(2,1)S(1)} %constant_dynamic-update-slice_fusion.8, bf16[160,6144]{1,0:T(8,128)(2,1)} %collective-permute-done.5), kind=kOutput, calls=%fused_computation.11 | convolution fusion | flops 157299200 | bytes 2974720 | tf_op jit(solution)/shard_map/channel/dot_general | solution.py:53
  108.7 2.3 %convolution_convert_fusion.7 = bf16[80,160]{1,0:T(8,128)(2,1)S(1)} fusion(bf16[80,6144]{1,0:T(8,128)(2,1)S(1)} %constant_dynamic-update-slice_fusion.8, bf16[160,6144]{1,0:T(8,128)(2,1)} %collective-permute-done.4), kind=kOutput, calls=%fused_computation.12 | convolution fusion | flops 157299200 | bytes 2974720 | tf_op jit(solution)/shard_map/channel/dot_general | solution.py:53
  112.1 8.1 %all-to-all-start.1 = ((bf16[8,80,640]{2,1,0:T(8,128)(2,1)}), bf16[8,80,640]{2,1,0:T(8,128)(2,1)S(1)}, u32[]{:S(2)}, u32[]{:S(2)}) async-start(bf16[8,80,640]{2,1,0:T(8,128)(2,1)} %broadcast_in_dim.2), calls=%async_computation.1 | async-start | bytes 1638400 | tf_op jit(solution)/shard_map/points/all_to_all | solution.py:92
  120.2 21.3 %all-to-all-done.1 = bf16[8,80,640]{2,1,0:T(8,128)(2,1)S(1)} async-done(((bf16[8,80,640]{2,1,0:T(8,128)(2,1)}), bf16[8,80,640]{2,1,0:T(8,128)(2,1)S(1)}, u32[]{:S(2)}, u32[]{:S(2)}) %all-to-all-start.1) | async-done | bytes 819232 | tf_op jit(solution)/shard_map/points/all_to_all | solution.py:92
  146.0 3.1 %collective-permute-done.8 = bf16[80,640]{1,0:T(8,128)(2,1)S(1)} collective-permute-done((bf16[80,640]{1,0:T(8,128)(2,1)S(1)}, bf16[80,640]{1,0:T(8,128)(2,1)S(1)}, u32[]{:S(2)}, u32[]{:S(2)}) %collective-permute-start.8) | collective-permute-done | bytes 102432 | tf_op jit(solution)/shard_map/mixed_gather/ppermute | solution.py:42
  151.1 3.7 %collective-permute-start.12 = (bf16[320,640]{1,0:T(8,128)(2,1)}, bf16[320,640]{1,0:T(8,128)(2,1)}, u32[]{:S(2)}, u32[]{:S(2)}) collective-permute-start(bf16[320,640]{1,0:T(8,128)(2,1)} %constant_dynamic-update-slice_fusion.10), channel_id=1, source_target_pairs={{0,16},{1,5},{2,18},{3,7},{4,20},{5,1},{6,22},{7,3},{32,48},{33,37... | collective-permute-start | bytes 1228808 | tf_op jit(solution)/shard_map/mixed_gather/ppermute | solution.py:42
  154.8 2.5 %collective-permute-start.11 = (bf16[320,640]{1,0:T(8,128)(2,1)}, bf16[320,640]{1,0:T(8,128)(2,1)}, u32[]{:S(2)}, u32[]{:S(2)}) collective-permute-start(bf16[320,640]{1,0:T(8,128)(2,1)} %constant_dynamic-update-slice_fusion.10), channel_id=1, source_target_pairs={{0,24},{1,7},{2,26},{3,1},{4,28},{5,3},{6,30},{7,5},{32,56},{33,39... | collective-permute-start | bytes 1228808 | tf_op jit(solution)/shard_map/mixed_gather/ppermute | solution.py:42
  157.7 2.6 %collective-permute-start.14 = (bf16[8,80,640]{2,1,0:T(8,128)(2,1)S(1)}, bf16[8,80,640]{2,1,0:T(8,128)(2,1)}, u32[]{:S(2)}, u32[]{:S(2)}) collective-permute-start(bf16[8,80,640]{2,1,0:T(8,128)(2,1)S(1)} %all-to-all-done.1), channel_id=1, source_target_pairs={{0,1},{1,0},{2,3},{3,2},{4,5},{5,4},{6,7},{7,6},{32,33},{33,32},{3... | collective-permute-start | bytes 2457608 | tf_op jit(solution)/shard_map/points/ppermute | solution.py:42
  160.3 2.5 %stack.32 = bf16[1,4,2,40,8,80]{5,4,3,2,1,0:T(8,128)(2,1)} reshape(bf16[320,640]{1,0:T(8,128)(2,1)} %constant_dynamic-update-slice_fusion.10) | data formatting | bytes 819200 | tf_op jit(solution)/shard_map/mixed_gather/stack | solution.py:109
  165.1 2.5 %stack.34 = bf16[1,4,2,40,8,80]{5,4,3,2,1,0:T(8,128)(2,1)} reshape(bf16[320,640]{1,0:T(8,128)(2,1)} %collective-permute-done.12) | data formatting | bytes 819200 | tf_op jit(solution)/shard_map/mixed_gather/stack | solution.py:109
  167.7 2.5 %stack.33 = bf16[1,4,2,40,8,80]{5,4,3,2,1,0:T(8,128)(2,1)} reshape(bf16[320,640]{1,0:T(8,128)(2,1)} %collective-permute-done.11) | data formatting | bytes 819200 | tf_op jit(solution)/shard_map/mixed_gather/stack | solution.py:109
  172.5 2.5 %stack.35 = bf16[1,4,2,40,8,80]{5,4,3,2,1,0:T(8,128)(2,1)} reshape(bf16[320,640]{1,0:T(8,128)(2,1)} %collective-permute-done.13) | data formatting | bytes 819200 | tf_op jit(solution)/shard_map/mixed_gather/stack | solution.py:109
  176.5 2.8 %fusion.38 = (bf16[1,4,4,40,80]{4,0,3,1,2:T(2,128)(2,1)S(1)}, bf16[1,4,4,40,80]{4,0,3,1,2:T(2,128)(2,1)S(1)}, bf16[1,4,4,40,80]{4,0,3,1,2:T(2,128)(2,1)S(1)}, bf...) fusion(bf16[8,4,4,40,80]{4,0,3,1,2:T(8,128)(2,1)S(1)} %get-tupl, ...), kind=kLoop, calls=%fused_computation.124 | loop fusion | bytes 1638400 | tf_op jit(solution)/shard_map/product/slice | solution.py:117
  179.6 2.8 %fusion.39 = (bf16[1,4,4,40,80]{4,0,3,2,1:T(2,128)(2,1)S(1)}, bf16[1,4,4,40,80]{4,0,3,2,1:T(2,128)(2,1)S(1)}, bf16[1,4,4,40,80]{4,0,3,2,1:T(2,128)(2,1)S(1)}, bf...) fusion(bf16[8,4,4,40,80]{4,0,3,2,1:T(8,128)(2,1)S(1)} %get-tupl, ...), kind=kLoop, calls=%fused_computation.125 | loop fusion | bytes 1638400 | tf_op jit(solution)/shard_map/product/slice | solution.py:116
  (101 shorter events, 38.1 us)
Async XLA Ops:
  0.0 157.2 %copy-start = (f32[8]{0:T(128)S(1)}, f32[8]{0:T(128)}, u32[]{:S(2)}) copy-start(f32[8]{0:T(128)} %param.6) | copy-start | bytes 100
  0.0 25.9 %collective-permute-start.3 = (bf16[192,6144]{1,0:T(8,128)(2,1)}, bf16[192,6144]{1,0:T(8,128)(2,1)}, u32[]{:S(2)}, u32[]{:S(2)}) collective-permute-start(bf16[192,6144]{1,0:T(8,128)(2,1)} %bitcast.188), channel_id=1, source_target_pairs={{0,1},{1,0},{2,3},{3,2},{4,5},{5,4},{6,7},{7,6},{32,33},{33,32},{3... | collective-permute-start | bytes 7077896 | tf_op jit(solution)/shard_map/rows_pair/ppermute | solution.py:42
  3.2 14.7 %collective-permute-start.2 = (bf16[40,6144]{1,0:T(8,128)(2,1)}, bf16[40,6144]{1,0:T(8,128)(2,1)S(1)}, u32[]{:S(2)}, u32[]{:S(2)}) collective-permute-start(bf16[40,6144]{1,0:T(8,128)(2,1)} %bitcast.175), channel_id=1, source_target_pairs={{0,2},{1,9},{2,4},{3,11},{4,6},{5,13},{6,32},{7,15},{32,34},{33,41... | collective-permute-start | bytes 1474568 | tf_op jit(solution)/shard_map/basis_line/ppermute | solution.py:42
  3.2 14.7 %collective-permute-start.1 = (bf16[40,6144]{1,0:T(8,128)(2,1)}, bf16[40,6144]{1,0:T(8,128)(2,1)S(1)}, u32[]{:S(2)}, u32[]{:S(2)}) collective-permute-start(bf16[40,6144]{1,0:T(8,128)(2,1)} %bitcast.176), channel_id=1, source_target_pairs={{0,4},{1,17},{2,38},{3,19},{4,32},{5,21},{6,2},{7,23},{32,36},{33,... | collective-permute-start | bytes 1474568 | tf_op jit(solution)/shard_map/basis_line/ppermute | solution.py:42
  5.4 13.1 %collective-permute-start = (bf16[40,6144]{1,0:T(8,128)(2,1)}, bf16[40,6144]{1,0:T(8,128)(2,1)S(1)}, u32[]{:S(2)}, u32[]{:S(2)}) collective-permute-start(bf16[40,6144]{1,0:T(8,128)(2,1)} %bitcast.177), channel_id=1, source_target_pairs={{0,38},{1,25},{2,0},{3,27},{4,2},{5,29},{6,4},{7,31},{32,6},{33,57... | collective-permute-start | bytes 1474568 | tf_op jit(solution)/shard_map/basis_line/ppermute | solution.py:42
  19.7 46.9 %collective-permute-start.4 = (bf16[160,6144]{1,0:T(8,128)(2,1)S(1)}, bf16[160,6144]{1,0:T(8,128)(2,1)}, u32[]{:S(2)}, u32[]{:S(2)}) collective-permute-start(bf16[160,6144]{1,0:T(8,128)(2,1)S(1)} %pad_maximum_fusion), channel_id=1, source_target_pairs={{0,24},{1,39},{2,26},{3,1},{4,28},{5,3},{6,30},{7,5},{32,56},{33,7... | collective-permute-start | bytes 5898248 | tf_op jit(solution)/shard_map/basis_plane/ppermute | solution.py:42
  23.9 47.4 %collective-permute-start.5 = (bf16[160,6144]{1,0:T(8,128)(2,1)S(1)}, bf16[160,6144]{1,0:T(8,128)(2,1)}, u32[]{:S(2)}, u32[]{:S(2)}) collective-permute-start(bf16[160,6144]{1,0:T(8,128)(2,1)S(1)} %pad_maximum_fusion), channel_id=1, source_target_pairs={{0,16},{1,5},{2,18},{3,39},{4,20},{5,33},{6,22},{7,3},{32,48},{33,... | collective-permute-start | bytes 5898248 | tf_op jit(solution)/shard_map/basis_plane/ppermute | solution.py:42
  23.9 42.6 %copy-start.2 = (bf16[1,192,6144]{2,1,0:T(8,128)(2,1)S(1)}, bf16[1,192,6144]{2,1,0:T(8,128)(2,1)}, u32[]{:S(2)}) copy-start(bf16[1,192,6144]{2,1,0:T(8,128)(2,1)} %param.4) | copy-start | bytes 7077892
  23.9 52.1 %collective-permute-start.6 = (bf16[160,6144]{1,0:T(8,128)(2,1)S(1)}, bf16[160,6144]{1,0:T(8,128)(2,1)S(1)}, u32[]{:S(2)}, u32[]{:S(2)}) collective-permute-start(bf16[160,6144]{1,0:T(8,128)(2,1)S(1)} %pad_maximum_fusion), channel_id=1, source_target_pairs={{0,8},{1,3},{2,10},{3,5},{4,12},{5,7},{6,14},{7,33},{32,40},{33,35... | collective-permute-start | bytes 5898248 | tf_op jit(solution)/shard_map/basis_plane/ppermute | solution.py:42
  95.4 9.3 %collective-permute-start.7 = (bf16[40,6144]{1,0:T(8,128)(2,1)S(1)}, bf16[40,6144]{1,0:T(8,128)(2,1)S(1)}, u32[]{:S(2)}, u32[]{:S(2)}) collective-permute-start(bf16[40,6144]{1,0:T(8,128)(2,1)S(1)} %bitcast.156), channel_id=1, source_target_pairs={{0,1},{1,0},{2,3},{3,2},{4,5},{5,4},{6,7},{7,6},{32,33},{33,32},{3... | collective-permute-start | bytes 1474568 | tf_op jit(solution)/shard_map/projected_exchange/ppermute | solution.py:42
  108.6 11.5 %copy-start.1 = (f32[8,8]{1,0:T(8,128)S(1)}, f32[8,8]{1,0:T(8,128)}, u32[]{:S(2)}) copy-start(f32[8,8]{1,0:T(8,128)} %param.7) | copy-start | bytes 772
  112.1 29.4 %all-to-all-start.1 = ((bf16[8,80,640]{2,1,0:T(8,128)(2,1)}), bf16[8,80,640]{2,1,0:T(8,128)(2,1)S(1)}, u32[]{:S(2)}, u32[]{:S(2)}) async-start(bf16[8,80,640]{2,1,0:T(8,128)(2,1)} %broadcast_in_dim.2), calls=%async_computation.1 | async-start | bytes 1638400 | tf_op jit(solution)/shard_map/points/all_to_all | solution.py:92
  142.6 7.8 %collective-permute-start.10 = (bf16[80,640]{1,0:T(8,128)(2,1)S(1)}, bf16[80,640]{1,0:T(8,128)(2,1)S(1)}, u32[]{:S(2)}, u32[]{:S(2)}) collective-permute-start(bf16[80,640]{1,0:T(8,128)(2,1)S(1)} %reshape.160), channel_id=1, source_target_pairs={{0,2},{1,9},{2,4},{3,11},{4,6},{5,13},{6,0},{7,15},{32,34},{33,41}... | collective-permute-start | bytes 307208 | tf_op jit(solution)/shard_map/mixed_gather/ppermute | solution.py:42
  142.7 7.1 %collective-permute-start.9 = (bf16[80,640]{1,0:T(8,128)(2,1)S(1)}, bf16[80,640]{1,0:T(8,128)(2,1)S(1)}, u32[]{:S(2)}, u32[]{:S(2)}) collective-permute-start(bf16[80,640]{1,0:T(8,128)(2,1)S(1)} %reshape.160), channel_id=1, source_target_pairs={{0,4},{1,17},{2,6},{3,19},{4,0},{5,21},{6,2},{7,23},{32,36},{33,49... | collective-permute-start | bytes 307208 | tf_op jit(solution)/shard_map/mixed_gather/ppermute | solution.py:42
  143.8 5.3 %collective-permute-start.8 = (bf16[80,640]{1,0:T(8,128)(2,1)S(1)}, bf16[80,640]{1,0:T(8,128)(2,1)S(1)}, u32[]{:S(2)}, u32[]{:S(2)}) collective-permute-start(bf16[80,640]{1,0:T(8,128)(2,1)S(1)} %reshape.160), channel_id=1, source_target_pairs={{0,6},{1,25},{2,0},{3,27},{4,2},{5,29},{6,4},{7,31},{32,38},{33,57... | collective-permute-start | bytes 307208 | tf_op jit(solution)/shard_map/mixed_gather/ppermute | solution.py:42
  151.1 14.0 %collective-permute-start.12 = (bf16[320,640]{1,0:T(8,128)(2,1)}, bf16[320,640]{1,0:T(8,128)(2,1)}, u32[]{:S(2)}, u32[]{:S(2)}) collective-permute-start(bf16[320,640]{1,0:T(8,128)(2,1)} %constant_dynamic-update-slice_fusion.10), channel_id=1, source_target_pairs={{0,16},{1,5},{2,18},{3,7},{4,20},{5,1},{6,22},{7,3},{32,48},{33,37... | collective-permute-start | bytes 1228808 | tf_op jit(solution)/shard_map/mixed_gather/ppermute | solution.py:42
  154.8 12.9 %collective-permute-start.11 = (bf16[320,640]{1,0:T(8,128)(2,1)}, bf16[320,640]{1,0:T(8,128)(2,1)}, u32[]{:S(2)}, u32[]{:S(2)}) collective-permute-start(bf16[320,640]{1,0:T(8,128)(2,1)} %constant_dynamic-update-slice_fusion.10), channel_id=1, source_target_pairs={{0,24},{1,7},{2,26},{3,1},{4,28},{5,3},{6,30},{7,5},{32,56},{33,39... | collective-permute-start | bytes 1228808 | tf_op jit(solution)/shard_map/mixed_gather/ppermute | solution.py:42
  157.2 15.3 %collective-permute-start.13 = (bf16[320,640]{1,0:T(8,128)(2,1)}, bf16[320,640]{1,0:T(8,128)(2,1)}, u32[]{:S(2)}, u32[]{:S(2)}) collective-permute-start(bf16[320,640]{1,0:T(8,128)(2,1)} %constant_dynamic-update-slice_fusion.10), channel_id=1, source_target_pairs={{0,8},{1,3},{2,10},{3,5},{4,12},{5,7},{6,14},{7,1},{32,40},{33,35}... | collective-permute-start | bytes 1228808 | tf_op jit(solution)/shard_map/mixed_gather/ppermute | solution.py:42
  157.7 26.2 %collective-permute-start.14 = (bf16[8,80,640]{2,1,0:T(8,128)(2,1)S(1)}, bf16[8,80,640]{2,1,0:T(8,128)(2,1)}, u32[]{:S(2)}, u32[]{:S(2)}) collective-permute-start(bf16[8,80,640]{2,1,0:T(8,128)(2,1)S(1)} %all-to-all-done.1), channel_id=1, source_target_pairs={{0,1},{1,0},{2,3},{3,2},{4,5},{5,4},{6,7},{7,6},{32,33},{33,32},{3... | collective-permute-start | bytes 2457608 | tf_op jit(solution)/shard_map/points/ppermute | solution.py:42
  192.8 2.0 %collective-permute-start.15 = (f32[40,80]{1,0:T(8,128)S(1)}, f32[40,80]{1,0:T(8,128)S(1)}, u32[]{:S(2)}, u32[]{:S(2)}) collective-permute-start(f32[40,80]{1,0:T(8,128)S(1)} %get-tuple-element.24), channel_id=1, source_target_pairs={{0,1},{1,0},{2,3},{3,2},{4,5},{5,4},{6,7},{7,6},{32,33},{33,32},{3... | collective-permute-start | bytes 38408 | tf_op jit(solution)/shard_map/output/ppermute | solution.py:42

commit v2 on v1

--- a/solution.py
+++ b/solution.py
@@ -1,6 +1,8 @@
 import jax
 import jax.numpy as jnp
 from jax import lax
+from jax.experimental import pallas as pl
+from jax.experimental.pallas import tpu as pltpu
 from jax.sharding import PartitionSpec as P
 
 BF = jnp.bfloat16
@@ -57,6 +59,47 @@
     return lax.dynamic_slice_in_dim(jnp.concatenate([blocks, blocks], 0), (4 - start) % 4, 4, 0)
 
 
+INTERPRET = False
+
+
+def product_kernel(own_ref, other_ref, m0, m1, m2, m3, linear_ref, out_ref, right_own, right_other):
+    points, side, _ = own_ref.shape
+    half = side // 2
+    part = m0.shape[0] // 2
+    for a, m in enumerate((m0, m1, m2, m3)):
+        right_own[a * part : (a + 1) * part] = m[:part]
+        right_other[a * part : (a + 1) * part] = m[part:]
+    total = linear_ref[...]
+    crossed = jnp.zeros((side, side), F32)
+    for r in range(points):
+        low = side * r // 128 * 128
+        high = min(-(-(side * r + side) // 128) * 128, points * side)
+        at = side * r - low
+        mine = jnp.dot(own_ref[r], right_own[:, low:high], preferred_element_type=F32)
+        total = total + mine[:, at : at + side]
+        theirs = jnp.dot(other_ref[r], right_other[:, low:high], preferred_element_type=F32)
+        crossed = crossed + theirs[:, at : at + side]
+    out_ref[:half] = total[:half] + crossed[half:]
+    out_ref[half:] = total[half:] + crossed[:half]
+
+
+def product(own, other, planes, linear):
+    points, side, lanes = own.shape
+    return pl.pallas_call(
+        product_kernel,
+        out_shape=jax.ShapeDtypeStruct((side, side), F32),
+        in_specs=[pl.BlockSpec(memory_space=pltpu.VMEM)] * 7,
+        out_specs=pl.BlockSpec(memory_space=pltpu.VMEM),
+        scratch_shapes=[pltpu.VMEM((lanes, points * side), BF)] * 2,
+        compiler_params=pltpu.CompilerParams(vmem_limit_bytes=32 * 1024 * 1024),
+        interpret=INTERPRET,
+    )(own, other, *planes, linear)
+
+
+def one_hot(spots, count):
+    return (jnp.arange(count)[:, None] == spots[None, :]).astype(BF)
+
+
 def shards(potential, basis, weights, coupling):
     point = lax.axis_index("pt")
     pan = lax.axis_index("pan")
@@ -76,6 +119,7 @@
         chip_rows = jnp.where(
             core == 0, jnp.concatenate([rows, other_rows], 0), jnp.concatenate([other_rows, rows], 0)
         )
+        chip_rows = lax.optimization_barrier(chip_rows)
     with jax.named_scope("basis_plane"):
         units = gather_line(line, along(False, True))
     with jax.named_scope("projected"):
@@ -88,34 +132,34 @@
         both = jnp.concatenate([own, send(own, CORE)], 0)
     with jax.named_scope("channel"):
         channel = jnp.concatenate([nt(both, u).astype(BF) for u in units], 1)
+    lanes, side = 16 * width, 2 * width
+    with jax.named_scope("columns_exchange"):
+        lane = jnp.arange(lanes)
+        want = lane // width
+        dy, dz = (want // 4 - y) % 4, (want % 4 - z) % 4
+        spot = jnp.where(core == 0, dy * 4 + dz, dz * 4 + dy) * width + lane % width
+        sorted_columns = jnp.dot(channel, one_hot(spot, lanes), preferred_element_type=F32).astype(BF)
+        sorted_columns = sorted_columns.reshape(side, 8, side).transpose(1, 0, 2)
+        chosen = lax.all_to_all(sorted_columns, "pt", 0, 0, tiled=True)
+        chosen, channel = lax.optimization_barrier((chosen, channel))
+        chosen = chosen.astype(F32)
+        antisym = coupling - coupling.T
+        mixed = jnp.einsum("qr,qin->irn", antisym, chosen, precision=lax.Precision.HIGHEST)
+        mixed = mixed.astype(BF).reshape(side, -1)
+        linear = jnp.einsum("q,qin->in", weights, chosen, precision=lax.Precision.HIGHEST)
+    with jax.named_scope("mixed_line"):
+        line = gather_line(mixed, along(True, False))
+        line = jnp.concatenate([m[:width] for m in line] + [m[width:] for m in line], 0)
     with jax.named_scope("points"):
         every = lax.all_to_all(jnp.broadcast_to(channel, (8,) + channel.shape), "pt", 0, 0, tiled=True)
-        every = every.reshape(8, 2 * width, 16 * width)
-        every_other = send(every, CORE)
-    with jax.named_scope("select"):
-        lane = jnp.arange(2 * width)
-        want = 2 * point + lane // width
-        dy, dz = (want // 4 - y) % 4, (want % 4 - z) % 4
-        spot = (jnp.where(core == 0, dy * 4 + dz, dz * 4 + dy)) * width + lane % width
-        pick = (jnp.arange(16 * width)[:, None] == spot[None, :]).astype(BF)
-        chosen = jnp.dot(every.reshape(-1, 16 * width), pick, preferred_element_type=F32)
-        chosen = chosen.reshape(8, 2 * width, 2 * width)
-        antisym = coupling - coupling.T
-        mixed = jnp.einsum("qr,qin->irn", antisym, chosen, precision=lax.Precision.HIGHEST)
-        mixed = mixed.astype(BF).reshape(2 * width, -1)
-        linear = jnp.einsum("q,qin->in", weights, chosen, precision=lax.Precision.HIGHEST)
-    with jax.named_scope("mixed_gather"):
-        mline = jnp.concatenate(gather_line(mixed, along(True, False)), 0)
-        mplane = jnp.stack(gather_line(mline, along(False, False)))
+        other = send(every, CORE)
+        spot = jnp.arange(lanes).reshape(4, 4, width).transpose(1, 0, 2).reshape(-1)
+        other = jnp.dot(other.reshape(-1, lanes), one_hot(spot, lanes), preferred_element_type=F32)
+        other = other.astype(BF).reshape(every.shape)
+    with jax.named_scope("mixed_plane"):
+        planes = gather_line(line, along(False, False))
     with jax.named_scope("product"):
-        right = mplane.reshape(4, 4, 2, width, 8, 2 * width)
-        right_own = right[:, :, 0].transpose(3, 0, 1, 2, 4).reshape(8, 16 * width, 2 * width)
-        right_other = right[:, :, 1].transpose(3, 1, 0, 2, 4).reshape(8, 16 * width, 2 * width)
-        total, crossed = linear, 0.0
-        for r in range(8):
-            total = total + jnp.dot(every[r], right_own[r], preferred_element_type=F32)
-            crossed = crossed + jnp.dot(every_other[r], right_other[r], preferred_element_type=F32)
-        total = total + jnp.concatenate([crossed[width:], crossed[:width]], 0)
+        total = product(every, other, planes, linear)
     with jax.named_scope("output"):
         mine = total[:width].reshape(width, 2, 1, width)
         theirs = send(total[width:], CORE).reshape(width, 2, 1, width)

time: 200 us -> 180 us (0.900); the launches traced: 196 us -> 179 us
  waiting for transfers between devices: 75.5 us -> 107 us
  local copies, waits for them, and re-layouts: 25.9 us -> 3.65 us
  matrix products: 36 us -> 18.1 us
  blocking collectives: 14.6 us -> 0 us
  other arithmetic: 2.03 us -> 7.87 us
    all_to_all x0 -> x2, waiting for transfers between devices: none -> 22.7 us  [the longest x1 13.2 us: shards(): lax.all_to_all(blocks, 'pan', 0, 0, axis_index_groups=CHIPS, tiled=True)]
    ppermute x16, waiting for transfers between devices: 54.2 us -> 72 us  [send(): return lax.ppermute(value, AXES, perm)]
    all_to_all x1 -> x0, blocking collectives: 14.6 us -> none  [shards(): lax.all_to_all(blocks, 'pan', 0, 0, axis_index_groups=CHIPS, tiled=True)]
    all_to_all x0 -> x2, starting transfers between devices: none -> 12.2 us  [the longest x1 8.42 us: shards(): chosen = lax.all_to_all(sorted_columns, 'pt', 0, 0, tiled=True)]
    another operation x5 -> x0, local copies, waits for them, and re-layouts: 11.3 us -> none  [shards(): mplane = jnp.stack(gather_line(mline, along(False, False)))]
    dot_general x17 -> x2, matrix products: 10.4 us -> 1.35 us  [the longest x1 0.92 us: shards(): jnp.dot(other.reshape(-1, lanes), one_hot(spot, lanes), preferred_element...]
    all_to_all x1, waiting for transfers between devices: 21.3 us -> 12.4 us  [shards(): lax.all_to_all(jnp.broadcast_to(channel, (8,) + channel.shape), 'pt', 0,...]
    dot_general x8, matrix products: 24.6 us -> 16.1 us  [nt(): lax.dot_general(a, b, (((1,), (1,)), ((), ())), preferred_element_type=F32)]
  transfers between devices with their start and end apart: 17 -> 19, of which waited for: 8 -> 14; matrix products, arithmetic and copies ran while one was open for 21% -> 9% of each run, Pallas kernels for 0% -> 0%
where the time goes in v2:
time: 180 us; the launch traced here: 179 us
  waiting for transfers between devices  107 us (59%)
  starting transfers between devices  41.4 us (23%)
  matrix products  18.1 us (10%)
  other arithmetic  7.87 us (4%)
  local copies, waits for them, and re-layouts  3.65 us (2%)
    ppermute x16, waiting for transfers between devices, send(): return lax.ppermute(value, AXES, perm)  72 us
    ppermute x16, starting transfers between devices, send(): return lax.ppermute(value, AXES, perm)  25.6 us
    dot_general x8, matrix products, nt(): lax.dot_general(a, b, (((1,), (1,)), ((), ())), preferred_element_type=F32)  16.1 us
    all_to_all x1, waiting for transfers between devices, shards(): lax.all_to_all(blocks, 'pan', 0, 0, axis_index_groups=CHIPS, tiled=True)  13.2 us
    all_to_all x1, waiting for transfers between devices, shards(): lax.all_to_all(jnp.broadcast_to(channel, (8,) + channel.shape), 'pt', 0,...  12.4 us
    all_to_all x1, waiting for transfers between devices, shards(): chosen = lax.all_to_all(sorted_columns, 'pt', 0, 0, tiled=True)  9.51 us
    all_to_all x1, starting transfers between devices, shards(): chosen = lax.all_to_all(sorted_columns, 'pt', 0, 0, tiled=True)  8.42 us
    select_n x1, other arithmetic, shards(): jnp.where(core == 0, jnp.concatenate([rows, other_rows], 0), jnp.concaten...  5 us
  transfers between devices with their start and end apart: 19, of which 14 were waited for; matrix products, arithmetic and copies ran while one was open for 9% of the time, Pallas kernels for 0%

profile of v2, /device:TPU:1, one launch (start us, length us, event | category | flops | bytes accessed | tf_op | source)
XLA Modules:
  0.0 179.3 jit_solution(8260405830355601877)
XLA Ops:
  0.0 3.2 %collective-permute-start.3 = (bf16[192,6144]{1,0:T(8,128)(2,1)}, bf16[192,6144]{1,0:T(8,128)(2,1)}, u32[]{:S(2)}, u32[]{:S(2)}) collective-permute-start(bf16[192,6144]{1,0:T(8,128)(2,1)} %bitcast.76), channel_id=1, source_target_pairs={{0,1},{1,0},{2,3},{3,2},{4,5},{5,4},{6,7},{7,6},{32,33},{33,32},{3... | collective-permute-start | bytes 7077896 | tf_op jit(solution)/shard_map/rows_pair/ppermute | solution.py:44
  5.3 6.1 %collective-permute-done = bf16[40,6144]{1,0:T(8,128)(2,1)S(1)} collective-permute-done((bf16[40,6144]{1,0:T(8,128)(2,1)}, bf16[40,6144]{1,0:T(8,128)(2,1)S(1)}, u32[]{:S(2)}, u32[]{:S(2)}) %collective-permute-start) | collective-permute-done | bytes 491552 | tf_op jit(solution)/shard_map/basis_line/ppermute | solution.py:44
  11.4 2.5 %collective-permute-done.1 = bf16[40,6144]{1,0:T(8,128)(2,1)S(1)} collective-permute-done((bf16[40,6144]{1,0:T(8,128)(2,1)}, bf16[40,6144]{1,0:T(8,128)(2,1)S(1)}, u32[]{:S(2)}, u32[]{:S(2)}) %collective-permute-start.1) | collective-permute-done | bytes 491552 | tf_op jit(solution)/shard_map/basis_line/ppermute | solution.py:44
  14.0 5.2 %collective-permute-done.2 = bf16[40,6144]{1,0:T(8,128)(2,1)S(1)} collective-permute-done((bf16[40,6144]{1,0:T(8,128)(2,1)}, bf16[40,6144]{1,0:T(8,128)(2,1)S(1)}, u32[]{:S(2)}, u32[]{:S(2)}) %collective-permute-start.2) | collective-permute-done | bytes 491552 | tf_op jit(solution)/shard_map/basis_line/ppermute | solution.py:44
  20.4 5.4 %collective-permute-start.4 = (bf16[160,6144]{1,0:T(8,128)(2,1)S(1)}, bf16[160,6144]{1,0:T(8,128)(2,1)}, u32[]{:S(2)}, u32[]{:S(2)}) collective-permute-start(bf16[160,6144]{1,0:T(8,128)(2,1)S(1)} %pad_maximum_fusion), channel_id=1, source_target_pairs={{0,24},{1,39},{2,26},{3,1},{4,28},{5,3},{6,30},{7,5},{32,56},{33,7... | collective-permute-start | bytes 5898248 | tf_op jit(solution)/shard_map/basis_plane/ppermute | solution.py:44
  25.8 1.9 %collective-permute-start.6 = (bf16[160,6144]{1,0:T(8,128)(2,1)S(1)}, bf16[160,6144]{1,0:T(8,128)(2,1)S(1)}, u32[]{:S(2)}, u32[]{:S(2)}) collective-permute-start(bf16[160,6144]{1,0:T(8,128)(2,1)S(1)} %pad_maximum_fusion), channel_id=1, source_target_pairs={{0,8},{1,3},{2,10},{3,5},{4,12},{5,7},{6,14},{7,33},{32,40},{33,35... | collective-permute-start | bytes 5898248 | tf_op jit(solution)/shard_map/basis_plane/ppermute | solution.py:44
  27.7 5.0 %maximum_select_fusion = bf16[384,6144]{1,0:T(8,128)(2,1)S(1)} fusion(bf16[192,6144]{1,0:T(8,128)(2,1)} %collective-permute-done.3, bf16[192,6144]{1,0:T(8,128)(2,1)} %bitcast.77, pred[]{:T(512)S(6)} %eq.47), kind=kLoop, calls=%fused_computation | loop fusion | flops 21233664 | bytes 9437185 | tf_op jit(solution)/shard_map/rows_pair/jit(_where)/select_n | solution.py:119
  34.4 34.0 %collective-permute-done.4 = bf16[160,6144]{1,0:T(8,128)(2,1)} collective-permute-done((bf16[160,6144]{1,0:T(8,128)(2,1)S(1)}, bf16[160,6144]{1,0:T(8,128)(2,1)}, u32[]{:S(2)}, u32[]{:S(2)}) %collective-permute-start.4) | collective-permute-done | bytes 1966112 | tf_op jit(solution)/shard_map/basis_plane/ppermute | solution.py:44
  68.4 3.2 %convolution_convert_fusion.3 = bf16[160,384]{1,0:T(8,128)(2,1)S(1)} fusion(bf16[160,6144]{1,0:T(8,128)(2,1)} %collective-permute-done.4, bf16[384,6144]{1,0:T(8,128)(2,1)S(1)} %maximum_select_fusion), kind=kOutput, calls=%fused_computation.10 | convolution fusion | flops 755036160 | bytes 6807552 | tf_op jit(solution)/shard_map/projected/dot_general | solution.py:55
  71.7 3.2 %convolution_convert_fusion.2 = bf16[160,384]{1,0:T(8,128)(2,1)S(1)} fusion(bf16[160,6144]{1,0:T(8,128)(2,1)} %collective-permute-done.5, bf16[384,6144]{1,0:T(8,128)(2,1)S(1)} %maximum_select_fusion), kind=kOutput, calls=%fused_computation.9 | convolution fusion | flops 755036160 | bytes 6807552 | tf_op jit(solution)/shard_map/projected/dot_general | solution.py:55
  78.0 3.7 %all-to-all-start = ((bf16[16,40,384]{2,1,0:T(8,128)(2,1)}), bf16[16,40,384]{2,1,0:T(8,128)(2,1)S(1)}, u32[]{:S(2)}, u32[]{:S(2)}) async-start(bf16[16,40,384]{2,1,0:T(8,128)(2,1)} %bitcast.11), calls=%async_computation | async-start | bytes 983040 | tf_op jit(solution)/shard_map/projected_exchange/all_to_all | solution.py:130
  81.8 13.2 %all-to-all-done = bf16[16,40,384]{2,1,0:T(8,128)(2,1)S(1)} async-done(((bf16[16,40,384]{2,1,0:T(8,128)(2,1)}), bf16[16,40,384]{2,1,0:T(8,128)(2,1)S(1)}, u32[]{:S(2)}, u32[]{:S(2)}) %all-to-all-start) | async-done | bytes 491552 | tf_op jit(solution)/shard_map/projected_exchange/all_to_all | solution.py:130
  95.0 3.4 %collective-permute-start.7 = (bf16[40,6144]{1,0:T(8,128)(2,1)S(1)}, bf16[40,6144]{1,0:T(8,128)(2,1)S(1)}, u32[]{:S(2)}, u32[]{:S(2)}) collective-permute-start(bf16[40,6144]{1,0:T(8,128)(2,1)S(1)} %bitcast.79), channel_id=1, source_target_pairs={{0,1},{1,0},{2,3},{3,2},{4,5},{5,4},{6,7},{7,6},{32,33},{33,32},{3... | collective-permute-start | bytes 1474568 | tf_op jit(solution)/shard_map/projected_exchange/ppermute | solution.py:44
  100.8 2.5 %convolution_convert_fusion.7 = bf16[80,160]{1,0:T(8,128)(2,1)S(1)} fusion(bf16[80,6144]{1,0:T(8,128)(2,1)S(1)} %constant_dynamic-update-slice_fusion.8, bf16[160,6144]{1,0:T(8,128)(2,1)} %collective-permute-done.4), kind=kOutput, calls=%fused_computation.16 | convolution fusion | flops 157299200 | bytes 2974720 | tf_op jit(solution)/shard_map/channel/dot_general | solution.py:55
  103.2 2.3 %convolution_convert_fusion.6 = bf16[80,160]{1,0:T(8,128)(2,1)S(1)} fusion(bf16[80,6144]{1,0:T(8,128)(2,1)S(1)} %constant_dynamic-update-slice_fusion.8, bf16[160,6144]{1,0:T(8,128)(2,1)} %collective-permute-done.5), kind=kOutput, calls=%fused_computation.15 | convolution fusion | flops 157299200 | bytes 2974720 | tf_op jit(solution)/shard_map/channel/dot_general | solution.py:55
  107.8 8.4 %all-to-all-start.1 = ((bf16[8,80,80]{2,1,0:T(8,128)(2,1)}), bf16[8,80,80]{2,1,0:T(8,128)(2,1)S(1)}, u32[]{:S(2)}, u32[]{:S(2)}) async-start(bf16[8,80,80]{2,1,0:T(8,128)(2,1)} %bitcast.73), calls=%async_computation.1 | async-start | bytes 327680 | tf_op jit(solution)/shard_map/columns_exchange/all_to_all | solution.py:143
  116.3 9.5 %all-to-all-done.1 = bf16[8,80,80]{2,1,0:T(8,128)(2,1)S(1)} async-done(((bf16[8,80,80]{2,1,0:T(8,128)(2,1)}), bf16[8,80,80]{2,1,0:T(8,128)(2,1)S(1)}, u32[]{:S(2)}, u32[]{:S(2)}) %all-to-all-start.1) | async-done | bytes 102432 | tf_op jit(solution)/shard_map/columns_exchange/all_to_all | solution.py:143
  126.8 3.5 %all-to-all-start.2 = ((bf16[8,80,640]{2,1,0:T(8,128)(2,1)}), bf16[8,80,640]{2,1,0:T(8,128)(2,1)S(1)}, u32[]{:S(2)}, u32[]{:S(2)}) async-start(bf16[8,80,640]{2,1,0:T(8,128)(2,1)} %broadcast_in_dim.2), calls=%async_computation.2 | async-start | bytes 1638400 | tf_op jit(solution)/shard_map/points/all_to_all | solution.py:154
  132.9 1.7 collective-permute-done.9
  134.6 2.3 %collective-permute-done.10 = bf16[80,640]{1,0:T(8,128)(2,1)S(1)} collective-permute-done((bf16[80,640]{1,0:T(8,128)(2,1)S(1)}, bf16[80,640]{1,0:T(8,128)(2,1)S(1)}, u32[]{:S(2)}, u32[]{:S(2)}) %collective-permute-start.10) | collective-permute-done | bytes 102432 | tf_op jit(solution)/shard_map/mixed_line/ppermute | solution.py:44
  138.2 12.4 %all-to-all-done.2.own_ref = bf16[8,80,640]{2,1,0:T(8,128)(2,1)S(1)} async-done(((bf16[8,80,640]{2,1,0:T(8,128)(2,1)}), bf16[8,80,640]{2,1,0:T(8,128)(2,1)S(1)}, u32[]{:S(2)}, u32[]{:S(2)}) %all-to-all-start.2) | async-done | bytes 819232 | tf_op jit(solution)/shard_map/points/all_to_all | solution.py:154
  150.5 4.8 %collective-permute-start.8 = (bf16[8,80,640]{2,1,0:T(8,128)(2,1)S(1)}, bf16[8,80,640]{2,1,0:T(8,128)(2,1)S(1)}, u32[]{:S(2)}, u32[]{:S(2)}) collective-permute-start(bf16[8,80,640]{2,1,0:T(8,128)(2,1)S(1)} %all-to-all-done.2.own_ref), channel_id=1, source_target_pairs={{0,1},{1,0},{2,3},{3,2},{4,5},{5,4},{6,7},{7,6},{32,33},{33,32},{3... | collective-permute-start | bytes 2457608 | tf_op jit(solution)/shard_map/points/ppermute | solution.py:44
  159.7 2.8 %collective-permute-done.12.m1 = bf16[320,640]{1,0:T(8,128)(2,1)S(1)} collective-permute-done((bf16[320,640]{1,0:T(8,128)(2,1)S(1)}, bf16[320,640]{1,0:T(8,128)(2,1)S(1)}, u32[]{:S(2)}, u32[]{:S(2)}) %collective-permute-start.12) | collective-permute-done | bytes 409632 | tf_op jit(solution)/shard_map/mixed_plane/ppermute | solution.py:44
  162.5 13.5 %collective-permute-done.13.m2 = bf16[320,640]{1,0:T(8,128)(2,1)S(1)} collective-permute-done((bf16[320,640]{1,0:T(8,128)(2,1)S(1)}, bf16[320,640]{1,0:T(8,128)(2,1)S(1)}, u32[]{:S(2)}, u32[]{:S(2)}) %collective-permute-start.13) | collective-permute-done | bytes 409632 | tf_op jit(solution)/shard_map/mixed_plane/ppermute | solution.py:44
  (76 shorter events, 25.1 us)
Async XLA Ops:
  0.0 158.5 %copy-start = (f32[8]{0:T(128)S(1)}, f32[8]{0:T(128)}, u32[]{:S(2)}) copy-start(f32[8]{0:T(128)} %param.6) | copy-start | bytes 100
  0.0 27.7 %collective-permute-start.3 = (bf16[192,6144]{1,0:T(8,128)(2,1)}, bf16[192,6144]{1,0:T(8,128)(2,1)}, u32[]{:S(2)}, u32[]{:S(2)}) collective-permute-start(bf16[192,6144]{1,0:T(8,128)(2,1)} %bitcast.76), channel_id=1, source_target_pairs={{0,1},{1,0},{2,3},{3,2},{4,5},{5,4},{6,7},{7,6},{32,33},{33,32},{3... | collective-permute-start | bytes 7077896 | tf_op jit(solution)/shard_map/rows_pair/ppermute | solution.py:44
  3.2 8.2 %collective-permute-start = (bf16[40,6144]{1,0:T(8,128)(2,1)}, bf16[40,6144]{1,0:T(8,128)(2,1)S(1)}, u32[]{:S(2)}, u32[]{:S(2)}) collective-permute-start(bf16[40,6144]{1,0:T(8,128)(2,1)} %bitcast.89), channel_id=1, source_target_pairs={{0,38},{1,25},{2,0},{3,27},{4,2},{5,29},{6,4},{7,31},{32,6},{33,57... | collective-permute-start | bytes 1474568 | tf_op jit(solution)/shard_map/basis_line/ppermute | solution.py:44
  4.2 9.7 %collective-permute-start.1 = (bf16[40,6144]{1,0:T(8,128)(2,1)}, bf16[40,6144]{1,0:T(8,128)(2,1)S(1)}, u32[]{:S(2)}, u32[]{:S(2)}) collective-permute-start(bf16[40,6144]{1,0:T(8,128)(2,1)} %bitcast.90), channel_id=1, source_target_pairs={{0,4},{1,17},{2,38},{3,19},{4,32},{5,21},{6,2},{7,23},{32,36},{33,... | collective-permute-start | bytes 1474568 | tf_op jit(solution)/shard_map/basis_line/ppermute | solution.py:44
  4.6 14.6 %collective-permute-start.2 = (bf16[40,6144]{1,0:T(8,128)(2,1)}, bf16[40,6144]{1,0:T(8,128)(2,1)S(1)}, u32[]{:S(2)}, u32[]{:S(2)}) collective-permute-start(bf16[40,6144]{1,0:T(8,128)(2,1)} %bitcast.91), channel_id=1, source_target_pairs={{0,2},{1,9},{2,4},{3,11},{4,6},{5,13},{6,32},{7,15},{32,34},{33,41... | collective-permute-start | bytes 1474568 | tf_op jit(solution)/shard_map/basis_line/ppermute | solution.py:44
  20.4 48.0 %collective-permute-start.4 = (bf16[160,6144]{1,0:T(8,128)(2,1)S(1)}, bf16[160,6144]{1,0:T(8,128)(2,1)}, u32[]{:S(2)}, u32[]{:S(2)}) collective-permute-start(bf16[160,6144]{1,0:T(8,128)(2,1)S(1)} %pad_maximum_fusion), channel_id=1, source_target_pairs={{0,24},{1,39},{2,26},{3,1},{4,28},{5,3},{6,30},{7,5},{32,56},{33,7... | collective-permute-start | bytes 5898248 | tf_op jit(solution)/shard_map/basis_plane/ppermute | solution.py:44
  25.8 46.0 %collective-permute-start.5 = (bf16[160,6144]{1,0:T(8,128)(2,1)S(1)}, bf16[160,6144]{1,0:T(8,128)(2,1)}, u32[]{:S(2)}, u32[]{:S(2)}) collective-permute-start(bf16[160,6144]{1,0:T(8,128)(2,1)S(1)} %pad_maximum_fusion), channel_id=1, source_target_pairs={{0,16},{1,5},{2,18},{3,39},{4,20},{5,33},{6,22},{7,3},{32,48},{33,... | collective-permute-start | bytes 5898248 | tf_op jit(solution)/shard_map/basis_plane/ppermute | solution.py:44
  25.8 49.3 %collective-permute-start.6 = (bf16[160,6144]{1,0:T(8,128)(2,1)S(1)}, bf16[160,6144]{1,0:T(8,128)(2,1)S(1)}, u32[]{:S(2)}, u32[]{:S(2)}) collective-permute-start(bf16[160,6144]{1,0:T(8,128)(2,1)S(1)} %pad_maximum_fusion), channel_id=1, source_target_pairs={{0,8},{1,3},{2,10},{3,5},{4,12},{5,7},{6,14},{7,33},{32,40},{33,35... | collective-permute-start | bytes 5898248 | tf_op jit(solution)/shard_map/basis_plane/ppermute | solution.py:44
  75.1 1.7 copy-start.1
  78.0 16.9 %all-to-all-start = ((bf16[16,40,384]{2,1,0:T(8,128)(2,1)}), bf16[16,40,384]{2,1,0:T(8,128)(2,1)S(1)}, u32[]{:S(2)}, u32[]{:S(2)}) async-start(bf16[16,40,384]{2,1,0:T(8,128)(2,1)} %bitcast.11), calls=%async_computation | async-start | bytes 983040 | tf_op jit(solution)/shard_map/projected_exchange/all_to_all | solution.py:130
  95.0 4.9 %collective-permute-start.7 = (bf16[40,6144]{1,0:T(8,128)(2,1)S(1)}, bf16[40,6144]{1,0:T(8,128)(2,1)S(1)}, u32[]{:S(2)}, u32[]{:S(2)}) collective-permute-start(bf16[40,6144]{1,0:T(8,128)(2,1)S(1)} %bitcast.79), channel_id=1, source_target_pairs={{0,1},{1,0},{2,3},{3,2},{4,5},{5,4},{6,7},{7,6},{32,33},{33,32},{3... | collective-permute-start | bytes 1474568 | tf_op jit(solution)/shard_map/projected_exchange/ppermute | solution.py:44
  100.8 4.8 %copy-start.2 = (bf16[160,6144]{1,0:T(8,128)(2,1)S(1)}, bf16[160,6144]{1,0:T(8,128)(2,1)}, u32[]{:S(2)}) copy-start(bf16[160,6144]{1,0:T(8,128)(2,1)} %copy-done.1) | copy-start | bytes 5898244
  105.6 10.7 %copy-start.3 = (f32[8,8]{1,0:T(8,128)S(1)}, f32[8,8]{1,0:T(8,128)}, u32[]{:S(2)}) copy-start(f32[8,8]{1,0:T(8,128)} %param.7) | copy-start | bytes 772
  107.8 18.0 %all-to-all-start.1 = ((bf16[8,80,80]{2,1,0:T(8,128)(2,1)}), bf16[8,80,80]{2,1,0:T(8,128)(2,1)S(1)}, u32[]{:S(2)}, u32[]{:S(2)}) async-start(bf16[8,80,80]{2,1,0:T(8,128)(2,1)} %bitcast.73), calls=%async_computation.1 | async-start | bytes 327680 | tf_op jit(solution)/shard_map/columns_exchange/all_to_all | solution.py:143
  126.8 23.7 %all-to-all-start.2 = ((bf16[8,80,640]{2,1,0:T(8,128)(2,1)}), bf16[8,80,640]{2,1,0:T(8,128)(2,1)S(1)}, u32[]{:S(2)}, u32[]{:S(2)}) async-start(bf16[8,80,640]{2,1,0:T(8,128)(2,1)} %broadcast_in_dim.2), calls=%async_computation.2 | async-start | bytes 1638400 | tf_op jit(solution)/shard_map/points/all_to_all | solution.py:154
  131.0 3.6 %collective-permute-start.9 = (bf16[80,640]{1,0:T(8,128)(2,1)S(1)}, bf16[80,640]{1,0:T(8,128)(2,1)S(1)}, u32[]{:S(2)}, u32[]{:S(2)}) collective-permute-start(bf16[80,640]{1,0:T(8,128)(2,1)S(1)} %reshape.174), channel_id=1, source_target_pairs={{0,6},{1,25},{2,0},{3,27},{4,2},{5,29},{6,4},{7,31},{32,38},{33,57... | collective-permute-start | bytes 307208 | tf_op jit(solution)/shard_map/mixed_line/ppermute | solution.py:44
  131.7 5.1 %collective-permute-start.10 = (bf16[80,640]{1,0:T(8,128)(2,1)S(1)}, bf16[80,640]{1,0:T(8,128)(2,1)S(1)}, u32[]{:S(2)}, u32[]{:S(2)}) collective-permute-start(bf16[80,640]{1,0:T(8,128)(2,1)S(1)} %reshape.174), channel_id=1, source_target_pairs={{0,4},{1,17},{2,6},{3,19},{4,0},{5,21},{6,2},{7,23},{32,36},{33,49... | collective-permute-start | bytes 307208 | tf_op jit(solution)/shard_map/mixed_line/ppermute | solution.py:44
  131.9 6.2 %collective-permute-start.11 = (bf16[80,640]{1,0:T(8,128)(2,1)S(1)}, bf16[80,640]{1,0:T(8,128)(2,1)S(1)}, u32[]{:S(2)}, u32[]{:S(2)}) collective-permute-start(bf16[80,640]{1,0:T(8,128)(2,1)S(1)} %reshape.174), channel_id=1, source_target_pairs={{0,2},{1,9},{2,4},{3,11},{4,6},{5,13},{6,0},{7,15},{32,34},{33,41}... | collective-permute-start | bytes 307208 | tf_op jit(solution)/shard_map/mixed_line/ppermute | solution.py:44
  150.5 8.3 %collective-permute-start.8 = (bf16[8,80,640]{2,1,0:T(8,128)(2,1)S(1)}, bf16[8,80,640]{2,1,0:T(8,128)(2,1)S(1)}, u32[]{:S(2)}, u32[]{:S(2)}) collective-permute-start(bf16[8,80,640]{2,1,0:T(8,128)(2,1)S(1)} %all-to-all-done.2.own_ref), channel_id=1, source_target_pairs={{0,1},{1,0},{2,3},{3,2},{4,5},{5,4},{6,7},{7,6},{32,33},{33,32},{3... | collective-permute-start | bytes 2457608 | tf_op jit(solution)/shard_map/points/ppermute | solution.py:44
  155.4 7.2 %collective-permute-start.12 = (bf16[320,640]{1,0:T(8,128)(2,1)S(1)}, bf16[320,640]{1,0:T(8,128)(2,1)S(1)}, u32[]{:S(2)}, u32[]{:S(2)}) collective-permute-start(bf16[320,640]{1,0:T(8,128)(2,1)S(1)} %slice_dynamic-update-slice_fusion.m0), channel_id=1, source_target_pairs={{0,24},{1,7},{2,26},{3,1},{4,28},{5,3},{6,30},{7,5},{32,56},{33,39... | collective-permute-start | bytes 1228808 | tf_op jit(solution)/shard_map/mixed_plane/ppermute | solution.py:44
  156.7 19.4 %collective-permute-start.13 = (bf16[320,640]{1,0:T(8,128)(2,1)S(1)}, bf16[320,640]{1,0:T(8,128)(2,1)S(1)}, u32[]{:S(2)}, u32[]{:S(2)}) collective-permute-start(bf16[320,640]{1,0:T(8,128)(2,1)S(1)} %slice_dynamic-update-slice_fusion.m0), channel_id=1, source_target_pairs={{0,16},{1,5},{2,18},{3,7},{4,20},{5,1},{6,22},{7,3},{32,48},{33,37... | collective-permute-start | bytes 1228808 | tf_op jit(solution)/shard_map/mixed_plane/ppermute | solution.py:44
  157.5 18.5 %collective-permute-start.14 = (bf16[320,640]{1,0:T(8,128)(2,1)S(1)}, bf16[320,640]{1,0:T(8,128)(2,1)S(1)}, u32[]{:S(2)}, u32[]{:S(2)}) collective-permute-start(bf16[320,640]{1,0:T(8,128)(2,1)S(1)} %slice_dynamic-update-slice_fusion.m0), channel_id=1, source_target_pairs={{0,8},{1,3},{2,10},{3,5},{4,12},{5,7},{6,14},{7,1},{32,40},{33,35}... | collective-permute-start | bytes 1228808 | tf_op jit(solution)/shard_map/mixed_plane/ppermute | solution.py:44
  177.1 1.3 collective-permute-start.15

commit v3 on v2

v3 whole, which is shorter than its diff:
```python
import jax
import jax.numpy as jnp
from jax import lax
from jax.experimental import pallas as pl
from jax.experimental.pallas import tpu as pltpu
from jax.sharding import PartitionSpec as P

BF = jnp.bfloat16
F32 = jnp.float32
AXES = ("pt", "pan")


def place(x, y, z, c):
    return ((x % 4) * 2 + (z % 8) // 4) * 32 + (y % 4) * 8 + (z % 4) * 2 + c


def pairs(move):
    return [
        (place(x, y, z, c), place(*move(x, y, z, c)))
        for x in range(4) for y in range(4) for z in range(8) for c in range(2)
    ]


def along(first, ring):
    def z_move(z, step):
        return z + step if ring else z // 4 * 4 + (z + step) % 4

    def perm(step):
        return pairs(
            lambda x, y, z, c: (x, y, z_move(z, step(z)), c) if (c == 0) == first else (x, y + step(y), z, c)
        )

    return perm


UP = lambda v: 1
DOWN = lambda v: -1
TWO = lambda v: 2 if v % 2 == 0 else -2
CROSS = lambda step: pairs(lambda x, y, z, c: (x + step(x), y, z, c))
CORE = pairs(lambda x, y, z, c: (x, y, z, 1 - c))
CHIPS = [[2 * chip + core for chip in range(16)] for core in range(2)]


def send(value, perm):
    return lax.ppermute(value, AXES, perm)


def gather_line(value, axis):
    up = send(value, axis(UP))
    down = send(value, axis(DOWN))
    two = send(value, axis(TWO))
    return value, down, two, up


def nt(a, b):
    return lax.dot_general(a, b, (((1,), (1,)), ((), ())), preferred_element_type=F32)


def unroll(blocks, start):
    return lax.dynamic_slice_in_dim(jnp.concatenate([blocks, blocks], 0), (4 - start) % 4, 4, 0)


INTERPRET = False


def product_kernel(left_ref, m0, m1, m2, m3, out_ref, right):
    points, side, lanes = left_ref.shape
    part = m0.shape[0]
    span = m0.shape[1] // points
    for a, m in enumerate((m0, m1, m2, m3)):
        right[a * part : (a + 1) * part] = m[...]
    total = jnp.zeros(out_ref.shape, F32)
    for r in range(points):
        low = span * r // 128 * 128
        high = min(-(-(span * r + span) // 128) * 128, points * span)
        at = span * r - low
        term = jnp.dot(left_ref[r], right[:, low:high], preferred_element_type=F32)
        total = total + term[:, at : at + span]
    out_ref[...] = total


def product(left, planes):
    points, side, lanes = left.shape
    return pl.pallas_call(
        product_kernel,
        out_shape=jax.ShapeDtypeStruct((side, planes[0].shape[1] // points), F32),
        in_specs=[pl.BlockSpec(memory_space=pltpu.VMEM)] * 5,
        out_specs=pl.BlockSpec(memory_space=pltpu.VMEM),
        scratch_shapes=[pltpu.VMEM((lanes, planes[0].shape[1]), BF)],
        compiler_params=pltpu.CompilerParams(vmem_limit_bytes=32 * 1024 * 1024),
        interpret=INTERPRET,
    )(left, *planes)


def one_hot(spots, count):
    return (jnp.arange(count)[:, None] == spots[None, :]).astype(BF)


def shards(potential, basis, weights, coupling):
    point = lax.axis_index("pt")
    pan = lax.axis_index("pan")
    core = pan % 2
    chip = pan // 2
    x, y, z = point // 2, chip // 4, chip % 4
    second = jnp.where(core == 0, y, z)
    first = jnp.where(core == 0, z, y)
    rows = potential[0]
    panel = basis.T
    width, depth = panel.shape

    with jax.named_scope("basis_line"):
        line = jnp.concatenate(gather_line(panel, along(True, True)), 0)
    with jax.named_scope("rows_pair"):
        line, other_rows = lax.optimization_barrier((line, send(rows, CORE)))
        chip_rows = jnp.where(
            core == 0, jnp.concatenate([rows, other_rows], 0), jnp.concatenate([other_rows, rows], 0)
        )
        chip_rows = lax.optimization_barrier(chip_rows)
    with jax.named_scope("basis_plane"):
        plane = along(False, True)
        fetched = lax.dynamic_index_in_dim(line.reshape(4, width, depth), x, 0, keepdims=False)
        fetched, line = lax.optimization_barrier((send(fetched, plane(TWO)), line))
        two = jnp.zeros((4, width, depth), BF)
        for step, perm in ((0, None), (1, CROSS(DOWN)), (3, CROSS(UP)), (2, CROSS(TWO))):
            piece = fetched if perm is None else send(fetched, perm)
            two = lax.dynamic_update_index_in_dim(two, piece, (x + step) % 4, 0)
        units = line, send(line, plane(DOWN)), two.reshape(4 * width, depth), send(line, plane(UP))
    with jax.named_scope("projected"):
        parts = [unroll(nt(u, chip_rows).astype(BF).reshape(4, width, -1), first) for u in units]
        blocks = unroll(jnp.stack(parts), second)
        blocks = jnp.where(core == 0, blocks, blocks.transpose(1, 0, 2, 3)).reshape(16, width, -1)
    with jax.named_scope("projected_exchange"):
        got = lax.all_to_all(blocks, "pan", 0, 0, axis_index_groups=CHIPS, tiled=True)
        own = got.transpose(1, 0, 2).reshape(width, depth)
        both = jnp.concatenate([own, send(own, CORE)], 0)
    with jax.named_scope("channel"):
        channel = jnp.concatenate([nt(both, u).astype(BF) for u in units], 1)
    lanes = 16 * width
    with jax.named_scope("columns_exchange"):
        crossed = send(channel[width:], CORE)
        block = jnp.arange(2 * lanes) // width
        dy, dz = (block // 8 - y) % 4, (block // 2 % 4 - z) % 4
        spot = jnp.where(block % 2 == 0, dy * 4 + dz, dz * 4 + dy) * width + jnp.arange(2 * lanes) % width
        mine = block % 2 == core
        ordered = jnp.dot(channel[:width], one_hot(jnp.where(mine, spot, -1), lanes), preferred_element_type=F32)
        ordered += jnp.dot(crossed, one_hot(jnp.where(mine, -1, spot), lanes), preferred_element_type=F32)
        ordered = ordered.astype(BF).reshape(width, 8, 4 * width).transpose(1, 0, 2)
        chosen = lax.all_to_all(ordered, "pt", 0, 0, tiled=True)
        chosen, channel = lax.optimization_barrier((chosen, channel))
        chosen = chosen.astype(F32)
        antisym = coupling - coupling.T
        mixed = jnp.einsum("qr,qin->irn", antisym, chosen, precision=lax.Precision.HIGHEST)
        mixed = mixed.astype(BF).reshape(width, -1)
        linear = jnp.einsum("q,qin->in", weights, chosen, precision=lax.Precision.HIGHEST)
    with jax.named_scope("mixed_line"):
        line = jnp.concatenate(gather_line(mixed, along(True, False)), 0)
    with jax.named_scope("points"):
        every = lax.all_to_all(jnp.broadcast_to(channel, (8,) + channel.shape), "pt", 0, 0, tiled=True)
    with jax.named_scope("mixed_plane"):
        planes = gather_line(line, along(False, False))
    with jax.named_scope("product"):
        total = product(every, planes)
    with jax.named_scope("output"):
        return linear + total[:width] + send(total[width:], CORE)


def solution(mesh):
    in_specs = (P("pt", "pan", None), P(None, "pan"), P(), P())
    return jax.shard_map(shards, mesh=mesh, in_specs=in_specs, out_specs=P("pan", "pt"), check_vma=False)
```

time: 180 us -> 169 us (0.939)
  the two profiles are of different devices: /device:TPU:1 before, /device:TPU:67 now
where the time goes in v3:
time: 169 us; the launch traced here: 168 us
  waiting for transfers between devices  91.1 us (54%)
  starting transfers between devices  52.6 us (31%)
  matrix products  11.7 us (7%)
  other arithmetic  7.47 us (4%)
  local copies, waits for them, and re-layouts  4.29 us (3%)
    ppermute x19, waiting for transfers between devices, send(): return lax.ppermute(value, AXES, perm)  72.1 us
    ppermute x19, starting transfers between devices, send(): return lax.ppermute(value, AXES, perm)  34.5 us
    all_to_all x1, waiting for transfers between devices, shards(): lax.all_to_all(blocks, 'pan', 0, 0, axis_index_groups=CHIPS, tiled=True)  10.9 us
    dot_general x8, matrix products, nt(): lax.dot_general(a, b, (((1,), (1,)), ((), ())), preferred_element_type=F32)  9.74 us
    all_to_all x1, waiting for transfers between devices, shards(): chosen = lax.all_to_all(ordered, 'pt', 0, 0, tiled=True)  8.12 us
    all_to_all x1, starting transfers between devices, shards(): lax.all_to_all(blocks, 'pan', 0, 0, axis_index_groups=CHIPS, tiled=True)  7.51 us
    all_to_all x1, starting transfers between devices, shards(): chosen = lax.all_to_all(ordered, 'pt', 0, 0, tiled=True)  5.79 us
    all_to_all x1, starting transfers between devices, shards(): lax.all_to_all(jnp.broadcast_to(channel, (8,) + channel.shape), 'pt', 0,...  4.86 us
  transfers between devices with their start and end apart: 22, of which 18 were waited for; matrix products, arithmetic and copies ran while one was open for 7% of the time, Pallas kernels for 0%

profile of v3, /device:TPU:67, one launch (start us, length us, event | category | flops | bytes accessed | tf_op | source)
XLA Modules:
  0.0 168.2 jit_solution(3774167741384754967)
XLA Ops:
  0.7 2.7 %collective-permute-start = (bf16[40,6144]{1,0:T(8,128)(2,1)}, bf16[40,6144]{1,0:T(8,128)(2,1)S(1)}, u32[]{:S(2)}, u32[]{:S(2)}) collective-permute-start(bf16[40,6144]{1,0:T(8,128)(2,1)} %bitcast.99), channel_id=1, source_target_pairs={{0,38},{1,25},{2,0},{3,27},{4,2},{5,29},{6,4},{7,31},{32,6},{33,57... | collective-permute-start | bytes 1474568 | tf_op jit(solution)/shard_map/basis_line/ppermute | solution.py:45
  4.5 10.3 %collective-permute-done = bf16[40,6144]{1,0:T(8,128)(2,1)S(1)} collective-permute-done((bf16[40,6144]{1,0:T(8,128)(2,1)}, bf16[40,6144]{1,0:T(8,128)(2,1)S(1)}, u32[]{:S(2)}, u32[]{:S(2)}) %collective-permute-start) | collective-permute-done | bytes 491552 | tf_op jit(solution)/shard_map/basis_line/ppermute | solution.py:45
  14.8 3.3 %collective-permute-done.2 = bf16[40,6144]{1,0:T(8,128)(2,1)S(1)} collective-permute-done((bf16[40,6144]{1,0:T(8,128)(2,1)}, bf16[40,6144]{1,0:T(8,128)(2,1)S(1)}, u32[]{:S(2)}, u32[]{:S(2)}) %collective-permute-start.2) | collective-permute-done | bytes 491552 | tf_op jit(solution)/shard_map/basis_line/ppermute | solution.py:45
  19.3 4.3 %collective-permute-start.4 = (bf16[40,6144]{1,0:T(8,128)(2,1)S(1)}, bf16[40,6144]{1,0:T(8,128)(2,1)S(1)}, u32[]{:S(2)}, u32[]{:S(2)}) collective-permute-start(bf16[40,6144]{1,0:T(8,128)(2,1)S(1)} %dynamic-slice_bitcast_fusion), channel_id=1, source_target_pairs={{0,16},{1,5},{2,18},{3,39},{4,20},{5,33},{6,22},{7,3},{32,48},{33,... | collective-permute-start | bytes 1474568 | tf_op jit(solution)/shard_map/basis_plane/ppermute | solution.py:45
  23.6 4.0 %maximum_select_fusion = bf16[384,6144]{1,0:T(8,128)(2,1)S(1)} fusion(bf16[192,6144]{1,0:T(8,128)(2,1)} %collective-permute-done.3, bf16[192,6144]{1,0:T(8,128)(2,1)S(1)} %bitcast.87, pred[]{:T(512)S(6)} %eq.75), kind=kLoop, calls=%fused_computation | loop fusion | flops 21233664 | bytes 9437185 | tf_op jit(solution)/shard_map/rows_pair/jit(_where)/select_n | solution.py:115
  27.6 1.8 %collective-permute-done.4 = bf16[40,6144]{1,0:T(8,128)(2,1)S(1)} collective-permute-done((bf16[40,6144]{1,0:T(8,128)(2,1)S(1)}, bf16[40,6144]{1,0:T(8,128)(2,1)S(1)}, u32[]{:S(2)}, u32[]{:S(2)}) %collective-permute-start.4) | collective-permute-done | bytes 491552 | tf_op jit(solution)/shard_map/basis_plane/ppermute | solution.py:45
  30.9 3.1 %collective-permute-start.8 = (bf16[40,6144]{1,0:T(8,128)(2,1)S(1)}, bf16[40,6144]{1,0:T(8,128)(2,1)S(1)}, u32[]{:S(2)}, u32[]{:S(2)}) collective-permute-start(bf16[40,6144]{1,0:T(8,128)(2,1)S(1)} %collective-permute-done.4), channel_id=1, source_target_pairs={{0,128},{1,129},{2,130},{3,131},{4,132},{5,133},{6,134},{7,135},{3... | collective-permute-start | bytes 1474568 | tf_op jit(solution)/shard_map/basis_plane/ppermute | solution.py:45
  35.6 1.7 %convolution_convert_fusion.4 = bf16[160,384]{1,0:T(8,128)(2,1)S(1)} fusion(bf16[160,6144]{1,0:T(8,128)(2,1)S(1)} %pad_maximum_fusion, bf16[384,6144]{1,0:T(8,128)(2,1)S(1)} %maximum_select_fusion), kind=kOutput, calls=%fused_computation.14 | convolution fusion | flops 755036160 | bytes 6807552 | tf_op jit(solution)/shard_map/projected/dot_general | solution.py:56
  37.4 3.8 %collective-permute-done.6 = bf16[40,6144]{1,0:T(8,128)(2,1)S(1)} collective-permute-done((bf16[40,6144]{1,0:T(8,128)(2,1)S(1)}, bf16[40,6144]{1,0:T(8,128)(2,1)S(1)}, u32[]{:S(2)}, u32[]{:S(2)}) %collective-permute-start.6) | collective-permute-done | bytes 491552 | tf_op jit(solution)/shard_map/basis_plane/ppermute | solution.py:45
  42.6 10.2 %collective-permute-done.8 = bf16[40,6144]{1,0:T(8,128)(2,1)S(1)} collective-permute-done((bf16[40,6144]{1,0:T(8,128)(2,1)S(1)}, bf16[40,6144]{1,0:T(8,128)(2,1)S(1)}, u32[]{:S(2)}, u32[]{:S(2)}) %collective-permute-start.8) | collective-permute-done | bytes 491552 | tf_op jit(solution)/shard_map/basis_plane/ppermute | solution.py:45
  52.8 1.6 convolution_convert_fusion.2
  54.4 3.3 %collective-permute-done.5 = bf16[160,6144]{1,0:T(8,128)(2,1)S(1)} collective-permute-done((bf16[160,6144]{1,0:T(8,128)(2,1)S(1)}, bf16[160,6144]{1,0:T(8,128)(2,1)S(1)}, u32[]{:S(2)}, u32[]{:S(2)}) %collective-permute-start.5) | collective-permute-done | bytes 1966112 | tf_op jit(solution)/shard_map/basis_plane/ppermute | solution.py:45
  62.5 7.5 %all-to-all-start = ((bf16[16,40,384]{2,1,0:T(8,128)(2,1)}), bf16[16,40,384]{2,1,0:T(8,128)(2,1)S(1)}, u32[]{:S(2)}, u32[]{:S(2)}) async-start(bf16[16,40,384]{2,1,0:T(8,128)(2,1)} %bitcast.18), calls=%async_computation | async-start | bytes 983040 | tf_op jit(solution)/shard_map/projected_exchange/all_to_all | solution.py:133
  70.1 10.9 %all-to-all-done = bf16[16,40,384]{2,1,0:T(8,128)(2,1)S(1)} async-done(((bf16[16,40,384]{2,1,0:T(8,128)(2,1)}), bf16[16,40,384]{2,1,0:T(8,128)(2,1)S(1)}, u32[]{:S(2)}, u32[]{:S(2)}) %all-to-all-start) | async-done | bytes 491552 | tf_op jit(solution)/shard_map/projected_exchange/all_to_all | solution.py:133
  81.0 3.6 %collective-permute-start.10 = (bf16[40,6144]{1,0:T(8,128)(2,1)S(1)}, bf16[40,6144]{1,0:T(8,128)(2,1)S(1)}, u32[]{:S(2)}, u32[]{:S(2)}) collective-permute-start(bf16[40,6144]{1,0:T(8,128)(2,1)S(1)} %bitcast.89), channel_id=1, source_target_pairs={{0,1},{1,0},{2,3},{3,2},{4,5},{5,4},{6,7},{7,6},{32,33},{33,32},{3... | collective-permute-start | bytes 1474568 | tf_op jit(solution)/shard_map/projected_exchange/ppermute | solution.py:45
  93.9 5.8 %all-to-all-start.1 = ((bf16[8,40,160]{2,1,0:T(8,128)(2,1)}), bf16[8,40,160]{2,1,0:T(8,128)(2,1)S(1)}, u32[]{:S(2)}, u32[]{:S(2)}) async-start(bf16[8,40,160]{2,1,0:T(8,128)(2,1)} %bitcast.82), calls=%async_computation.1 | async-start | bytes 327680 | tf_op jit(solution)/shard_map/columns_exchange/all_to_all | solution.py:148
  99.8 8.1 %all-to-all-done.1 = bf16[8,40,160]{2,1,0:T(8,128)(2,1)S(1)} async-done(((bf16[8,40,160]{2,1,0:T(8,128)(2,1)}), bf16[8,40,160]{2,1,0:T(8,128)(2,1)S(1)}, u32[]{:S(2)}, u32[]{:S(2)}) %all-to-all-start.1) | async-done | bytes 102432 | tf_op jit(solution)/shard_map/columns_exchange/all_to_all | solution.py:148
  108.9 4.9 %all-to-all-start.2 = ((bf16[8,80,640]{2,1,0:T(8,128)(2,1)}), bf16[8,80,640]{2,1,0:T(8,128)(2,1)S(1)}, u32[]{:S(2)}, u32[]{:S(2)}) async-start(bf16[8,80,640]{2,1,0:T(8,128)(2,1)} %broadcast_in_dim.32), calls=%async_computation.2 | async-start | bytes 1638400 | tf_op jit(solution)/shard_map/points/all_to_all | solution.py:158
  118.4 2.2 %collective-permute-done.13 = bf16[40,1280]{1,0:T(8,128)(2,1)S(1)} collective-permute-done((bf16[40,1280]{1,0:T(8,128)(2,1)S(1)}, bf16[40,1280]{1,0:T(8,128)(2,1)S(1)}, u32[]{:S(2)}, u32[]{:S(2)}) %collective-permute-start.13) | collective-permute-done | bytes 102432 | tf_op jit(solution)/shard_map/mixed_line/ppermute | solution.py:45
  121.7 3.1 %collective-permute-start.15 = (bf16[160,1280]{1,0:T(8,128)(2,1)S(1)}, bf16[160,1280]{1,0:T(8,128)(2,1)S(1)}, u32[]{:S(2)}, u32[]{:S(2)}) collective-permute-start(bf16[160,1280]{1,0:T(8,128)(2,1)S(1)} %constant_dynamic-update-slice_fusion.2.m0), channel_id=1, source_target_pairs={{0,24},{1,7},{2,26},{3,1},{4,28},{5,3},{6,30},{7,5},{32,56},{33,39... | collective-permute-start | bytes 1228808 | tf_op jit(solution)/shard_map/mixed_plane/ppermute | solution.py:45
  126.1 23.0 %collective-permute-done.15.m1 = bf16[160,1280]{1,0:T(8,128)(2,1)S(1)} collective-permute-done((bf16[160,1280]{1,0:T(8,128)(2,1)S(1)}, bf16[160,1280]{1,0:T(8,128)(2,1)S(1)}, u32[]{:S(2)}, u32[]{:S(2)}) %collective-permute-start.15) | collective-permute-done | bytes 409632 | tf_op jit(solution)/shard_map/mixed_plane/ppermute | solution.py:45
  149.1 4.4 %collective-permute-done.16.m2 = bf16[160,1280]{1,0:T(8,128)(2,1)S(1)} collective-permute-done((bf16[160,1280]{1,0:T(8,128)(2,1)S(1)}, bf16[160,1280]{1,0:T(8,128)(2,1)S(1)}, u32[]{:S(2)}, u32[]{:S(2)}) %collective-permute-start.16) | collective-permute-done | bytes 409632 | tf_op jit(solution)/shard_map/mixed_plane/ppermute | solution.py:45
  153.5 3.7 %collective-permute-done.17.m3 = bf16[160,1280]{1,0:T(8,128)(2,1)S(1)} collective-permute-done((bf16[160,1280]{1,0:T(8,128)(2,1)S(1)}, bf16[160,1280]{1,0:T(8,128)(2,1)S(1)}, u32[]{:S(2)}, u32[]{:S(2)}) %collective-permute-start.17) | collective-permute-done | bytes 409632 | tf_op jit(solution)/shard_map/mixed_plane/ppermute | solution.py:45
  157.9 8.8 %collective-permute-start.18 = (f32[40,160]{1,0:T(8,128)S(1)}, f32[40,160]{1,0:T(8,128)S(1)}, u32[]{:S(2)}, u32[]{:S(2)}) collective-permute-start(f32[40,160]{1,0:T(8,128)S(1)} %slice.19), channel_id=1, source_target_pairs={{0,1},{1,0},{2,3},{3,2},{4,5},{5,4},{6,7},{7,6},{32,33},{33,32},{3... | collective-permute-start | bytes 76808 | tf_op jit(solution)/shard_map/output/ppermute | solution.py:45
  (87 shorter events, 31.9 us)
Async XLA Ops:
  0.0 166.7 %copy-start = (f32[8]{0:T(128)S(1)}, f32[8]{0:T(128)}, u32[]{:S(2)}) copy-start(f32[8]{0:T(128)} %param.6) | copy-start | bytes 100
  0.0 19.3 %collective-permute-start.3 = (bf16[192,6144]{1,0:T(8,128)(2,1)}, bf16[192,6144]{1,0:T(8,128)(2,1)}, u32[]{:S(2)}, u32[]{:S(2)}) collective-permute-start(bf16[192,6144]{1,0:T(8,128)(2,1)} %bitcast.86), channel_id=1, source_target_pairs={{0,1},{1,0},{2,3},{3,2},{4,5},{5,4},{6,7},{7,6},{32,33},{33,32},{3... | collective-permute-start | bytes 7077896 | tf_op jit(solution)/shard_map/rows_pair/ppermute | solution.py:45
  0.7 14.1 %collective-permute-start = (bf16[40,6144]{1,0:T(8,128)(2,1)}, bf16[40,6144]{1,0:T(8,128)(2,1)S(1)}, u32[]{:S(2)}, u32[]{:S(2)}) collective-permute-start(bf16[40,6144]{1,0:T(8,128)(2,1)} %bitcast.99), channel_id=1, source_target_pairs={{0,38},{1,25},{2,0},{3,27},{4,2},{5,29},{6,4},{7,31},{32,6},{33,57... | collective-permute-start | bytes 1474568 | tf_op jit(solution)/shard_map/basis_line/ppermute | solution.py:45
  3.4 11.4 %collective-permute-start.1 = (bf16[40,6144]{1,0:T(8,128)(2,1)}, bf16[40,6144]{1,0:T(8,128)(2,1)S(1)}, u32[]{:S(2)}, u32[]{:S(2)}) collective-permute-start(bf16[40,6144]{1,0:T(8,128)(2,1)} %bitcast.100), channel_id=1, source_target_pairs={{0,4},{1,17},{2,38},{3,19},{4,32},{5,21},{6,2},{7,23},{32,36},{33,... | collective-permute-start | bytes 1474568 | tf_op jit(solution)/shard_map/basis_line/ppermute | solution.py:45
  3.8 14.3 %collective-permute-start.2 = (bf16[40,6144]{1,0:T(8,128)(2,1)}, bf16[40,6144]{1,0:T(8,128)(2,1)S(1)}, u32[]{:S(2)}, u32[]{:S(2)}) collective-permute-start(bf16[40,6144]{1,0:T(8,128)(2,1)} %bitcast.101), channel_id=1, source_target_pairs={{0,2},{1,9},{2,4},{3,11},{4,6},{5,13},{6,32},{7,15},{32,34},{33,41... | collective-permute-start | bytes 1474568 | tf_op jit(solution)/shard_map/basis_line/ppermute | solution.py:45
  4.5 19.2 %copy-start.7 = (bf16[1,192,6144]{2,1,0:T(8,128)(2,1)S(1)}, bf16[1,192,6144]{2,1,0:T(8,128)(2,1)}, u32[]{:S(2)}) copy-start(bf16[1,192,6144]{2,1,0:T(8,128)(2,1)} %param.4) | copy-start | bytes 7077892
  19.3 10.1 %collective-permute-start.4 = (bf16[40,6144]{1,0:T(8,128)(2,1)S(1)}, bf16[40,6144]{1,0:T(8,128)(2,1)S(1)}, u32[]{:S(2)}, u32[]{:S(2)}) collective-permute-start(bf16[40,6144]{1,0:T(8,128)(2,1)S(1)} %dynamic-slice_bitcast_fusion), channel_id=1, source_target_pairs={{0,16},{1,5},{2,18},{3,39},{4,20},{5,33},{6,22},{7,3},{32,48},{33,... | collective-permute-start | bytes 1474568 | tf_op jit(solution)/shard_map/basis_plane/ppermute | solution.py:45
  29.4 11.9 %collective-permute-start.6 = (bf16[40,6144]{1,0:T(8,128)(2,1)S(1)}, bf16[40,6144]{1,0:T(8,128)(2,1)S(1)}, u32[]{:S(2)}, u32[]{:S(2)}) collective-permute-start(bf16[40,6144]{1,0:T(8,128)(2,1)S(1)} %collective-permute-done.4), channel_id=1, source_target_pairs={{0,192},{1,193},{2,194},{3,195},{4,196},{5,197},{6,198},{7,199},{3... | collective-permute-start | bytes 1474568 | tf_op jit(solution)/shard_map/basis_plane/ppermute | solution.py:45
  29.7 12.9 %collective-permute-start.7 = (bf16[40,6144]{1,0:T(8,128)(2,1)S(1)}, bf16[40,6144]{1,0:T(8,128)(2,1)S(1)}, u32[]{:S(2)}, u32[]{:S(2)}) collective-permute-start(bf16[40,6144]{1,0:T(8,128)(2,1)S(1)} %collective-permute-done.4), channel_id=1, source_target_pairs={{0,64},{1,65},{2,66},{3,67},{4,68},{5,69},{6,70},{7,71},{32,96},{3... | collective-permute-start | bytes 1474568 | tf_op jit(solution)/shard_map/basis_plane/ppermute | solution.py:45
  30.9 21.9 %collective-permute-start.8 = (bf16[40,6144]{1,0:T(8,128)(2,1)S(1)}, bf16[40,6144]{1,0:T(8,128)(2,1)S(1)}, u32[]{:S(2)}, u32[]{:S(2)}) collective-permute-start(bf16[40,6144]{1,0:T(8,128)(2,1)S(1)} %collective-permute-done.4), channel_id=1, source_target_pairs={{0,128},{1,129},{2,130},{3,131},{4,132},{5,133},{6,134},{7,135},{3... | collective-permute-start | bytes 1474568 | tf_op jit(solution)/shard_map/basis_plane/ppermute | solution.py:45
  33.9 23.8 %collective-permute-start.5 = (bf16[160,6144]{1,0:T(8,128)(2,1)S(1)}, bf16[160,6144]{1,0:T(8,128)(2,1)S(1)}, u32[]{:S(2)}, u32[]{:S(2)}) collective-permute-start(bf16[160,6144]{1,0:T(8,128)(2,1)S(1)} %pad_maximum_fusion), channel_id=1, source_target_pairs={{0,24},{1,39},{2,26},{3,1},{4,28},{5,3},{6,30},{7,5},{32,56},{33,7... | collective-permute-start | bytes 5898248 | tf_op jit(solution)/shard_map/basis_plane/ppermute | solution.py:45
  34.7 24.8 %collective-permute-start.9 = (bf16[160,6144]{1,0:T(8,128)(2,1)S(1)}, bf16[160,6144]{1,0:T(8,128)(2,1)S(1)}, u32[]{:S(2)}, u32[]{:S(2)}) collective-permute-start(bf16[160,6144]{1,0:T(8,128)(2,1)S(1)} %pad_maximum_fusion), channel_id=1, source_target_pairs={{0,8},{1,3},{2,10},{3,5},{4,12},{5,7},{6,14},{7,33},{32,40},{33,35... | collective-permute-start | bytes 5898248 | tf_op jit(solution)/shard_map/basis_plane/ppermute | solution.py:45
  62.5 18.5 %all-to-all-start = ((bf16[16,40,384]{2,1,0:T(8,128)(2,1)}), bf16[16,40,384]{2,1,0:T(8,128)(2,1)S(1)}, u32[]{:S(2)}, u32[]{:S(2)}) async-start(bf16[16,40,384]{2,1,0:T(8,128)(2,1)} %bitcast.18), calls=%async_computation | async-start | bytes 983040 | tf_op jit(solution)/shard_map/projected_exchange/all_to_all | solution.py:133
  81.0 5.1 %collective-permute-start.10 = (bf16[40,6144]{1,0:T(8,128)(2,1)S(1)}, bf16[40,6144]{1,0:T(8,128)(2,1)S(1)}, u32[]{:S(2)}, u32[]{:S(2)}) collective-permute-start(bf16[40,6144]{1,0:T(8,128)(2,1)S(1)} %bitcast.89), channel_id=1, source_target_pairs={{0,1},{1,0},{2,3},{3,2},{4,5},{5,4},{6,7},{7,6},{32,33},{33,32},{3... | collective-permute-start | bytes 1474568 | tf_op jit(solution)/shard_map/projected_exchange/ppermute | solution.py:45
  91.0 1.3 collective-permute-start.11
  93.9 14.0 %all-to-all-start.1 = ((bf16[8,40,160]{2,1,0:T(8,128)(2,1)}), bf16[8,40,160]{2,1,0:T(8,128)(2,1)S(1)}, u32[]{:S(2)}, u32[]{:S(2)}) async-start(bf16[8,40,160]{2,1,0:T(8,128)(2,1)} %bitcast.82), calls=%async_computation.1 | async-start | bytes 327680 | tf_op jit(solution)/shard_map/columns_exchange/all_to_all | solution.py:148
  108.9 48.3 %all-to-all-start.2 = ((bf16[8,80,640]{2,1,0:T(8,128)(2,1)}), bf16[8,80,640]{2,1,0:T(8,128)(2,1)S(1)}, u32[]{:S(2)}, u32[]{:S(2)}) async-start(bf16[8,80,640]{2,1,0:T(8,128)(2,1)} %broadcast_in_dim.32), calls=%async_computation.2 | async-start | bytes 1638400 | tf_op jit(solution)/shard_map/points/all_to_all | solution.py:158
  114.3 4.1 %collective-permute-start.12 = (bf16[40,1280]{1,0:T(8,128)(2,1)S(1)}, bf16[40,1280]{1,0:T(8,128)(2,1)S(1)}, u32[]{:S(2)}, u32[]{:S(2)}) collective-permute-start(bf16[40,1280]{1,0:T(8,128)(2,1)S(1)} %reshape.142), channel_id=1, source_target_pairs={{0,6},{1,25},{2,0},{3,27},{4,2},{5,29},{6,4},{7,31},{32,38},{33,57... | collective-permute-start | bytes 307208 | tf_op jit(solution)/shard_map/mixed_line/ppermute | solution.py:45
  115.5 5.1 %collective-permute-start.13 = (bf16[40,1280]{1,0:T(8,128)(2,1)S(1)}, bf16[40,1280]{1,0:T(8,128)(2,1)S(1)}, u32[]{:S(2)}, u32[]{:S(2)}) collective-permute-start(bf16[40,1280]{1,0:T(8,128)(2,1)S(1)} %reshape.142), channel_id=1, source_target_pairs={{0,4},{1,17},{2,6},{3,19},{4,0},{5,21},{6,2},{7,23},{32,36},{33,49... | collective-permute-start | bytes 307208 | tf_op jit(solution)/shard_map/mixed_line/ppermute | solution.py:45
  116.8 4.9 %collective-permute-start.14 = (bf16[40,1280]{1,0:T(8,128)(2,1)S(1)}, bf16[40,1280]{1,0:T(8,128)(2,1)S(1)}, u32[]{:S(2)}, u32[]{:S(2)}) collective-permute-start(bf16[40,1280]{1,0:T(8,128)(2,1)S(1)} %reshape.142), channel_id=1, source_target_pairs={{0,2},{1,9},{2,4},{3,11},{4,6},{5,13},{6,0},{7,15},{32,34},{33,41}... | collective-permute-start | bytes 307208 | tf_op jit(solution)/shard_map/mixed_line/ppermute | solution.py:45
  121.7 27.5 %collective-permute-start.15 = (bf16[160,1280]{1,0:T(8,128)(2,1)S(1)}, bf16[160,1280]{1,0:T(8,128)(2,1)S(1)}, u32[]{:S(2)}, u32[]{:S(2)}) collective-permute-start(bf16[160,1280]{1,0:T(8,128)(2,1)S(1)} %constant_dynamic-update-slice_fusion.2.m0), channel_id=1, source_target_pairs={{0,24},{1,7},{2,26},{3,1},{4,28},{5,3},{6,30},{7,5},{32,56},{33,39... | collective-permute-start | bytes 1228808 | tf_op jit(solution)/shard_map/mixed_plane/ppermute | solution.py:45
  124.8 28.7 %collective-permute-start.16 = (bf16[160,1280]{1,0:T(8,128)(2,1)S(1)}, bf16[160,1280]{1,0:T(8,128)(2,1)S(1)}, u32[]{:S(2)}, u32[]{:S(2)}) collective-permute-start(bf16[160,1280]{1,0:T(8,128)(2,1)S(1)} %constant_dynamic-update-slice_fusion.2.m0), channel_id=1, source_target_pairs={{0,16},{1,5},{2,18},{3,7},{4,20},{5,1},{6,22},{7,3},{32,48},{33,37... | collective-permute-start | bytes 1228808 | tf_op jit(solution)/shard_map/mixed_plane/ppermute | solution.py:45
  125.1 32.1 %collective-permute-start.17 = (bf16[160,1280]{1,0:T(8,128)(2,1)S(1)}, bf16[160,1280]{1,0:T(8,128)(2,1)S(1)}, u32[]{:S(2)}, u32[]{:S(2)}) collective-permute-start(bf16[160,1280]{1,0:T(8,128)(2,1)S(1)} %constant_dynamic-update-slice_fusion.2.m0), channel_id=1, source_target_pairs={{0,8},{1,3},{2,10},{3,5},{4,12},{5,7},{6,14},{7,1},{32,40},{33,35}... | collective-permute-start | bytes 1228808 | tf_op jit(solution)/shard_map/mixed_plane/ppermute | solution.py:45
  157.9 9.6 %collective-permute-start.18 = (f32[40,160]{1,0:T(8,128)S(1)}, f32[40,160]{1,0:T(8,128)S(1)}, u32[]{:S(2)}, u32[]{:S(2)}) collective-permute-start(f32[40,160]{1,0:T(8,128)S(1)} %slice.19), channel_id=1, source_target_pairs={{0,1},{1,0},{2,3},{3,2},{4,5},{5,4},{6,7},{7,6},{32,33},{33,32},{3... | collective-permute-start | bytes 76808 | tf_op jit(solution)/shard_map/output/ppermute | solution.py:45
  (7 other events, 19.2 us)

commit v4 on v3

--- a/solution.py
+++ b/solution.py
@@ -38,6 +38,8 @@
 TWO = lambda v: 2 if v % 2 == 0 else -2
 CROSS = lambda step: pairs(lambda x, y, z, c: (x + step(x), y, z, c))
 CORE = pairs(lambda x, y, z, c: (x, y, z, 1 - c))
+HALF = pairs(lambda x, y, z, c: (x, y, z + 4, c))
+ALONG_X = [[2 * x + half for x in range(4)] for half in range(2)]
 CHIPS = [[2 * chip + core for chip in range(16)] for core in range(2)]
 
 
@@ -137,7 +139,8 @@
         channel = jnp.concatenate([nt(both, u).astype(BF) for u in units], 1)
     lanes = 16 * width
     with jax.named_scope("columns_exchange"):
-        crossed = send(channel[width:], CORE)
+        crossed, later = lax.optimization_barrier((send(channel[width:], CORE), channel))
+        channel_pair = jnp.stack([channel, send(later, HALF)])
         block = jnp.arange(2 * lanes) // width
         dy, dz = (block // 8 - y) % 4, (block // 2 % 4 - z) % 4
         spot = jnp.where(block % 2 == 0, dy * 4 + dz, dz * 4 + dy) * width + jnp.arange(2 * lanes) % width
@@ -146,16 +149,22 @@
         ordered += jnp.dot(crossed, one_hot(jnp.where(mine, -1, spot), lanes), preferred_element_type=F32)
         ordered = ordered.astype(BF).reshape(width, 8, 4 * width).transpose(1, 0, 2)
         chosen = lax.all_to_all(ordered, "pt", 0, 0, tiled=True)
-        chosen, channel = lax.optimization_barrier((chosen, channel))
         chosen = chosen.astype(F32)
         antisym = coupling - coupling.T
-        mixed = jnp.einsum("qr,qin->irn", antisym, chosen, precision=lax.Precision.HIGHEST)
+        turned = antisym.reshape(8, 4, 2)[:, :, ::-1].reshape(8, 8)
+        turned = jnp.where(point % 2 == 0, antisym, turned)
+        mixed = jnp.einsum("qr,qin->irn", turned, chosen, precision=lax.Precision.HIGHEST)
         mixed = mixed.astype(BF).reshape(width, -1)
         linear = jnp.einsum("q,qin->in", weights, chosen, precision=lax.Precision.HIGHEST)
     with jax.named_scope("mixed_line"):
-        line = jnp.concatenate(gather_line(mixed, along(True, False)), 0)
+        pieces = list(gather_line(mixed, along(True, False)))
     with jax.named_scope("points"):
-        every = lax.all_to_all(jnp.broadcast_to(channel, (8,) + channel.shape), "pt", 0, 0, tiled=True)
+        channel_pair, pieces[1] = lax.optimization_barrier((channel_pair, pieces[1]))
+        every = jnp.broadcast_to(channel_pair, (4,) + channel_pair.shape)
+        every = lax.all_to_all(every, "pt", 0, 0, axis_index_groups=ALONG_X, tiled=True)
+        every = every.reshape((8,) + channel.shape)
+    with jax.named_scope("mixed_line"):
+        line = jnp.concatenate(pieces, 0)
     with jax.named_scope("mixed_plane"):
         planes = gather_line(line, along(False, False))
     with jax.named_scope("product"):

time: 169 us -> 150 us (0.89)
  the two profiles are of different devices: /device:TPU:67 before, /device:TPU:1 now
where the time goes in v4:
time: 150 us; the launch traced here: 149 us
  waiting for transfers between devices  78.9 us (53%)
  starting transfers between devices  45.5 us (30%)
  matrix products  11.7 us (8%)
  other arithmetic  7.61 us (5%)
  local copies, waits for them, and re-layouts  4.32 us (3%)
    ppermute x20, waiting for transfers between devices, send(): return lax.ppermute(value, AXES, perm)  65.6 us
    ppermute x20, starting transfers between devices, send(): return lax.ppermute(value, AXES, perm)  32.1 us
    all_to_all x1, waiting for transfers between devices, shards(): lax.all_to_all(blocks, 'pan', 0, 0, axis_index_groups=CHIPS, tiled=True)  13.1 us
    dot_general x8, matrix products, nt(): lax.dot_general(a, b, (((1,), (1,)), ((), ())), preferred_element_type=F32)  9.74 us
    all_to_all x1, starting transfers between devices, shards(): chosen = lax.all_to_all(ordered, 'pt', 0, 0, tiled=True)  5.82 us
    all_to_all x1, starting transfers between devices, shards(): lax.all_to_all(every, 'pt', 0, 0, axis_index_groups=ALONG_X, tiled=True)  3.99 us
    select_n x1, other arithmetic, shards(): jnp.where(core == 0, jnp.concatenate([rows, other_rows], 0), jnp.concaten...  3.97 us
    all_to_all x1, starting transfers between devices, shards(): lax.all_to_all(blocks, 'pan', 0, 0, axis_index_groups=CHIPS, tiled=True)  3.57 us
  transfers between devices with their start and end apart: 23, of which 18 were waited for; matrix products, arithmetic and copies ran while one was open for 9% of the time, Pallas kernels for 0%

profile of v4, /device:TPU:1, one launch (start us, length us, event | category | flops | bytes accessed | tf_op | source)
XLA Modules:
  0.0 149.1 jit_solution(1691825282021729279)
XLA Ops:
  0.0 3.2 %collective-permute-start.3 = (bf16[192,6144]{1,0:T(8,128)(2,1)}, bf16[192,6144]{1,0:T(8,128)(2,1)}, u32[]{:S(2)}, u32[]{:S(2)}) collective-permute-start(bf16[192,6144]{1,0:T(8,128)(2,1)} %bitcast.90), channel_id=1, source_target_pairs={{0,1},{1,0},{2,3},{3,2},{4,5},{5,4},{6,7},{7,6},{32,33},{33,32},{3... | collective-permute-start | bytes 7077896 | tf_op jit(solution)/shard_map/rows_pair/ppermute | solution.py:47
  5.3 6.1 %collective-permute-done = bf16[40,6144]{1,0:T(8,128)(2,1)S(1)} collective-permute-done((bf16[40,6144]{1,0:T(8,128)(2,1)}, bf16[40,6144]{1,0:T(8,128)(2,1)S(1)}, u32[]{:S(2)}, u32[]{:S(2)}) %collective-permute-start) | collective-permute-done | bytes 491552 | tf_op jit(solution)/shard_map/basis_line/ppermute | solution.py:47
  11.4 2.5 %collective-permute-done.1 = bf16[40,6144]{1,0:T(8,128)(2,1)S(1)} collective-permute-done((bf16[40,6144]{1,0:T(8,128)(2,1)}, bf16[40,6144]{1,0:T(8,128)(2,1)S(1)}, u32[]{:S(2)}, u32[]{:S(2)}) %collective-permute-start.1) | collective-permute-done | bytes 491552 | tf_op jit(solution)/shard_map/basis_line/ppermute | solution.py:47
  14.0 5.2 %collective-permute-done.2 = bf16[40,6144]{1,0:T(8,128)(2,1)S(1)} collective-permute-done((bf16[40,6144]{1,0:T(8,128)(2,1)}, bf16[40,6144]{1,0:T(8,128)(2,1)S(1)}, u32[]{:S(2)}, u32[]{:S(2)}) %collective-permute-start.2) | collective-permute-done | bytes 491552 | tf_op jit(solution)/shard_map/basis_line/ppermute | solution.py:47
  20.5 2.8 %collective-permute-start.4 = (bf16[40,6144]{1,0:T(8,128)(2,1)S(1)}, bf16[40,6144]{1,0:T(8,128)(2,1)S(1)}, u32[]{:S(2)}, u32[]{:S(2)}) collective-permute-start(bf16[40,6144]{1,0:T(8,128)(2,1)S(1)} %dynamic-slice_bitcast_fusion), channel_id=1, source_target_pairs={{0,16},{1,5},{2,18},{3,39},{4,20},{5,33},{6,22},{7,3},{32,48},{33,... | collective-permute-start | bytes 1474568 | tf_op jit(solution)/shard_map/basis_plane/ppermute | solution.py:47
  23.2 4.0 %maximum_select_fusion = bf16[384,6144]{1,0:T(8,128)(2,1)S(1)} fusion(bf16[192,6144]{1,0:T(8,128)(2,1)} %collective-permute-done.3, bf16[192,6144]{1,0:T(8,128)(2,1)S(1)} %bitcast.91, pred[]{:T(512)S(6)} %eq.79), kind=kLoop, calls=%fused_computation | loop fusion | flops 21233664 | bytes 9437185 | tf_op jit(solution)/shard_map/rows_pair/jit(_where)/select_n | solution.py:117
  27.2 5.6 %collective-permute-done.4 = bf16[40,6144]{1,0:T(8,128)(2,1)S(1)} collective-permute-done((bf16[40,6144]{1,0:T(8,128)(2,1)S(1)}, bf16[40,6144]{1,0:T(8,128)(2,1)S(1)}, u32[]{:S(2)}, u32[]{:S(2)}) %collective-permute-start.4) | collective-permute-done | bytes 491552 | tf_op jit(solution)/shard_map/basis_plane/ppermute | solution.py:47
  32.8 2.5 %collective-permute-start.6 = (bf16[40,6144]{1,0:T(8,128)(2,1)S(1)}, bf16[40,6144]{1,0:T(8,128)(2,1)S(1)}, u32[]{:S(2)}, u32[]{:S(2)}) collective-permute-start(bf16[40,6144]{1,0:T(8,128)(2,1)S(1)} %collective-permute-done.4), channel_id=1, source_target_pairs={{0,192},{1,193},{2,194},{3,195},{4,196},{5,197},{6,198},{7,199},{3... | collective-permute-start | bytes 1474568 | tf_op jit(solution)/shard_map/basis_plane/ppermute | solution.py:47
  37.0 2.8 %collective-permute-start.5 = (bf16[160,6144]{1,0:T(8,128)(2,1)S(1)}, bf16[160,6144]{1,0:T(8,128)(2,1)S(1)}, u32[]{:S(2)}, u32[]{:S(2)}) collective-permute-start(bf16[160,6144]{1,0:T(8,128)(2,1)S(1)} %pad_maximum_fusion), channel_id=1, source_target_pairs={{0,24},{1,39},{2,26},{3,1},{4,28},{5,3},{6,30},{7,5},{32,56},{33,7... | collective-permute-start | bytes 5898248 | tf_op jit(solution)/shard_map/basis_plane/ppermute | solution.py:47
  41.9 2.8 %collective-permute-done.6 = bf16[40,6144]{1,0:T(8,128)(2,1)S(1)} collective-permute-done((bf16[40,6144]{1,0:T(8,128)(2,1)S(1)}, bf16[40,6144]{1,0:T(8,128)(2,1)S(1)}, u32[]{:S(2)}, u32[]{:S(2)}) %collective-permute-start.6) | collective-permute-done | bytes 491552 | tf_op jit(solution)/shard_map/basis_plane/ppermute | solution.py:47
  44.7 3.2 %collective-permute-done.7 = bf16[40,6144]{1,0:T(8,128)(2,1)S(1)} collective-permute-done((bf16[40,6144]{1,0:T(8,128)(2,1)S(1)}, bf16[40,6144]{1,0:T(8,128)(2,1)S(1)}, u32[]{:S(2)}, u32[]{:S(2)}) %collective-permute-start.7) | collective-permute-done | bytes 491552 | tf_op jit(solution)/shard_map/basis_plane/ppermute | solution.py:47
  48.0 8.7 %collective-permute-done.8 = bf16[40,6144]{1,0:T(8,128)(2,1)S(1)} collective-permute-done((bf16[40,6144]{1,0:T(8,128)(2,1)S(1)}, bf16[40,6144]{1,0:T(8,128)(2,1)S(1)}, u32[]{:S(2)}, u32[]{:S(2)}) %collective-permute-start.8) | collective-permute-done | bytes 491552 | tf_op jit(solution)/shard_map/basis_plane/ppermute | solution.py:47
  58.4 3.0 %collective-permute-done.5 = bf16[160,6144]{1,0:T(8,128)(2,1)S(1)} collective-permute-done((bf16[160,6144]{1,0:T(8,128)(2,1)S(1)}, bf16[160,6144]{1,0:T(8,128)(2,1)S(1)}, u32[]{:S(2)}, u32[]{:S(2)}) %collective-permute-start.5) | collective-permute-done | bytes 1966112 | tf_op jit(solution)/shard_map/basis_plane/ppermute | solution.py:47
  67.8 3.6 %all-to-all-start = ((bf16[16,40,384]{2,1,0:T(8,128)(2,1)}), bf16[16,40,384]{2,1,0:T(8,128)(2,1)S(1)}, u32[]{:S(2)}, u32[]{:S(2)}) async-start(bf16[16,40,384]{2,1,0:T(8,128)(2,1)} %bitcast.18), calls=%async_computation | async-start | bytes 983040 | tf_op jit(solution)/shard_map/projected_exchange/all_to_all | solution.py:135
  71.6 13.1 %all-to-all-done = bf16[16,40,384]{2,1,0:T(8,128)(2,1)S(1)} async-done(((bf16[16,40,384]{2,1,0:T(8,128)(2,1)}), bf16[16,40,384]{2,1,0:T(8,128)(2,1)S(1)}, u32[]{:S(2)}, u32[]{:S(2)}) %all-to-all-start) | async-done | bytes 491552 | tf_op jit(solution)/shard_map/projected_exchange/all_to_all | solution.py:135
  84.8 3.4 %collective-permute-start.10 = (bf16[40,6144]{1,0:T(8,128)(2,1)S(1)}, bf16[40,6144]{1,0:T(8,128)(2,1)S(1)}, u32[]{:S(2)}, u32[]{:S(2)}) collective-permute-start(bf16[40,6144]{1,0:T(8,128)(2,1)S(1)} %bitcast.93), channel_id=1, source_target_pairs={{0,1},{1,0},{2,3},{3,2},{4,5},{5,4},{6,7},{7,6},{32,33},{33,32},{3... | collective-permute-start | bytes 1474568 | tf_op jit(solution)/shard_map/projected_exchange/ppermute | solution.py:47
  97.5 5.8 %all-to-all-start.1 = ((bf16[8,40,160]{2,1,0:T(8,128)(2,1)}), bf16[8,40,160]{2,1,0:T(8,128)(2,1)S(1)}, u32[]{:S(2)}, u32[]{:S(2)}) async-start(bf16[8,40,160]{2,1,0:T(8,128)(2,1)} %bitcast.85), calls=%async_computation.1 | async-start | bytes 327680 | tf_op jit(solution)/shard_map/columns_exchange/all_to_all | solution.py:151
  103.3 5.4 %collective-permute-start.12 = (bf16[80,640]{1,0:T(8,128)(2,1)S(1)}, bf16[80,640]{1,0:T(8,128)(2,1)S(1)}, u32[]{:S(2)}, u32[]{:S(2)}) collective-permute-start(bf16[80,640]{1,0:T(8,128)(2,1)S(1)} %pad_maximum_fusion.2), channel_id=1, source_target_pairs={{0,32},{1,33},{2,34},{3,35},{4,36},{5,37},{6,38},{7,39},{32,0},{33... | collective-permute-start | bytes 307208 | tf_op jit(solution)/shard_map/columns_exchange/ppermute | solution.py:47
  108.8 4.0 %collective-permute-done.12 = bf16[80,640]{1,0:T(8,128)(2,1)S(1)} collective-permute-done((bf16[80,640]{1,0:T(8,128)(2,1)S(1)}, bf16[80,640]{1,0:T(8,128)(2,1)S(1)}, u32[]{:S(2)}, u32[]{:S(2)}) %collective-permute-start.12) | collective-permute-done | bytes 102432 | tf_op jit(solution)/shard_map/columns_exchange/ppermute | solution.py:47
  115.3 1.7 %collective-permute-done.13 = bf16[40,1280]{1,0:T(8,128)(2,1)S(1)} collective-permute-done((bf16[40,1280]{1,0:T(8,128)(2,1)S(1)}, bf16[40,1280]{1,0:T(8,128)(2,1)S(1)}, u32[]{:S(2)}, u32[]{:S(2)}) %collective-permute-start.13) | collective-permute-done | bytes 102432 | tf_op jit(solution)/shard_map/mixed_line/ppermute | solution.py:47
  118.0 4.0 %all-to-all-start.2 = ((bf16[4,2,80,640]{3,2,1,0:T(8,128)(2,1)}), bf16[4,2,80,640]{3,2,1,0:T(8,128)(2,1)S(1)}, u32[]{:S(2)}, u32[]{:S(2)}) async-start(bf16[4,2,80,640]{3,2,1,0:T(8,128)(2,1)} %broadcast_in_dim.32), calls=%async_computation.2 | async-start | bytes 1638400 | tf_op jit(solution)/shard_map/points/all_to_all | solution.py:164
  123.5 4.4 %collective-permute-start.17 = (bf16[160,1280]{1,0:T(8,128)(2,1)S(1)}, bf16[160,1280]{1,0:T(8,128)(2,1)S(1)}, u32[]{:S(2)}, u32[]{:S(2)}) collective-permute-start(bf16[160,1280]{1,0:T(8,128)(2,1)S(1)} %constant_dynamic-update-slice_fusion.2.m0), channel_id=1, source_target_pairs={{0,16},{1,5},{2,18},{3,7},{4,20},{5,1},{6,22},{7,3},{32,48},{33,37... | collective-permute-start | bytes 1228808 | tf_op jit(solution)/shard_map/mixed_plane/ppermute | solution.py:47
  127.9 4.5 %collective-permute-done.16.m1 = bf16[160,1280]{1,0:T(8,128)(2,1)S(1)} collective-permute-done((bf16[160,1280]{1,0:T(8,128)(2,1)S(1)}, bf16[160,1280]{1,0:T(8,128)(2,1)S(1)}, u32[]{:S(2)}, u32[]{:S(2)}) %collective-permute-start.16) | collective-permute-done | bytes 409632 | tf_op jit(solution)/shard_map/mixed_plane/ppermute | solution.py:47
  132.4 14.0 %collective-permute-done.17.m2 = bf16[160,1280]{1,0:T(8,128)(2,1)S(1)} collective-permute-done((bf16[160,1280]{1,0:T(8,128)(2,1)S(1)}, bf16[160,1280]{1,0:T(8,128)(2,1)S(1)}, u32[]{:S(2)}, u32[]{:S(2)}) %collective-permute-start.17) | collective-permute-done | bytes 409632 | tf_op jit(solution)/shard_map/mixed_plane/ppermute | solution.py:47
  (93 shorter events, 32.3 us)
Async XLA Ops:
  0.0 147.3 %copy-start = (f32[8]{0:T(128)S(1)}, f32[8]{0:T(128)}, u32[]{:S(2)}) copy-start(f32[8]{0:T(128)} %param.6) | copy-start | bytes 100
  0.0 20.4 %collective-permute-start.3 = (bf16[192,6144]{1,0:T(8,128)(2,1)}, bf16[192,6144]{1,0:T(8,128)(2,1)}, u32[]{:S(2)}, u32[]{:S(2)}) collective-permute-start(bf16[192,6144]{1,0:T(8,128)(2,1)} %bitcast.90), channel_id=1, source_target_pairs={{0,1},{1,0},{2,3},{3,2},{4,5},{5,4},{6,7},{7,6},{32,33},{33,32},{3... | collective-permute-start | bytes 7077896 | tf_op jit(solution)/shard_map/rows_pair/ppermute | solution.py:47
  3.2 8.2 %collective-permute-start = (bf16[40,6144]{1,0:T(8,128)(2,1)}, bf16[40,6144]{1,0:T(8,128)(2,1)S(1)}, u32[]{:S(2)}, u32[]{:S(2)}) collective-permute-start(bf16[40,6144]{1,0:T(8,128)(2,1)} %bitcast.103), channel_id=1, source_target_pairs={{0,38},{1,25},{2,0},{3,27},{4,2},{5,29},{6,4},{7,31},{32,6},{33,57... | collective-permute-start | bytes 1474568 | tf_op jit(solution)/shard_map/basis_line/ppermute | solution.py:47
  4.2 9.7 %collective-permute-start.1 = (bf16[40,6144]{1,0:T(8,128)(2,1)}, bf16[40,6144]{1,0:T(8,128)(2,1)S(1)}, u32[]{:S(2)}, u32[]{:S(2)}) collective-permute-start(bf16[40,6144]{1,0:T(8,128)(2,1)} %bitcast.104), channel_id=1, source_target_pairs={{0,4},{1,17},{2,38},{3,19},{4,32},{5,21},{6,2},{7,23},{32,36},{33,... | collective-permute-start | bytes 1474568 | tf_op jit(solution)/shard_map/basis_line/ppermute | solution.py:47
  4.6 14.6 %collective-permute-start.2 = (bf16[40,6144]{1,0:T(8,128)(2,1)}, bf16[40,6144]{1,0:T(8,128)(2,1)S(1)}, u32[]{:S(2)}, u32[]{:S(2)}) collective-permute-start(bf16[40,6144]{1,0:T(8,128)(2,1)} %bitcast.105), channel_id=1, source_target_pairs={{0,2},{1,9},{2,4},{3,11},{4,6},{5,13},{6,32},{7,15},{32,34},{33,41... | collective-permute-start | bytes 1474568 | tf_op jit(solution)/shard_map/basis_line/ppermute | solution.py:47
  20.5 12.3 %collective-permute-start.4 = (bf16[40,6144]{1,0:T(8,128)(2,1)S(1)}, bf16[40,6144]{1,0:T(8,128)(2,1)S(1)}, u32[]{:S(2)}, u32[]{:S(2)}) collective-permute-start(bf16[40,6144]{1,0:T(8,128)(2,1)S(1)} %dynamic-slice_bitcast_fusion), channel_id=1, source_target_pairs={{0,16},{1,5},{2,18},{3,39},{4,20},{5,33},{6,22},{7,3},{32,48},{33,... | collective-permute-start | bytes 1474568 | tf_op jit(solution)/shard_map/basis_plane/ppermute | solution.py:47
  32.8 11.9 %collective-permute-start.6 = (bf16[40,6144]{1,0:T(8,128)(2,1)S(1)}, bf16[40,6144]{1,0:T(8,128)(2,1)S(1)}, u32[]{:S(2)}, u32[]{:S(2)}) collective-permute-start(bf16[40,6144]{1,0:T(8,128)(2,1)S(1)} %collective-permute-done.4), channel_id=1, source_target_pairs={{0,192},{1,193},{2,194},{3,195},{4,196},{5,197},{6,198},{7,199},{3... | collective-permute-start | bytes 1474568 | tf_op jit(solution)/shard_map/basis_plane/ppermute | solution.py:47
  35.3 12.7 %collective-permute-start.7 = (bf16[40,6144]{1,0:T(8,128)(2,1)S(1)}, bf16[40,6144]{1,0:T(8,128)(2,1)S(1)}, u32[]{:S(2)}, u32[]{:S(2)}) collective-permute-start(bf16[40,6144]{1,0:T(8,128)(2,1)S(1)} %collective-permute-done.4), channel_id=1, source_target_pairs={{0,64},{1,65},{2,66},{3,67},{4,68},{5,69},{6,70},{7,71},{32,96},{3... | collective-permute-start | bytes 1474568 | tf_op jit(solution)/shard_map/basis_plane/ppermute | solution.py:47
  35.3 21.4 %collective-permute-start.8 = (bf16[40,6144]{1,0:T(8,128)(2,1)S(1)}, bf16[40,6144]{1,0:T(8,128)(2,1)S(1)}, u32[]{:S(2)}, u32[]{:S(2)}) collective-permute-start(bf16[40,6144]{1,0:T(8,128)(2,1)S(1)} %collective-permute-done.4), channel_id=1, source_target_pairs={{0,128},{1,129},{2,130},{3,131},{4,132},{5,133},{6,134},{7,135},{3... | collective-permute-start | bytes 1474568 | tf_op jit(solution)/shard_map/basis_plane/ppermute | solution.py:47
  37.0 24.4 %collective-permute-start.5 = (bf16[160,6144]{1,0:T(8,128)(2,1)S(1)}, bf16[160,6144]{1,0:T(8,128)(2,1)S(1)}, u32[]{:S(2)}, u32[]{:S(2)}) collective-permute-start(bf16[160,6144]{1,0:T(8,128)(2,1)S(1)} %pad_maximum_fusion), channel_id=1, source_target_pairs={{0,24},{1,39},{2,26},{3,1},{4,28},{5,3},{6,30},{7,5},{32,56},{33,7... | collective-permute-start | bytes 5898248 | tf_op jit(solution)/shard_map/basis_plane/ppermute | solution.py:47
  39.8 25.0 %collective-permute-start.9 = (bf16[160,6144]{1,0:T(8,128)(2,1)S(1)}, bf16[160,6144]{1,0:T(8,128)(2,1)S(1)}, u32[]{:S(2)}, u32[]{:S(2)}) collective-permute-start(bf16[160,6144]{1,0:T(8,128)(2,1)S(1)} %pad_maximum_fusion), channel_id=1, source_target_pairs={{0,8},{1,3},{2,10},{3,5},{4,12},{5,7},{6,14},{7,33},{32,40},{33,35... | collective-permute-start | bytes 5898248 | tf_op jit(solution)/shard_map/basis_plane/ppermute | solution.py:47
  67.8 16.9 %all-to-all-start = ((bf16[16,40,384]{2,1,0:T(8,128)(2,1)}), bf16[16,40,384]{2,1,0:T(8,128)(2,1)S(1)}, u32[]{:S(2)}, u32[]{:S(2)}) async-start(bf16[16,40,384]{2,1,0:T(8,128)(2,1)} %bitcast.18), calls=%async_computation | async-start | bytes 983040 | tf_op jit(solution)/shard_map/projected_exchange/all_to_all | solution.py:135
  84.8 4.9 %collective-permute-start.10 = (bf16[40,6144]{1,0:T(8,128)(2,1)S(1)}, bf16[40,6144]{1,0:T(8,128)(2,1)S(1)}, u32[]{:S(2)}, u32[]{:S(2)}) collective-permute-start(bf16[40,6144]{1,0:T(8,128)(2,1)S(1)} %bitcast.93), channel_id=1, source_target_pairs={{0,1},{1,0},{2,3},{3,2},{4,5},{5,4},{6,7},{7,6},{32,33},{33,32},{3... | collective-permute-start | bytes 1474568 | tf_op jit(solution)/shard_map/projected_exchange/ppermute | solution.py:47
  94.6 1.3 collective-permute-start.11
  97.5 15.5 %all-to-all-start.1 = ((bf16[8,40,160]{2,1,0:T(8,128)(2,1)}), bf16[8,40,160]{2,1,0:T(8,128)(2,1)S(1)}, u32[]{:S(2)}, u32[]{:S(2)}) async-start(bf16[8,40,160]{2,1,0:T(8,128)(2,1)} %bitcast.85), calls=%async_computation.1 | async-start | bytes 327680 | tf_op jit(solution)/shard_map/columns_exchange/all_to_all | solution.py:151
  103.3 9.5 %collective-permute-start.12 = (bf16[80,640]{1,0:T(8,128)(2,1)S(1)}, bf16[80,640]{1,0:T(8,128)(2,1)S(1)}, u32[]{:S(2)}, u32[]{:S(2)}) collective-permute-start(bf16[80,640]{1,0:T(8,128)(2,1)S(1)} %pad_maximum_fusion.2), channel_id=1, source_target_pairs={{0,32},{1,33},{2,34},{3,35},{4,36},{5,37},{6,38},{7,39},{32,0},{33... | collective-permute-start | bytes 307208 | tf_op jit(solution)/shard_map/columns_exchange/ppermute | solution.py:47
  113.5 3.6 %collective-permute-start.13 = (bf16[40,1280]{1,0:T(8,128)(2,1)S(1)}, bf16[40,1280]{1,0:T(8,128)(2,1)S(1)}, u32[]{:S(2)}, u32[]{:S(2)}) collective-permute-start(bf16[40,1280]{1,0:T(8,128)(2,1)S(1)} %reshape.153), channel_id=1, source_target_pairs={{0,6},{1,25},{2,0},{3,27},{4,2},{5,29},{6,4},{7,31},{32,38},{33,57... | collective-permute-start | bytes 307208 | tf_op jit(solution)/shard_map/mixed_line/ppermute | solution.py:47
  114.1 7.9 %collective-permute-start.14 = (bf16[40,1280]{1,0:T(8,128)(2,1)S(1)}, bf16[40,1280]{1,0:T(8,128)(2,1)S(1)}, u32[]{:S(2)}, u32[]{:S(2)}) collective-permute-start(bf16[40,1280]{1,0:T(8,128)(2,1)S(1)} %reshape.153), channel_id=1, source_target_pairs={{0,4},{1,17},{2,6},{3,19},{4,0},{5,21},{6,2},{7,23},{32,36},{33,49... | collective-permute-start | bytes 307208 | tf_op jit(solution)/shard_map/mixed_line/ppermute | solution.py:47
  115.3 6.7 %collective-permute-start.15 = (bf16[40,1280]{1,0:T(8,128)(2,1)S(1)}, bf16[40,1280]{1,0:T(8,128)(2,1)S(1)}, u32[]{:S(2)}, u32[]{:S(2)}) collective-permute-start(bf16[40,1280]{1,0:T(8,128)(2,1)S(1)} %reshape.153), channel_id=1, source_target_pairs={{0,2},{1,9},{2,4},{3,11},{4,6},{5,13},{6,0},{7,15},{32,34},{33,41}... | collective-permute-start | bytes 307208 | tf_op jit(solution)/shard_map/mixed_line/ppermute | solution.py:47
  118.0 28.4 %all-to-all-start.2 = ((bf16[4,2,80,640]{3,2,1,0:T(8,128)(2,1)}), bf16[4,2,80,640]{3,2,1,0:T(8,128)(2,1)S(1)}, u32[]{:S(2)}, u32[]{:S(2)}) async-start(bf16[4,2,80,640]{3,2,1,0:T(8,128)(2,1)} %broadcast_in_dim.32), calls=%async_computation.2 | async-start | bytes 1638400 | tf_op jit(solution)/shard_map/points/all_to_all | solution.py:164
  122.1 10.3 %collective-permute-start.16 = (bf16[160,1280]{1,0:T(8,128)(2,1)S(1)}, bf16[160,1280]{1,0:T(8,128)(2,1)S(1)}, u32[]{:S(2)}, u32[]{:S(2)}) collective-permute-start(bf16[160,1280]{1,0:T(8,128)(2,1)S(1)} %constant_dynamic-update-slice_fusion.2.m0), channel_id=1, source_target_pairs={{0,24},{1,7},{2,26},{3,1},{4,28},{5,3},{6,30},{7,5},{32,56},{33,39... | collective-permute-start | bytes 1228808 | tf_op jit(solution)/shard_map/mixed_plane/ppermute | solution.py:47
  123.5 22.9 %collective-permute-start.17 = (bf16[160,1280]{1,0:T(8,128)(2,1)S(1)}, bf16[160,1280]{1,0:T(8,128)(2,1)S(1)}, u32[]{:S(2)}, u32[]{:S(2)}) collective-permute-start(bf16[160,1280]{1,0:T(8,128)(2,1)S(1)} %constant_dynamic-update-slice_fusion.2.m0), channel_id=1, source_target_pairs={{0,16},{1,5},{2,18},{3,7},{4,20},{5,1},{6,22},{7,3},{32,48},{33,37... | collective-permute-start | bytes 1228808 | tf_op jit(solution)/shard_map/mixed_plane/ppermute | solution.py:47
  127.9 18.5 %collective-permute-start.18 = (bf16[160,1280]{1,0:T(8,128)(2,1)S(1)}, bf16[160,1280]{1,0:T(8,128)(2,1)S(1)}, u32[]{:S(2)}, u32[]{:S(2)}) collective-permute-start(bf16[160,1280]{1,0:T(8,128)(2,1)S(1)} %constant_dynamic-update-slice_fusion.2.m0), channel_id=1, source_target_pairs={{0,8},{1,3},{2,10},{3,5},{4,12},{5,7},{6,14},{7,1},{32,40},{33,35}... | collective-permute-start | bytes 1228808 | tf_op jit(solution)/shard_map/mixed_plane/ppermute | solution.py:47
  147.2 1.3 collective-permute-start.19
  (8 other events, 33.1 us)

commit v5 on v4

--- a/solution.py
+++ b/solution.py
@@ -40,7 +40,6 @@
 CORE = pairs(lambda x, y, z, c: (x, y, z, 1 - c))
 HALF = pairs(lambda x, y, z, c: (x, y, z + 4, c))
 ALONG_X = [[2 * x + half for x in range(4)] for half in range(2)]
-CHIPS = [[2 * chip + core for chip in range(16)] for core in range(2)]
 
 
 def send(value, perm):
@@ -58,11 +57,40 @@
     return lax.dot_general(a, b, (((1,), (1,)), ((), ())), preferred_element_type=F32)
 
 
-def unroll(blocks, start):
-    return lax.dynamic_slice_in_dim(jnp.concatenate([blocks, blocks], 0), (4 - start) % 4, 4, 0)
-
-
 INTERPRET = False
+
+
+def channel_kernel(place_ref, own_ref, other_ref, u0, u1, u2, u3, out_ref, left):
+    y, z, core = place_ref[0], place_ref[1], place_ref[2]
+    _, _, width, depth = own_ref.shape
+    pad = -(-width // 16) * 16
+    for first in range(4):
+        for second in range(4):
+            straight = (y + second) % 4 * 4 + (z + first) % 4
+            across = (y + first) % 4 * 4 + (z + second) % 4
+            mine = pl.multiple_of(jnp.where(core == 0, straight, across) * depth, depth)
+            theirs = pl.multiple_of(jnp.where(core == 0, across, straight) * depth, depth)
+            left[:width, pl.ds(mine, depth)] = own_ref[first, second]
+            left[pad : pad + width, pl.ds(theirs, depth)] = other_ref[first, second]
+    for a, u in enumerate((u0, u1, u2, u3)):
+        part = u.shape[0]
+        block = nt(left[...], u[...]).astype(BF)
+        out_ref[0, :, a * part : (a + 1) * part] = block[:width]
+        out_ref[1, :, a * part : (a + 1) * part] = block[pad : pad + width]
+
+
+def channel_blocks(place_index, own, other, units):
+    _, _, width, depth = own.shape
+    vmem = pl.BlockSpec(memory_space=pltpu.VMEM)
+    return pl.pallas_call(
+        channel_kernel,
+        out_shape=jax.ShapeDtypeStruct((2, width, 4 * units[0].shape[0]), BF),
+        in_specs=[pl.BlockSpec(memory_space=pltpu.SMEM)] + [vmem] * 6,
+        out_specs=vmem,
+        scratch_shapes=[pltpu.VMEM((2 * (-(-width // 16) * 16), 16 * depth), BF)],
+        compiler_params=pltpu.CompilerParams(vmem_limit_bytes=48 * 1024 * 1024),
+        interpret=INTERPRET,
+    )(place_index, own, other, *units)
 
 
 def product_kernel(left_ref, m0, m1, m2, m3, out_ref, right):
@@ -104,8 +132,6 @@
     core = pan % 2
     chip = pan // 2
     x, y, z = point // 2, chip // 4, chip % 4
-    second = jnp.where(core == 0, y, z)
-    first = jnp.where(core == 0, z, y)
     rows = potential[0]
     panel = basis.T
     width, depth = panel.shape
@@ -128,24 +154,27 @@
             two = lax.dynamic_update_index_in_dim(two, piece, (x + step) % 4, 0)
         units = line, send(line, plane(DOWN)), two.reshape(4 * width, depth), send(line, plane(UP))
     with jax.named_scope("projected"):
-        parts = [unroll(nt(u, chip_rows).astype(BF).reshape(4, width, -1), first) for u in units]
-        blocks = unroll(jnp.stack(parts), second)
-        blocks = jnp.where(core == 0, blocks, blocks.transpose(1, 0, 2, 3)).reshape(16, width, -1)
-    with jax.named_scope("projected_exchange"):
-        got = lax.all_to_all(blocks, "pan", 0, 0, axis_index_groups=CHIPS, tiled=True)
-        own = got.transpose(1, 0, 2).reshape(width, depth)
-        both = jnp.concatenate([own, send(own, CORE)], 0)
+        back, aside = along(False, False), along(True, False)
+        parts = [nt(u, chip_rows).astype(BF).reshape(4, width, -1) for u in units]
+    with jax.named_scope("projected_back"):
+        parts = parts[0], send(parts[3], back(DOWN)), send(parts[2], back(TWO)), send(parts[1], back(UP))
+    with jax.named_scope("projected_aside"):
+        parts = [jnp.stack([part[b] for part in parts]) for b in range(4)]
+        own = jnp.stack(
+            [parts[0], send(parts[3], aside(DOWN)), send(parts[2], aside(TWO)), send(parts[1], aside(UP))]
+        )
+        other = send(own, CORE)
     with jax.named_scope("channel"):
-        channel = jnp.concatenate([nt(both, u).astype(BF) for u in units], 1)
+        channel = channel_blocks(jnp.stack([y, z, core]), own, other, units)
     lanes = 16 * width
     with jax.named_scope("columns_exchange"):
-        crossed, later = lax.optimization_barrier((send(channel[width:], CORE), channel))
-        channel_pair = jnp.stack([channel, send(later, HALF)])
+        channel_pair = jnp.stack([channel, send(channel, HALF)])
+        crossed = send(channel[1], CORE)
         block = jnp.arange(2 * lanes) // width
         dy, dz = (block // 8 - y) % 4, (block // 2 % 4 - z) % 4
         spot = jnp.where(block % 2 == 0, dy * 4 + dz, dz * 4 + dy) * width + jnp.arange(2 * lanes) % width
         mine = block % 2 == core
-        ordered = jnp.dot(channel[:width], one_hot(jnp.where(mine, spot, -1), lanes), preferred_element_type=F32)
+        ordered = jnp.dot(channel[0], one_hot(jnp.where(mine, spot, -1), lanes), preferred_element_type=F32)
         ordered += jnp.dot(crossed, one_hot(jnp.where(mine, -1, spot), lanes), preferred_element_type=F32)
         ordered = ordered.astype(BF).reshape(width, 8, 4 * width).transpose(1, 0, 2)
         chosen = lax.all_to_all(ordered, "pt", 0, 0, tiled=True)
@@ -162,7 +191,7 @@
         channel_pair, pieces[1] = lax.optimization_barrier((channel_pair, pieces[1]))
         every = jnp.broadcast_to(channel_pair, (4,) + channel_pair.shape)
         every = lax.all_to_all(every, "pt", 0, 0, axis_index_groups=ALONG_X, tiled=True)
-        every = every.reshape((8,) + channel.shape)
+        every = every.reshape(8, 2 * width, -1)
     with jax.named_scope("mixed_line"):
         line = jnp.concatenate(pieces, 0)
     with jax.named_scope("mixed_plane"):

time: 150 us -> 151 us (level)
  Pallas kernels: 0.72 us -> 5.65 us
  matrix products: 11.7 us -> 8.59 us
    all_to_all x1 -> x0, waiting for transfers between devices: 13.1 us -> none  [shards(): lax.all_to_all(blocks, 'pan', 0, 0, axis_index_groups=CHIPS, tiled=True)]
    all_to_all x1, waiting for transfers between devices: 0.19 us -> 8.96 us  [shards(): chosen = lax.all_to_all(ordered, 'pt', 0, 0, tiled=True)]
    ppermute x20 -> x26, starting transfers between devices: 32.1 us -> 38.7 us  [send(): return lax.ppermute(value, AXES, perm)]
    ppermute x20 -> x26, waiting for transfers between devices: 65.6 us -> 70.6 us  [send(): return lax.ppermute(value, AXES, perm)]
    pallas_call x0 -> x1, Pallas kernels: none -> 4.94 us  [channel_blocks(): pl.pallas_call(channel_kernel, out_shape=jax.ShapeDtypeStruct((2, width,...]
    all_to_all x1 -> x0, starting transfers between devices: 3.57 us -> none  [shards(): lax.all_to_all(blocks, 'pan', 0, 0, axis_index_groups=CHIPS, tiled=True)]
    dot_general x8 -> x4, matrix products: 9.74 us -> 6.63 us  [nt(): lax.dot_general(a, b, (((1,), (1,)), ((), ())), preferred_element_type=F32)]
    all_to_all x1, starting transfers between devices: 5.82 us -> 3.76 us  [shards(): chosen = lax.all_to_all(ordered, 'pt', 0, 0, tiled=True)]
  transfers between devices with their start and end apart: 23 -> 28, of which waited for: 18 -> 20; matrix products, arithmetic and copies ran while one was open for 9% -> 11% of each run, Pallas kernels for 0% -> 0%
where the time goes in v5:
time: 151 us
  waiting for transfers between devices  79.6 us (53%)
  starting transfers between devices  45.9 us (30%)
  matrix products  8.59 us (6%)
  other arithmetic  6.15 us (4%)
  Pallas kernels  5.65 us (4%)
  local copies, waits for them, and re-layouts  4.21 us (3%)
    ppermute x26, waiting for transfers between devices, send(): return lax.ppermute(value, AXES, perm)  70.6 us
    ppermute x26, starting transfers between devices, send(): return lax.ppermute(value, AXES, perm)  38.7 us
    all_to_all x1, waiting for transfers between devices, shards(): chosen = lax.all_to_all(ordered, 'pt', 0, 0, tiled=True)  8.96 us
    dot_general x4, matrix products, nt(): lax.dot_general(a, b, (((1,), (1,)), ((), ())), preferred_element_type=F32)  6.63 us
    pallas_call x1, Pallas kernels, channel_blocks(): pl.pallas_call(channel_kernel, out_shape=jax.ShapeDtypeStruct((2, width,...  4.94 us
    select_n x1, other arithmetic, shards(): jnp.where(core == 0, jnp.concatenate([rows, other_rows], 0), jnp.concaten...  3.97 us
    all_to_all x1, starting transfers between devices, shards(): chosen = lax.all_to_all(ordered, 'pt', 0, 0, tiled=True)  3.76 us
    all_to_all x1, starting transfers between devices, shards(): lax.all_to_all(every, 'pt', 0, 0, axis_index_groups=ALONG_X, tiled=True)  3.5 us
  transfers between devices with their start and end apart: 28, of which 20 were waited for; matrix products, arithmetic and copies ran while one was open for 11% of the time, Pallas kernels for 0%

profile of v5, /device:TPU:1, one launch (start us, length us, event | category | flops | bytes accessed | tf_op | source)
XLA Modules:
  0.0 150.5 jit_solution(15427254633514185616)
XLA Ops:
  0.0 3.2 %collective-permute-start.3 = (bf16[192,6144]{1,0:T(8,128)(2,1)}, bf16[192,6144]{1,0:T(8,128)(2,1)}, u32[]{:S(2)}, u32[]{:S(2)}) collective-permute-start(bf16[192,6144]{1,0:T(8,128)(2,1)} %bitcast.72), channel_id=1, source_target_pairs={{0,1},{1,0},{2,3},{3,2},{4,5},{5,4},{6,7},{7,6},{32,33},{33,32},{3... | collective-permute-start | bytes 7077896 | tf_op jit(solution)/shard_map/rows_pair/ppermute | solution.py:46
  5.3 6.1 %collective-permute-done = bf16[40,6144]{1,0:T(8,128)(2,1)S(1)} collective-permute-done((bf16[40,6144]{1,0:T(8,128)(2,1)}, bf16[40,6144]{1,0:T(8,128)(2,1)S(1)}, u32[]{:S(2)}, u32[]{:S(2)}) %collective-permute-start) | collective-permute-done | bytes 491552 | tf_op jit(solution)/shard_map/basis_line/ppermute | solution.py:46
  11.4 2.5 %collective-permute-done.1 = bf16[40,6144]{1,0:T(8,128)(2,1)S(1)} collective-permute-done((bf16[40,6144]{1,0:T(8,128)(2,1)}, bf16[40,6144]{1,0:T(8,128)(2,1)S(1)}, u32[]{:S(2)}, u32[]{:S(2)}) %collective-permute-start.1) | collective-permute-done | bytes 491552 | tf_op jit(solution)/shard_map/basis_line/ppermute | solution.py:46
  14.0 5.2 %collective-permute-done.2 = bf16[40,6144]{1,0:T(8,128)(2,1)S(1)} collective-permute-done((bf16[40,6144]{1,0:T(8,128)(2,1)}, bf16[40,6144]{1,0:T(8,128)(2,1)S(1)}, u32[]{:S(2)}, u32[]{:S(2)}) %collective-permute-start.2) | collective-permute-done | bytes 491552 | tf_op jit(solution)/shard_map/basis_line/ppermute | solution.py:46
  20.5 2.8 %collective-permute-start.4 = (bf16[40,6144]{1,0:T(8,128)(2,1)S(1)}, bf16[40,6144]{1,0:T(8,128)(2,1)S(1)}, u32[]{:S(2)}, u32[]{:S(2)}) collective-permute-start(bf16[40,6144]{1,0:T(8,128)(2,1)S(1)} %dynamic-slice_bitcast_fusion), channel_id=1, source_target_pairs={{0,16},{1,5},{2,18},{3,39},{4,20},{5,33},{6,22},{7,3},{32,48},{33,... | collective-permute-start | bytes 1474568 | tf_op jit(solution)/shard_map/basis_plane/ppermute | solution.py:46
  23.2 4.0 %maximum_select_fusion = bf16[384,6144]{1,0:T(8,128)(2,1)S(1)} fusion(bf16[192,6144]{1,0:T(8,128)(2,1)} %collective-permute-done.3, bf16[192,6144]{1,0:T(8,128)(2,1)S(1)} %bitcast.73, pred[]{:T(512)S(6)} %eq.71), kind=kLoop, calls=%fused_computation | loop fusion | flops 21233664 | bytes 9437185 | tf_op jit(solution)/shard_map/rows_pair/jit(_where)/select_n | solution.py:143
  27.2 5.6 %collective-permute-done.4 = bf16[40,6144]{1,0:T(8,128)(2,1)S(1)} collective-permute-done((bf16[40,6144]{1,0:T(8,128)(2,1)S(1)}, bf16[40,6144]{1,0:T(8,128)(2,1)S(1)}, u32[]{:S(2)}, u32[]{:S(2)}) %collective-permute-start.4) | collective-permute-done | bytes 491552 | tf_op jit(solution)/shard_map/basis_plane/ppermute | solution.py:46
  32.8 2.5 %collective-permute-start.7 = (bf16[40,6144]{1,0:T(8,128)(2,1)S(1)}, bf16[40,6144]{1,0:T(8,128)(2,1)S(1)}, u32[]{:S(2)}, u32[]{:S(2)}) collective-permute-start(bf16[40,6144]{1,0:T(8,128)(2,1)S(1)} %collective-permute-done.4), channel_id=1, source_target_pairs={{0,192},{1,193},{2,194},{3,195},{4,196},{5,197},{6,198},{7,199},{3... | collective-permute-start | bytes 1474568 | tf_op jit(solution)/shard_map/basis_plane/ppermute | solution.py:46
  37.0 2.8 %collective-permute-start.11 = (bf16[160,6144]{1,0:T(8,128)(2,1)S(1)}, bf16[160,6144]{1,0:T(8,128)(2,1)S(1)}, u32[]{:S(2)}, u32[]{:S(2)}) collective-permute-start(bf16[160,6144]{1,0:T(8,128)(2,1)S(1)} %pad_maximum_fusion.u0), channel_id=1, source_target_pairs={{0,24},{1,39},{2,26},{3,1},{4,28},{5,3},{6,30},{7,5},{32,56},{33,7... | collective-permute-start | bytes 5898248 | tf_op jit(solution)/shard_map/basis_plane/ppermute | solution.py:46
  41.8 2.9 %collective-permute-done.7 = bf16[40,6144]{1,0:T(8,128)(2,1)S(1)} collective-permute-done((bf16[40,6144]{1,0:T(8,128)(2,1)S(1)}, bf16[40,6144]{1,0:T(8,128)(2,1)S(1)}, u32[]{:S(2)}, u32[]{:S(2)}) %collective-permute-start.7) | collective-permute-done | bytes 491552 | tf_op jit(solution)/shard_map/basis_plane/ppermute | solution.py:46
  44.7 3.2 %collective-permute-done.8 = bf16[40,6144]{1,0:T(8,128)(2,1)S(1)} collective-permute-done((bf16[40,6144]{1,0:T(8,128)(2,1)S(1)}, bf16[40,6144]{1,0:T(8,128)(2,1)S(1)}, u32[]{:S(2)}, u32[]{:S(2)}) %collective-permute-start.8) | collective-permute-done | bytes 491552 | tf_op jit(solution)/shard_map/basis_plane/ppermute | solution.py:46
  48.0 8.7 %collective-permute-done.9 = bf16[40,6144]{1,0:T(8,128)(2,1)S(1)} collective-permute-done((bf16[40,6144]{1,0:T(8,128)(2,1)S(1)}, bf16[40,6144]{1,0:T(8,128)(2,1)S(1)}, u32[]{:S(2)}, u32[]{:S(2)}) %collective-permute-start.9) | collective-permute-done | bytes 491552 | tf_op jit(solution)/shard_map/basis_plane/ppermute | solution.py:46
  60.1 3.5 %collective-permute-done.10 = bf16[4,40,384]{2,1,0:T(8,128)(2,1)S(1)} collective-permute-done((bf16[4,40,384]{2,1,0:T(8,128)(2,1)S(1)}, bf16[4,40,384]{2,1,0:T(8,128)(2,1)S(1)}, u32[]{:S(2)}, u32[]{:S(2)}) %collective-permute-start.10) | collective-permute-done | bytes 122912 | tf_op jit(solution)/shard_map/projected_back/ppermute | solution.py:46
  65.3 3.4 %collective-permute-start.6 = (bf16[4,40,384]{2,1,0:T(8,128)(2,1)S(1)}, bf16[4,40,384]{2,1,0:T(8,128)(2,1)S(1)}, u32[]{:S(2)}, u32[]{:S(2)}) collective-permute-start(bf16[4,40,384]{2,1,0:T(8,128)(2,1)S(1)} %bitcast.82), channel_id=1, source_target_pairs={{0,24},{1,7},{2,26},{3,1},{4,28},{5,3},{6,30},{7,5},{32,56},{33,39... | collective-permute-start | bytes 368648 | tf_op jit(solution)/shard_map/projected_back/ppermute | solution.py:46
  70.6 5.4 %collective-permute-done.12 = bf16[4,40,384]{2,1,0:T(8,128)(2,1)S(1)} collective-permute-done((bf16[4,40,384]{2,1,0:T(8,128)(2,1)S(1)}, bf16[4,40,384]{2,1,0:T(8,128)(2,1)S(1)}, u32[]{:S(2)}, u32[]{:S(2)}) %collective-permute-start.12) | collective-permute-done | bytes 122912 | tf_op jit(solution)/shard_map/projected_back/ppermute | solution.py:46
  77.8 2.0 %collective-permute-done.13 = bf16[4,40,384]{2,1,0:T(8,128)(2,1)S(1)} collective-permute-done((bf16[4,40,384]{2,1,0:T(8,128)(2,1)S(1)}, bf16[4,40,384]{2,1,0:T(8,128)(2,1)S(1)}, u32[]{:S(2)}, u32[]{:S(2)}) %collective-permute-start.13) | collective-permute-done | bytes 122912 | tf_op jit(solution)/shard_map/projected_aside/ppermute | solution.py:46
  82.8 8.3 %collective-permute-start.16 = (bf16[4,4,40,384]{3,2,1,0:T(8,128)(2,1)S(1)}, bf16[4,4,40,384]{3,2,1,0:T(8,128)(2,1)S(1)}, u32[]{:S(2)}, u32[]{:S(2)}) collective-permute-start(bf16[4,4,40,384]{3,2,1,0:T(8,128)(2,1)S(1)} %pad_maximum_fusion.1.own_ref), channel_id=1, source_target_pairs={{0,1},{1,0},{2,3},{3,2},{4,5},{5,4},{6,7},{7,6},{32,33},{33,32},{3... | collective-permute-start | bytes 1474568 | tf_op jit(solution)/shard_map/projected_aside/ppermute | solution.py:46
  94.2 4.9 %channel.1 = bf16[2,40,640]{2,1,0:T(8,128)(2,1)S(1)} custom-call(s32[3]{0:T(128)S(1)} %pad_add_fusion.place_ref, bf16[4,4,40,384]{3,2,1,0:T(8,128)(2,1)S(1)} %pad_maximum_fusion.1.own_ref, bf16[4,4,40,384]{3,2,1,0:T(8,128)(2,1)S(1)} %collective-permute-done.16.other_ref, bf16[160,6144]{1,0:T(8,128)(2,1)S(1)} %pad_maximum_fusion.u0, ...), custom_call_target="tpu_custom_call" | custom-call | tf_op jit(solution)/shard_map/channel/pallas_call | solution.py:85
  99.7 3.2 %collective-permute-start.18 = (bf16[2,40,640]{2,1,0:T(8,128)(2,1)S(1)}, bf16[2,40,640]{2,1,0:T(8,128)(2,1)S(1)}, u32[]{:S(2)}, u32[]{:S(2)}) collective-permute-start(bf16[2,40,640]{2,1,0:T(8,128)(2,1)S(1)} %channel.1), channel_id=1, source_target_pairs={{0,32},{1,33},{2,34},{3,35},{4,36},{5,37},{6,38},{7,39},{32,0},{33... | collective-permute-start | bytes 307208 | tf_op jit(solution)/shard_map/columns_exchange/ppermute | solution.py:46
  105.2 3.8 %all-to-all-start = ((bf16[8,40,160]{2,1,0:T(8,128)(2,1)}), bf16[8,40,160]{2,1,0:T(8,128)(2,1)S(1)}, u32[]{:S(2)}, u32[]{:S(2)}) async-start(bf16[8,40,160]{2,1,0:T(8,128)(2,1)} %bitcast.66), calls=%async_computation | async-start | bytes 327680 | tf_op jit(solution)/shard_map/columns_exchange/all_to_all | solution.py:180
  109.6 9.0 %all-to-all-done = bf16[8,40,160]{2,1,0:T(8,128)(2,1)S(1)} async-done(((bf16[8,40,160]{2,1,0:T(8,128)(2,1)}), bf16[8,40,160]{2,1,0:T(8,128)(2,1)S(1)}, u32[]{:S(2)}, u32[]{:S(2)}) %all-to-all-start) | async-done | bytes 102432 | tf_op jit(solution)/shard_map/columns_exchange/all_to_all | solution.py:180
  123.8 3.5 %all-to-all-start.1 = ((bf16[4,2,2,40,640]{4,3,2,1,0:T(8,128)(2,1)}), bf16[4,2,2,40,640]{4,3,2,1,0:T(8,128)(2,1)S(1)}, u32[]{:S(2)}, u32[]{:S(2)}) async-start(bf16[4,2,2,40,640]{4,3,2,1,0:T(8,128)(2,1)} %broadcast_in_dim.32), calls=%async_computation.1 | async-start | bytes 1638400 | tf_op jit(solution)/shard_map/points/all_to_all | solution.py:193
  130.2 4.8 %collective-permute-done.22.m1 = bf16[160,1280]{1,0:T(8,128)(2,1)S(1)} collective-permute-done((bf16[160,1280]{1,0:T(8,128)(2,1)S(1)}, bf16[160,1280]{1,0:T(8,128)(2,1)S(1)}, u32[]{:S(2)}, u32[]{:S(2)}) %collective-permute-start.22) | collective-permute-done | bytes 409632 | tf_op jit(solution)/shard_map/mixed_plane/ppermute | solution.py:46
  135.0 12.9 %collective-permute-done.23.m2 = bf16[160,1280]{1,0:T(8,128)(2,1)S(1)} collective-permute-done((bf16[160,1280]{1,0:T(8,128)(2,1)S(1)}, bf16[160,1280]{1,0:T(8,128)(2,1)S(1)}, u32[]{:S(2)}, u32[]{:S(2)}) %collective-permute-start.23) | collective-permute-done | bytes 409632 | tf_op jit(solution)/shard_map/mixed_plane/ppermute | solution.py:46
  (91 shorter events, 36.0 us)
Async XLA Ops:
  0.0 20.4 %collective-permute-start.3 = (bf16[192,6144]{1,0:T(8,128)(2,1)}, bf16[192,6144]{1,0:T(8,128)(2,1)}, u32[]{:S(2)}, u32[]{:S(2)}) collective-permute-start(bf16[192,6144]{1,0:T(8,128)(2,1)} %bitcast.72), channel_id=1, source_target_pairs={{0,1},{1,0},{2,3},{3,2},{4,5},{5,4},{6,7},{7,6},{32,33},{33,32},{3... | collective-permute-start | bytes 7077896 | tf_op jit(solution)/shard_map/rows_pair/ppermute | solution.py:46
  3.2 8.2 %collective-permute-start = (bf16[40,6144]{1,0:T(8,128)(2,1)}, bf16[40,6144]{1,0:T(8,128)(2,1)S(1)}, u32[]{:S(2)}, u32[]{:S(2)}) collective-permute-start(bf16[40,6144]{1,0:T(8,128)(2,1)} %bitcast.74), channel_id=1, source_target_pairs={{0,38},{1,25},{2,0},{3,27},{4,2},{5,29},{6,4},{7,31},{32,6},{33,57... | collective-permute-start | bytes 1474568 | tf_op jit(solution)/shard_map/basis_line/ppermute | solution.py:46
  4.2 9.7 %collective-permute-start.1 = (bf16[40,6144]{1,0:T(8,128)(2,1)}, bf16[40,6144]{1,0:T(8,128)(2,1)S(1)}, u32[]{:S(2)}, u32[]{:S(2)}) collective-permute-start(bf16[40,6144]{1,0:T(8,128)(2,1)} %bitcast.75), channel_id=1, source_target_pairs={{0,4},{1,17},{2,38},{3,19},{4,32},{5,21},{6,2},{7,23},{32,36},{33,... | collective-permute-start | bytes 1474568 | tf_op jit(solution)/shard_map/basis_line/ppermute | solution.py:46
  4.6 14.6 %collective-permute-start.2 = (bf16[40,6144]{1,0:T(8,128)(2,1)}, bf16[40,6144]{1,0:T(8,128)(2,1)S(1)}, u32[]{:S(2)}, u32[]{:S(2)}) collective-permute-start(bf16[40,6144]{1,0:T(8,128)(2,1)} %bitcast.76), channel_id=1, source_target_pairs={{0,2},{1,9},{2,4},{3,11},{4,6},{5,13},{6,32},{7,15},{32,34},{33,41... | collective-permute-start | bytes 1474568 | tf_op jit(solution)/shard_map/basis_line/ppermute | solution.py:46
  20.5 12.3 %collective-permute-start.4 = (bf16[40,6144]{1,0:T(8,128)(2,1)S(1)}, bf16[40,6144]{1,0:T(8,128)(2,1)S(1)}, u32[]{:S(2)}, u32[]{:S(2)}) collective-permute-start(bf16[40,6144]{1,0:T(8,128)(2,1)S(1)} %dynamic-slice_bitcast_fusion), channel_id=1, source_target_pairs={{0,16},{1,5},{2,18},{3,39},{4,20},{5,33},{6,22},{7,3},{32,48},{33,... | collective-permute-start | bytes 1474568 | tf_op jit(solution)/shard_map/basis_plane/ppermute | solution.py:46
  32.8 11.9 %collective-permute-start.7 = (bf16[40,6144]{1,0:T(8,128)(2,1)S(1)}, bf16[40,6144]{1,0:T(8,128)(2,1)S(1)}, u32[]{:S(2)}, u32[]{:S(2)}) collective-permute-start(bf16[40,6144]{1,0:T(8,128)(2,1)S(1)} %collective-permute-done.4), channel_id=1, source_target_pairs={{0,192},{1,193},{2,194},{3,195},{4,196},{5,197},{6,198},{7,199},{3... | collective-permute-start | bytes 1474568 | tf_op jit(solution)/shard_map/basis_plane/ppermute | solution.py:46
  35.3 12.7 %collective-permute-start.8 = (bf16[40,6144]{1,0:T(8,128)(2,1)S(1)}, bf16[40,6144]{1,0:T(8,128)(2,1)S(1)}, u32[]{:S(2)}, u32[]{:S(2)}) collective-permute-start(bf16[40,6144]{1,0:T(8,128)(2,1)S(1)} %collective-permute-done.4), channel_id=1, source_target_pairs={{0,64},{1,65},{2,66},{3,67},{4,68},{5,69},{6,70},{7,71},{32,96},{3... | collective-permute-start | bytes 1474568 | tf_op jit(solution)/shard_map/basis_plane/ppermute | solution.py:46
  35.3 21.4 %collective-permute-start.9 = (bf16[40,6144]{1,0:T(8,128)(2,1)S(1)}, bf16[40,6144]{1,0:T(8,128)(2,1)S(1)}, u32[]{:S(2)}, u32[]{:S(2)}) collective-permute-start(bf16[40,6144]{1,0:T(8,128)(2,1)S(1)} %collective-permute-done.4), channel_id=1, source_target_pairs={{0,128},{1,129},{2,130},{3,131},{4,132},{5,133},{6,134},{7,135},{3... | collective-permute-start | bytes 1474568 | tf_op jit(solution)/shard_map/basis_plane/ppermute | solution.py:46
  37.0 26.6 %collective-permute-start.5 = (bf16[160,6144]{1,0:T(8,128)(2,1)S(1)}, bf16[160,6144]{1,0:T(8,128)(2,1)S(1)}, u32[]{:S(2)}, u32[]{:S(2)}) collective-permute-start(bf16[160,6144]{1,0:T(8,128)(2,1)S(1)} %pad_maximum_fusion.u0), channel_id=1, source_target_pairs={{0,8},{1,3},{2,10},{3,5},{4,12},{5,7},{6,14},{7,33},{32,40},{33,35... | collective-permute-start | bytes 5898248 | tf_op jit(solution)/shard_map/basis_plane/ppermute | solution.py:46
  37.0 31.7 %collective-permute-start.11 = (bf16[160,6144]{1,0:T(8,128)(2,1)S(1)}, bf16[160,6144]{1,0:T(8,128)(2,1)S(1)}, u32[]{:S(2)}, u32[]{:S(2)}) collective-permute-start(bf16[160,6144]{1,0:T(8,128)(2,1)S(1)} %pad_maximum_fusion.u0), channel_id=1, source_target_pairs={{0,24},{1,39},{2,26},{3,1},{4,28},{5,3},{6,30},{7,5},{32,56},{33,7... | collective-permute-start | bytes 5898248 | tf_op jit(solution)/shard_map/basis_plane/ppermute | solution.py:46
  58.4 5.2 %collective-permute-start.10 = (bf16[4,40,384]{2,1,0:T(8,128)(2,1)S(1)}, bf16[4,40,384]{2,1,0:T(8,128)(2,1)S(1)}, u32[]{:S(2)}, u32[]{:S(2)}) collective-permute-start(bf16[4,40,384]{2,1,0:T(8,128)(2,1)S(1)} %bitcast.83), channel_id=1, source_target_pairs={{0,16},{1,5},{2,18},{3,7},{4,20},{5,1},{6,22},{7,3},{32,48},{33,37... | collective-permute-start | bytes 368648 | tf_op jit(solution)/shard_map/projected_back/ppermute | solution.py:46
  65.3 5.3 %collective-permute-start.6 = (bf16[4,40,384]{2,1,0:T(8,128)(2,1)S(1)}, bf16[4,40,384]{2,1,0:T(8,128)(2,1)S(1)}, u32[]{:S(2)}, u32[]{:S(2)}) collective-permute-start(bf16[4,40,384]{2,1,0:T(8,128)(2,1)S(1)} %bitcast.82), channel_id=1, source_target_pairs={{0,24},{1,7},{2,26},{3,1},{4,28},{5,3},{6,30},{7,5},{32,56},{33,39... | collective-permute-start | bytes 368648 | tf_op jit(solution)/shard_map/projected_back/ppermute | solution.py:46
  70.3 5.6 %collective-permute-start.12 = (bf16[4,40,384]{2,1,0:T(8,128)(2,1)S(1)}, bf16[4,40,384]{2,1,0:T(8,128)(2,1)S(1)}, u32[]{:S(2)}, u32[]{:S(2)}) collective-permute-start(bf16[4,40,384]{2,1,0:T(8,128)(2,1)S(1)} %bitcast.81), channel_id=1, source_target_pairs={{0,8},{1,3},{2,10},{3,5},{4,12},{5,7},{6,14},{7,1},{32,40},{33,35}... | collective-permute-start | bytes 368648 | tf_op jit(solution)/shard_map/projected_back/ppermute | solution.py:46
  76.1 5.4 %collective-permute-start.14 = (bf16[4,40,384]{2,1,0:T(8,128)(2,1)S(1)}, bf16[4,40,384]{2,1,0:T(8,128)(2,1)S(1)}, u32[]{:S(2)}, u32[]{:S(2)}) collective-permute-start(bf16[4,40,384]{2,1,0:T(8,128)(2,1)S(1)} %pad_maximum_fusion.4), channel_id=1, source_target_pairs={{0,4},{1,17},{2,6},{3,19},{4,0},{5,21},{6,2},{7,23},{32,36},{33,49... | collective-permute-start | bytes 368648 | tf_op jit(solution)/shard_map/projected_aside/ppermute | solution.py:46
  76.3 6.5 %collective-permute-start.15 = (bf16[4,40,384]{2,1,0:T(8,128)(2,1)S(1)}, bf16[4,40,384]{2,1,0:T(8,128)(2,1)S(1)}, u32[]{:S(2)}, u32[]{:S(2)}) collective-permute-start(bf16[4,40,384]{2,1,0:T(8,128)(2,1)S(1)} %pad_maximum_fusion.5), channel_id=1, source_target_pairs={{0,2},{1,9},{2,4},{3,11},{4,6},{5,13},{6,0},{7,15},{32,34},{33,41}... | collective-permute-start | bytes 368648 | tf_op jit(solution)/shard_map/projected_aside/ppermute | solution.py:46
  82.8 9.8 %collective-permute-start.16 = (bf16[4,4,40,384]{3,2,1,0:T(8,128)(2,1)S(1)}, bf16[4,4,40,384]{3,2,1,0:T(8,128)(2,1)S(1)}, u32[]{:S(2)}, u32[]{:S(2)}) collective-permute-start(bf16[4,4,40,384]{3,2,1,0:T(8,128)(2,1)S(1)} %pad_maximum_fusion.1.own_ref), channel_id=1, source_target_pairs={{0,1},{1,0},{2,3},{3,2},{4,5},{5,4},{6,7},{7,6},{32,33},{33,32},{3... | collective-permute-start | bytes 1474568 | tf_op jit(solution)/shard_map/projected_aside/ppermute | solution.py:46
  99.7 9.9 %collective-permute-start.18 = (bf16[2,40,640]{2,1,0:T(8,128)(2,1)S(1)}, bf16[2,40,640]{2,1,0:T(8,128)(2,1)S(1)}, u32[]{:S(2)}, u32[]{:S(2)}) collective-permute-start(bf16[2,40,640]{2,1,0:T(8,128)(2,1)S(1)} %channel.1), channel_id=1, source_target_pairs={{0,32},{1,33},{2,34},{3,35},{4,36},{5,37},{6,38},{7,39},{32,0},{33... | collective-permute-start | bytes 307208 | tf_op jit(solution)/shard_map/columns_exchange/ppermute | solution.py:46
  105.2 13.4 %all-to-all-start = ((bf16[8,40,160]{2,1,0:T(8,128)(2,1)}), bf16[8,40,160]{2,1,0:T(8,128)(2,1)S(1)}, u32[]{:S(2)}, u32[]{:S(2)}) async-start(bf16[8,40,160]{2,1,0:T(8,128)(2,1)} %bitcast.66), calls=%async_computation | async-start | bytes 327680 | tf_op jit(solution)/shard_map/columns_exchange/all_to_all | solution.py:180
  119.4 8.0 %collective-permute-start.20 = (bf16[40,1280]{1,0:T(8,128)(2,1)S(1)}, bf16[40,1280]{1,0:T(8,128)(2,1)S(1)}, u32[]{:S(2)}, u32[]{:S(2)}) collective-permute-start(bf16[40,1280]{1,0:T(8,128)(2,1)S(1)} %reshape.146), channel_id=1, source_target_pairs={{0,4},{1,17},{2,6},{3,19},{4,0},{5,21},{6,2},{7,23},{32,36},{33,49... | collective-permute-start | bytes 307208 | tf_op jit(solution)/shard_map/mixed_line/ppermute | solution.py:46
  120.2 7.1 %collective-permute-start.21 = (bf16[40,1280]{1,0:T(8,128)(2,1)S(1)}, bf16[40,1280]{1,0:T(8,128)(2,1)S(1)}, u32[]{:S(2)}, u32[]{:S(2)}) collective-permute-start(bf16[40,1280]{1,0:T(8,128)(2,1)S(1)} %reshape.146), channel_id=1, source_target_pairs={{0,2},{1,9},{2,4},{3,11},{4,6},{5,13},{6,0},{7,15},{32,34},{33,41}... | collective-permute-start | bytes 307208 | tf_op jit(solution)/shard_map/mixed_line/ppermute | solution.py:46
  123.8 24.0 %all-to-all-start.1 = ((bf16[4,2,2,40,640]{4,3,2,1,0:T(8,128)(2,1)}), bf16[4,2,2,40,640]{4,3,2,1,0:T(8,128)(2,1)S(1)}, u32[]{:S(2)}, u32[]{:S(2)}) async-start(bf16[4,2,2,40,640]{4,3,2,1,0:T(8,128)(2,1)} %broadcast_in_dim.32), calls=%async_computation.1 | async-start | bytes 1638400 | tf_op jit(solution)/shard_map/points/all_to_all | solution.py:193
  127.4 7.5 %collective-permute-start.22 = (bf16[160,1280]{1,0:T(8,128)(2,1)S(1)}, bf16[160,1280]{1,0:T(8,128)(2,1)S(1)}, u32[]{:S(2)}, u32[]{:S(2)}) collective-permute-start(bf16[160,1280]{1,0:T(8,128)(2,1)S(1)} %constant_dynamic-update-slice_fusion.m0), channel_id=1, source_target_pairs={{0,24},{1,7},{2,26},{3,1},{4,28},{5,3},{6,30},{7,5},{32,56},{33,39... | collective-permute-start | bytes 1228808 | tf_op jit(solution)/shard_map/mixed_plane/ppermute | solution.py:46
  129.2 18.6 %collective-permute-start.23 = (bf16[160,1280]{1,0:T(8,128)(2,1)S(1)}, bf16[160,1280]{1,0:T(8,128)(2,1)S(1)}, u32[]{:S(2)}, u32[]{:S(2)}) collective-permute-start(bf16[160,1280]{1,0:T(8,128)(2,1)S(1)} %constant_dynamic-update-slice_fusion.m0), channel_id=1, source_target_pairs={{0,16},{1,5},{2,18},{3,7},{4,20},{5,1},{6,22},{7,3},{32,48},{33,37... | collective-permute-start | bytes 1228808 | tf_op jit(solution)/shard_map/mixed_plane/ppermute | solution.py:46
  129.2 18.6 %collective-permute-start.24 = (bf16[160,1280]{1,0:T(8,128)(2,1)S(1)}, bf16[160,1280]{1,0:T(8,128)(2,1)S(1)}, u32[]{:S(2)}, u32[]{:S(2)}) collective-permute-start(bf16[160,1280]{1,0:T(8,128)(2,1)S(1)} %constant_dynamic-update-slice_fusion.m0), channel_id=1, source_target_pairs={{0,8},{1,3},{2,10},{3,5},{4,12},{5,7},{6,14},{7,1},{32,40},{33,35}... | collective-permute-start | bytes 1228808 | tf_op jit(solution)/shard_map/mixed_plane/ppermute | solution.py:46
  (11 other events, 191.3 us)

commit v6 on v5

v6 whole, which is shorter than its diff:
```python
import jax
import jax.numpy as jnp
from jax import lax
from jax.experimental import pallas as pl
from jax.experimental.pallas import tpu as pltpu
from jax.sharding import PartitionSpec as P

BF = jnp.bfloat16
F32 = jnp.float32
AXES = ("pt", "pan")


def place(x, y, z, c):
    return ((x % 4) * 2 + (z % 8) // 4) * 32 + (y % 4) * 8 + (z % 4) * 2 + c


def pairs(move):
    return [
        (place(x, y, z, c), place(*move(x, y, z, c)))
        for x in range(4) for y in range(4) for z in range(8) for c in range(2)
    ]


def along(first, ring):
    def z_move(z, step):
        return z + step if ring else z // 4 * 4 + (z + step) % 4

    def perm(step):
        return pairs(
            lambda x, y, z, c: (x, y, z_move(z, step(z)), c) if (c == 0) == first else (x, y + step(y), z, c)
        )

    return perm


UP = lambda v: 1
DOWN = lambda v: -1
TWO = lambda v: 2 if v % 2 == 0 else -2
CROSS = lambda step: pairs(lambda x, y, z, c: (x + step(x), y, z, c))
CORE = pairs(lambda x, y, z, c: (x, y, z, 1 - c))
HALF = pairs(lambda x, y, z, c: (x, y, z + 4, c))


def send(value, perm):
    return lax.ppermute(value, AXES, perm)


def gather_line(value, axis):
    up = send(value, axis(UP))
    down = send(value, axis(DOWN))
    two = send(value, axis(TWO))
    return value, down, two, up


def nt(a, b):
    return lax.dot_general(a, b, (((1,), (1,)), ((), ())), preferred_element_type=F32)


INTERPRET = False


def channel_kernel(
    place_ref, own_ref, other_ref, u0, u1, u2, u3, out_ref, mine_ref, theirs_ref, left, by_chip, held, sems
):
    y, z, core = place_ref[0], place_ref[1], place_ref[2]
    _, _, width, depth = own_ref.shape
    pad = -(-width // 16) * 16
    copies = [pltpu.make_async_copy(u, held.at[a], sems.at[a]) for a, u in enumerate((u0, u1, u2, u3))]
    for copy in copies:
        copy.start()
    for first in range(4):
        for second in range(4):
            straight = (y + second) % 4 * 4 + (z + first) % 4
            across = (y + first) % 4 * 4 + (z + second) % 4
            mine = pl.multiple_of(jnp.where(core == 0, straight, across) * depth, depth)
            theirs = pl.multiple_of(jnp.where(core == 0, across, straight) * depth, depth)
            left[:width, pl.ds(mine, depth)] = own_ref[first, second]
            left[pad : pad + width, pl.ds(theirs, depth)] = other_ref[first, second]
    columns = []
    for a, copy in enumerate(copies):
        copy.wait()
        column = nt(held[a], left[...])
        columns.append(column)
        for b in range(4):
            straight = (y + a) % 4 * 4 + (z + b) % 4
            across = (y + b) % 4 * 4 + (z + a) % 4
            by_chip[jnp.where(core == 0, straight, across)] = column[b * width : (b + 1) * width]
    block = jnp.concatenate(columns, 0).T
    out_ref[...] = jnp.concatenate([block[:width], block[pad : pad + width]], 0).astype(BF)
    for point in range(8):
        block = jnp.concatenate([by_chip[2 * point], by_chip[2 * point + 1]], 0).T.astype(BF)
        mine_ref[point] = block[:width]
        theirs_ref[point] = block[pad : pad + width]


def channel_blocks(place_index, own, other, units):
    _, _, width, depth = own.shape
    pad = -(-width // 16) * 16
    vmem = pl.BlockSpec(memory_space=pltpu.VMEM)
    part = jax.ShapeDtypeStruct((8, width, 2 * width), BF)
    return pl.pallas_call(
        channel_kernel,
        out_shape=[jax.ShapeDtypeStruct((2 * width, 16 * width), BF), part, part],
        in_specs=[pl.BlockSpec(memory_space=pltpu.SMEM)] + [vmem] * 2 + [pl.BlockSpec(memory_space=pl.ANY)] * 4,
        out_specs=[vmem] * 3,
        scratch_shapes=[
            pltpu.VMEM((2 * pad, 16 * depth), BF),
            pltpu.VMEM((16, width, 2 * pad), F32),
            pltpu.VMEM((4,) + units[0].shape, BF),
            pltpu.SemaphoreType.DMA((4,)),
        ],
        compiler_params=pltpu.CompilerParams(vmem_limit_bytes=24 * 1024 * 1024),
        interpret=INTERPRET,
    )(place_index, own, other, *units)


def product_kernel(place_ref, l0, l1, l2, l3, m0, m1, m2, m3, linear_ref, mine_ref, theirs_ref, right):
    width, span = linear_ref.shape
    part, lanes = m0.shape
    for a, m in enumerate((m0, m1, m2, m3)):
        right[a * part : (a + 1) * part] = m[...]
    total = jnp.zeros((2 * width, span), F32)
    for r in range(8):
        low = span * r // 128 * 128
        high = min(-(-(span * r + span) // 128) * 128, lanes)
        at = span * r - low
        left = (l0, l1, l2, l3)[r // 2]
        term = jnp.dot(left[r % 2], right[:, low:high], preferred_element_type=F32)
        total = total + term[:, at : at + span]

    def in_order(value):
        piece = [value[:, k * span // 4 : (k + 1) * span // 4] for k in range(4)]
        even = jnp.concatenate([piece[0], piece[2], piece[1], piece[3]], 1)
        odd = jnp.concatenate([piece[2], piece[0], piece[3], piece[1]], 1)
        return jnp.where(place_ref[2] == 0, even, odd)

    mine_ref[...] = in_order(total[:width] + linear_ref[...])
    theirs_ref[...] = in_order(total[width:])


def product(place_index, left, planes, linear):
    vmem = pl.BlockSpec(memory_space=pltpu.VMEM)
    return pl.pallas_call(
        product_kernel,
        out_shape=[jax.ShapeDtypeStruct(linear.shape, F32)] * 2,
        in_specs=[pl.BlockSpec(memory_space=pltpu.SMEM)] + [vmem] * 9,
        out_specs=[vmem] * 2,
        scratch_shapes=[pltpu.VMEM((4 * planes[0].shape[0], planes[0].shape[1]), BF)],
        compiler_params=pltpu.CompilerParams(vmem_limit_bytes=12 * 1024 * 1024),
        interpret=INTERPRET,
    )(place_index, *left, *planes, linear)


def shards(potential, basis, weights, coupling):
    point = lax.axis_index("pt")
    pan = lax.axis_index("pan")
    core = pan % 2
    chip = pan // 2
    x, y, z = point // 2, chip // 4, chip % 4
    rows = potential[0]
    panel = basis.T
    width, depth = panel.shape

    with jax.named_scope("basis_line"):
        line = jnp.concatenate(gather_line(panel, along(True, True)), 0)
    with jax.named_scope("rows_pair"):
        line, other_rows = lax.optimization_barrier((line, send(rows, CORE)))
        chip_rows = jnp.where(
            core == 0, jnp.concatenate([rows, other_rows], 0), jnp.concatenate([other_rows, rows], 0)
        )
        chip_rows = lax.optimization_barrier(chip_rows)
    with jax.named_scope("basis_plane"):
        plane = along(False, True)
        fetched = lax.dynamic_index_in_dim(line.reshape(4, width, depth), x, 0, keepdims=False)
        fetched, line = lax.optimization_barrier((send(fetched, plane(TWO)), line))
        two = jnp.zeros((4, width, depth), BF)
        for step, perm in ((0, None), (1, CROSS(DOWN)), (3, CROSS(UP)), (2, CROSS(TWO))):
            piece = fetched if perm is None else send(fetched, perm)
            two = lax.dynamic_update_index_in_dim(two, piece, (x + step) % 4, 0)
        units = line, send(line, plane(DOWN)), two.reshape(4 * width, depth), send(line, plane(UP))
    with jax.named_scope("projected"):
        back, aside = along(False, False), along(True, False)
        project = lambda unit: nt(unit, chip_rows).astype(BF).reshape(4, width, -1)
        parts = [project(units[0]), project(units[1]), None, project(units[3])]
        two, parts[1], parts[3] = lax.optimization_barrier((units[2], parts[1], parts[3]))
        parts[2] = project(two)
    with jax.named_scope("projected_back"):
        parts = parts[0], send(parts[3], back(DOWN)), send(parts[2], back(TWO)), send(parts[1], back(UP))
    with jax.named_scope("projected_aside"):
        parts = [jnp.stack([part[b] for part in parts]) for b in range(4)]
        own = jnp.stack(
            [parts[0], send(parts[3], aside(DOWN)), send(parts[2], aside(TWO)), send(parts[1], aside(UP))]
        )
        other = send(own, CORE)
    with jax.named_scope("channel"):
        place_index = jnp.stack([y, z, core])
        channel, mine, theirs = channel_blocks(place_index, own, other, units)
    with jax.named_scope("columns_exchange"):
        mine = jnp.stack([mine, send(theirs, CORE)], 1)
        left = [jnp.stack([channel, send(channel, HALF)])]
        chosen = lax.all_to_all(mine, "pt", 0, 0, tiled=True).astype(F32)
        antisym = coupling - coupling.T
        offset = jnp.arange(8)
        order = (x + offset // 2) % 4 * 2 + (offset + point) % 2
        turned = jnp.take(antisym, order, axis=1)
        mixed = jnp.einsum("qr,qein->iren", turned, chosen, precision=lax.Precision.HIGHEST)
        mixed = mixed.astype(BF).reshape(width, -1)
        linear = jnp.einsum("q,qein->ien", weights, chosen, precision=lax.Precision.HIGHEST)
        linear = linear.reshape(width, -1)
    with jax.named_scope("points"):
        left = gather_line(left[0], CROSS)
    with jax.named_scope("mixed_line"):
        line = jnp.concatenate(gather_line(mixed, along(True, False)), 0)
    with jax.named_scope("mixed_plane"):
        planes = gather_line(line, along(False, False))
    with jax.named_scope("product"):
        total, rest = product(place_index, left, planes, linear)
    with jax.named_scope("output"):
        return total + send(rest, CORE)


def solution(mesh):
    in_specs = (P("pt", "pan", None), P(None, "pan"), P(), P())
    return jax.shard_map(shards, mesh=mesh, in_specs=in_specs, out_specs=P("pan", "pt"), check_vma=False)
```

time: 151 us -> 157 us (1.040)
  starting transfers between devices: 45.9 us -> 51.4 us
  waiting for transfers between devices: 79.6 us -> 76.7 us
  local copies, waits for them, and re-layouts: 4.21 us -> 6.91 us
  Pallas kernels: 5.65 us -> 7.95 us
    ppermute x26 -> x29, starting transfers between devices: 38.7 us -> 46.6 us  [send(): return lax.ppermute(value, AXES, perm)]
    unnamed x18 -> x22, local copies, waits for them, and re-layouts: 1.67 us -> 4.75 us
    all_to_all x2 -> x1, starting transfers between devices: 7.26 us -> 4.76 us  [shards(): chosen = lax.all_to_all(mine, 'pt', 0, 0, tiled=True).astype(F32)]
    pallas_call x2, Pallas kernels: 5.65 us -> 7.95 us  [the longest x1 6.61 us: channel_blocks(): pl.pallas_call(channel_kernel, out_shape=[jax.ShapeDtypeStruct((2 * width...]
    all_to_all x2 -> x1, waiting for transfers between devices: 8.97 us -> 6.77 us  [shards(): chosen = lax.all_to_all(mine, 'pt', 0, 0, tiled=True).astype(F32)]
    ppermute x26 -> x29, waiting for transfers between devices: 70.6 us -> 69.9 us  [send(): return lax.ppermute(value, AXES, perm)]
  transfers between devices with their start and end apart: 28 -> 30, of which waited for: 20 -> 23; matrix products, arithmetic and copies ran while one was open for 11% -> 8% of each run, Pallas kernels for 0% -> 0%
where the time goes in v6:
time: 157 us
  waiting for transfers between devices  76.7 us (49%)
  starting transfers between devices  51.4 us (33%)
  Pallas kernels  7.95 us (5%)
  matrix products  7.26 us (5%)
  local copies, waits for them, and re-layouts  6.91 us (4%)
  other arithmetic  6.14 us (4%)
    ppermute x29, waiting for transfers between devices, send(): return lax.ppermute(value, AXES, perm)  69.9 us
    ppermute x29, starting transfers between devices, send(): return lax.ppermute(value, AXES, perm)  46.6 us
    all_to_all x1, waiting for transfers between devices, shards(): chosen = lax.all_to_all(mine, 'pt', 0, 0, tiled=True).astype(F32)  6.77 us
    dot_general x4, matrix products, nt(): lax.dot_general(a, b, (((1,), (1,)), ((), ())), preferred_element_type=F32)  6.63 us
    pallas_call x1, Pallas kernels, channel_blocks(): pl.pallas_call(channel_kernel, out_shape=[jax.ShapeDtypeStruct((2 * width...  6.61 us
    all_to_all x1, starting transfers between devices, shards(): chosen = lax.all_to_all(mine, 'pt', 0, 0, tiled=True).astype(F32)  4.76 us
    unnamed x22, local copies, waits for them, and re-layouts  4.75 us
    select_n x1, other arithmetic, shards(): jnp.where(core == 0, jnp.concatenate([rows, other_rows], 0), jnp.concaten...  3.96 us
  transfers between devices with their start and end apart: 30, of which 23 were waited for; matrix products, arithmetic and copies ran while one was open for 8% of the time, Pallas kernels for 0%

profile of v6, /device:TPU:1, one launch (start us, length us, event | category | flops | bytes accessed | tf_op | source)
XLA Modules:
  0.0 156.7 jit_solution(15795009769106722959)
XLA Ops:
  0.0 3.2 %collective-permute-start.3 = (bf16[192,6144]{1,0:T(8,128)(2,1)}, bf16[192,6144]{1,0:T(8,128)(2,1)}, u32[]{:S(2)}, u32[]{:S(2)}) collective-permute-start(bf16[192,6144]{1,0:T(8,128)(2,1)} %bitcast.71), channel_id=1, source_target_pairs={{0,1},{1,0},{2,3},{3,2},{4,5},{5,4},{6,7},{7,6},{32,33},{33,32},{3... | collective-permute-start | bytes 7077896 | tf_op jit(solution)/shard_map/rows_pair/ppermute | solution.py:45
  3.2 2.2 %collective-permute-start.1 = (bf16[40,6144]{1,0:T(8,128)(2,1)}, bf16[40,6144]{1,0:T(8,128)(2,1)S(1)}, u32[]{:S(2)}, u32[]{:S(2)}) collective-permute-start(bf16[40,6144]{1,0:T(8,128)(2,1)} %bitcast.74), channel_id=1, source_target_pairs={{0,4},{1,17},{2,38},{3,19},{4,32},{5,21},{6,2},{7,23},{32,36},{33,... | collective-permute-start | bytes 1474568 | tf_op jit(solution)/shard_map/basis_line/ppermute | solution.py:45
  6.5 11.4 %collective-permute-done.2 = bf16[40,6144]{1,0:T(8,128)(2,1)S(1)} collective-permute-done((bf16[40,6144]{1,0:T(8,128)(2,1)}, bf16[40,6144]{1,0:T(8,128)(2,1)S(1)}, u32[]{:S(2)}, u32[]{:S(2)}) %collective-permute-start.2) | collective-permute-done | bytes 491552 | tf_op jit(solution)/shard_map/basis_line/ppermute | solution.py:45
  21.5 4.0 %maximum_select_fusion = bf16[384,6144]{1,0:T(8,128)(2,1)S(1)} fusion(bf16[192,6144]{1,0:T(8,128)(2,1)} %collective-permute-done.3, bf16[192,6144]{1,0:T(8,128)(2,1)S(1)} %bitcast.72, pred[]{:T(512)S(6)} %eq.13), kind=kLoop, calls=%fused_computation.1 | loop fusion | flops 21233664 | bytes 9437185 | tf_op jit(solution)/shard_map/rows_pair/jit(_where)/select_n | solution.py:168
  25.4 5.6 %collective-permute-done.4 = bf16[40,6144]{1,0:T(8,128)(2,1)S(1)} collective-permute-done((bf16[40,6144]{1,0:T(8,128)(2,1)S(1)}, bf16[40,6144]{1,0:T(8,128)(2,1)S(1)}, u32[]{:S(2)}, u32[]{:S(2)}) %collective-permute-start.4) | collective-permute-done | bytes 491552 | tf_op jit(solution)/shard_map/basis_plane/ppermute | solution.py:45
  31.0 2.5 %collective-permute-start.5 = (bf16[40,6144]{1,0:T(8,128)(2,1)S(1)}, bf16[40,6144]{1,0:T(8,128)(2,1)S(1)}, u32[]{:S(2)}, u32[]{:S(2)}) collective-permute-start(bf16[40,6144]{1,0:T(8,128)(2,1)S(1)} %collective-permute-done.4), channel_id=1, source_target_pairs={{0,192},{1,193},{2,194},{3,195},{4,196},{5,197},{6,198},{7,199},{3... | collective-permute-start | bytes 1474568 | tf_op jit(solution)/shard_map/basis_plane/ppermute | solution.py:45
  35.2 3.1 %collective-permute-start.8 = (bf16[160,6144]{1,0:T(8,128)(2,1)S(1)}, bf16[160,6144]{1,0:T(8,128)(2,1)S(1)}, u32[]{:S(2)}, u32[]{:S(2)}) collective-permute-start(bf16[160,6144]{1,0:T(8,128)(2,1)S(1)} %pad_maximum_fusion.u0), channel_id=1, source_target_pairs={{0,24},{1,39},{2,26},{3,1},{4,28},{5,3},{6,30},{7,5},{32,56},{33,7... | collective-permute-start | bytes 5898248 | tf_op jit(solution)/shard_map/basis_plane/ppermute | solution.py:45
  40.3 2.4 %collective-permute-done.5 = bf16[40,6144]{1,0:T(8,128)(2,1)S(1)} collective-permute-done((bf16[40,6144]{1,0:T(8,128)(2,1)S(1)}, bf16[40,6144]{1,0:T(8,128)(2,1)S(1)}, u32[]{:S(2)}, u32[]{:S(2)}) %collective-permute-start.5) | collective-permute-done | bytes 491552 | tf_op jit(solution)/shard_map/basis_plane/ppermute | solution.py:45
  42.8 3.2 %collective-permute-done.6 = bf16[40,6144]{1,0:T(8,128)(2,1)S(1)} collective-permute-done((bf16[40,6144]{1,0:T(8,128)(2,1)S(1)}, bf16[40,6144]{1,0:T(8,128)(2,1)S(1)}, u32[]{:S(2)}, u32[]{:S(2)}) %collective-permute-start.6) | collective-permute-done | bytes 491552 | tf_op jit(solution)/shard_map/basis_plane/ppermute | solution.py:45
  46.1 8.7 %collective-permute-done.7 = bf16[40,6144]{1,0:T(8,128)(2,1)S(1)} collective-permute-done((bf16[40,6144]{1,0:T(8,128)(2,1)S(1)}, bf16[40,6144]{1,0:T(8,128)(2,1)S(1)}, u32[]{:S(2)}, u32[]{:S(2)}) %collective-permute-start.7) | collective-permute-done | bytes 491552 | tf_op jit(solution)/shard_map/basis_plane/ppermute | solution.py:45
  54.8 5.1 %collective-permute-done.8.u1 = bf16[160,6144]{1,0:T(8,128)(2,1)S(1)} collective-permute-done((bf16[160,6144]{1,0:T(8,128)(2,1)S(1)}, bf16[160,6144]{1,0:T(8,128)(2,1)S(1)}, u32[]{:S(2)}, u32[]{:S(2)}) %collective-permute-start.8) | collective-permute-done | bytes 1966112 | tf_op jit(solution)/shard_map/basis_plane/ppermute | solution.py:45
  67.7 2.5 %collective-permute-start.10 = (bf16[4,40,384]{2,1,0:T(8,128)(2,1)S(1)}, bf16[4,40,384]{2,1,0:T(8,128)(2,1)S(1)}, u32[]{:S(2)}, u32[]{:S(2)}) collective-permute-start(bf16[4,40,384]{2,1,0:T(8,128)(2,1)S(1)} %bitcast.81), channel_id=1, source_target_pairs={{0,24},{1,7},{2,26},{3,1},{4,28},{5,3},{6,30},{7,5},{32,56},{33,39... | collective-permute-start | bytes 368648 | tf_op jit(solution)/shard_map/projected_back/ppermute | solution.py:45
  70.6 2.9 %collective-permute-done.11 = bf16[4,40,384]{2,1,0:T(8,128)(2,1)S(1)} collective-permute-done((bf16[4,40,384]{2,1,0:T(8,128)(2,1)S(1)}, bf16[4,40,384]{2,1,0:T(8,128)(2,1)S(1)}, u32[]{:S(2)}, u32[]{:S(2)}) %collective-permute-start.11) | collective-permute-done | bytes 122912 | tf_op jit(solution)/shard_map/projected_back/ppermute | solution.py:45
  74.2 2.8 %collective-permute-start.14 = (bf16[4,40,384]{2,1,0:T(8,128)(2,1)S(1)}, bf16[4,40,384]{2,1,0:T(8,128)(2,1)S(1)}, u32[]{:S(2)}, u32[]{:S(2)}) collective-permute-start(bf16[4,40,384]{2,1,0:T(8,128)(2,1)S(1)} %pad_maximum_fusion.5), channel_id=1, source_target_pairs={{0,4},{1,17},{2,6},{3,19},{4,0},{5,21},{6,2},{7,23},{32,36},{33,49... | collective-permute-start | bytes 368648 | tf_op jit(solution)/shard_map/projected_aside/ppermute | solution.py:45
  80.9 9.0 %collective-permute-start.16 = (bf16[4,4,40,384]{3,2,1,0:T(8,128)(2,1)S(1)}, bf16[4,4,40,384]{3,2,1,0:T(8,128)(2,1)S(1)}, u32[]{:S(2)}, u32[]{:S(2)}) collective-permute-start(bf16[4,4,40,384]{3,2,1,0:T(8,128)(2,1)S(1)} %pad_maximum_fusion.1.own_ref), channel_id=1, source_target_pairs={{0,1},{1,0},{2,3},{3,2},{4,5},{5,4},{6,7},{7,6},{32,33},{33,32},{3... | collective-permute-start | bytes 1474568 | tf_op jit(solution)/shard_map/projected_aside/ppermute | solution.py:45
  96.1 6.6 %channel.1 = (bf16[80,640]{1,0:T(8,128)(2,1)S(1)}, bf16[8,40,80]{2,1,0:T(8,128)(2,1)S(1)}, bf16[8,40,80]{2,1,0:T(8,128)(2,1)S(1)}) custom-call(s32[3]{0:T(128)S(1)} %pad_add_fusion.place_ref, bf16[4,4,40,384]{3,2,1,0:T(8,128)(2,1)S(1)} %pad_maximum_fusion.1.own_ref, bf16[4,4,40,384]{3,2,1,0:T(8,128)(2,1)S(1)} %collective-permute-done.16.other_ref, ...), custom_call_target="tpu_custom_call" | custom-call | tf_op jit(solution)/shard_map/channel/pallas_call | solution.py:101
  103.7 3.2 %collective-permute-start.17 = (bf16[80,640]{1,0:T(8,128)(2,1)S(1)}, bf16[80,640]{1,0:T(8,128)(2,1)S(1)}, u32[]{:S(2)}, u32[]{:S(2)}) collective-permute-start(bf16[80,640]{1,0:T(8,128)(2,1)S(1)} %get-tuple-element.24), channel_id=1, source_target_pairs={{0,32},{1,33},{2,34},{3,35},{4,36},{5,37},{6,38},{7,39},{32,0},{33... | collective-permute-start | bytes 307208 | tf_op jit(solution)/shard_map/columns_exchange/ppermute | solution.py:45
  107.7 4.8 %all-to-all-start = ((bf16[8,2,40,80]{3,2,1,0:T(8,128)(2,1)}), bf16[8,2,40,80]{3,2,1,0:T(8,128)(2,1)S(1)}, u32[]{:S(2)}, u32[]{:S(2)}) async-start(bf16[8,2,40,80]{3,2,1,0:T(8,128)(2,1)} %copy.8), calls=%async_computation | async-start | bytes 327680 | tf_op jit(solution)/shard_map/columns_exchange/all_to_all | solution.py:201
  112.5 2.8 %collective-permute-start.18 = (bf16[2,80,640]{2,1,0:T(8,128)(2,1)S(1)}, bf16[2,80,640]{2,1,0:T(8,128)(2,1)S(1)}, u32[]{:S(2)}, u32[]{:S(2)}) collective-permute-start(bf16[2,80,640]{2,1,0:T(8,128)(2,1)S(1)} %pad_maximum_fusion.2.l0), channel_id=1, source_target_pairs={{0,192},{1,193},{2,194},{3,195},{4,196},{5,197},{6,198},{7,199},{3... | collective-permute-start | bytes 614408 | tf_op jit(solution)/shard_map/points/ppermute | solution.py:45
  115.3 6.8 %all-to-all-done = bf16[8,2,40,80]{3,2,1,0:T(8,128)(2,1)S(1)} async-done(((bf16[8,2,40,80]{3,2,1,0:T(8,128)(2,1)}), bf16[8,2,40,80]{3,2,1,0:T(8,128)(2,1)S(1)}, u32[]{:S(2)}, u32[]{:S(2)}) %all-to-all-start) | async-done | bytes 102432 | tf_op jit(solution)/shard_map/columns_exchange/all_to_all | solution.py:201
  127.6 2.5 %collective-permute-done.23 = bf16[40,1280]{1,0:T(8,128)(2,1)S(1)} collective-permute-done((bf16[40,1280]{1,0:T(8,128)(2,1)S(1)}, bf16[40,1280]{1,0:T(8,128)(2,1)S(1)}, u32[]{:S(2)}, u32[]{:S(2)}) %collective-permute-start.23) | collective-permute-done | bytes 102432 | tf_op jit(solution)/shard_map/mixed_line/ppermute | solution.py:45
  132.7 2.2 %collective-permute-start.26 = (bf16[160,1280]{1,0:T(8,128)(2,1)S(1)}, bf16[160,1280]{1,0:T(8,128)(2,1)S(1)}, u32[]{:S(2)}, u32[]{:S(2)}) collective-permute-start(bf16[160,1280]{1,0:T(8,128)(2,1)S(1)} %constant_dynamic-update-slice_fusion.m0), channel_id=1, source_target_pairs={{0,16},{1,5},{2,18},{3,7},{4,20},{5,1},{6,22},{7,3},{32,48},{33,37... | collective-permute-start | bytes 1228808 | tf_op jit(solution)/shard_map/mixed_plane/ppermute | solution.py:45
  136.7 4.4 %collective-permute-done.19.l2 = bf16[2,80,640]{2,1,0:T(8,128)(2,1)S(1)} collective-permute-done((bf16[2,80,640]{2,1,0:T(8,128)(2,1)S(1)}, bf16[2,80,640]{2,1,0:T(8,128)(2,1)S(1)}, u32[]{:S(2)}, u32[]{:S(2)}) %collective-permute-start.19) | collective-permute-done | bytes 204832 | tf_op jit(solution)/shard_map/points/ppermute | solution.py:45
  143.2 10.2 %collective-permute-done.26.m2 = bf16[160,1280]{1,0:T(8,128)(2,1)S(1)} collective-permute-done((bf16[160,1280]{1,0:T(8,128)(2,1)S(1)}, bf16[160,1280]{1,0:T(8,128)(2,1)S(1)}, u32[]{:S(2)}, u32[]{:S(2)}) %collective-permute-start.26) | collective-permute-done | bytes 409632 | tf_op jit(solution)/shard_map/mixed_plane/ppermute | solution.py:45
  (98 shorter events, 44.4 us)
Async XLA Ops:
  0.0 19.7 %collective-permute-start.3 = (bf16[192,6144]{1,0:T(8,128)(2,1)}, bf16[192,6144]{1,0:T(8,128)(2,1)}, u32[]{:S(2)}, u32[]{:S(2)}) collective-permute-start(bf16[192,6144]{1,0:T(8,128)(2,1)} %bitcast.71), channel_id=1, source_target_pairs={{0,1},{1,0},{2,3},{3,2},{4,5},{5,4},{6,7},{7,6},{32,33},{33,32},{3... | collective-permute-start | bytes 7077896 | tf_op jit(solution)/shard_map/rows_pair/ppermute | solution.py:45
  3.2 14.7 %collective-permute-start.2 = (bf16[40,6144]{1,0:T(8,128)(2,1)}, bf16[40,6144]{1,0:T(8,128)(2,1)S(1)}, u32[]{:S(2)}, u32[]{:S(2)}) collective-permute-start(bf16[40,6144]{1,0:T(8,128)(2,1)} %bitcast.73), channel_id=1, source_target_pairs={{0,2},{1,9},{2,4},{3,11},{4,6},{5,13},{6,32},{7,15},{32,34},{33,41... | collective-permute-start | bytes 1474568 | tf_op jit(solution)/shard_map/basis_line/ppermute | solution.py:45
  3.2 14.7 %collective-permute-start.1 = (bf16[40,6144]{1,0:T(8,128)(2,1)}, bf16[40,6144]{1,0:T(8,128)(2,1)S(1)}, u32[]{:S(2)}, u32[]{:S(2)}) collective-permute-start(bf16[40,6144]{1,0:T(8,128)(2,1)} %bitcast.74), channel_id=1, source_target_pairs={{0,4},{1,17},{2,38},{3,19},{4,32},{5,21},{6,2},{7,23},{32,36},{33,... | collective-permute-start | bytes 1474568 | tf_op jit(solution)/shard_map/basis_line/ppermute | solution.py:45
  5.4 13.1 %collective-permute-start = (bf16[40,6144]{1,0:T(8,128)(2,1)}, bf16[40,6144]{1,0:T(8,128)(2,1)S(1)}, u32[]{:S(2)}, u32[]{:S(2)}) collective-permute-start(bf16[40,6144]{1,0:T(8,128)(2,1)} %bitcast.75), channel_id=1, source_target_pairs={{0,38},{1,25},{2,0},{3,27},{4,2},{5,29},{6,4},{7,31},{32,6},{33,57... | collective-permute-start | bytes 1474568 | tf_op jit(solution)/shard_map/basis_line/ppermute | solution.py:45
  19.8 11.2 %collective-permute-start.4 = (bf16[40,6144]{1,0:T(8,128)(2,1)S(1)}, bf16[40,6144]{1,0:T(8,128)(2,1)S(1)}, u32[]{:S(2)}, u32[]{:S(2)}) collective-permute-start(bf16[40,6144]{1,0:T(8,128)(2,1)S(1)} %dynamic-slice_bitcast_fusion), channel_id=1, source_target_pairs={{0,16},{1,5},{2,18},{3,39},{4,20},{5,33},{6,22},{7,3},{32,48},{33,... | collective-permute-start | bytes 1474568 | tf_op jit(solution)/shard_map/basis_plane/ppermute | solution.py:45
  31.0 11.8 %collective-permute-start.5 = (bf16[40,6144]{1,0:T(8,128)(2,1)S(1)}, bf16[40,6144]{1,0:T(8,128)(2,1)S(1)}, u32[]{:S(2)}, u32[]{:S(2)}) collective-permute-start(bf16[40,6144]{1,0:T(8,128)(2,1)S(1)} %collective-permute-done.4), channel_id=1, source_target_pairs={{0,192},{1,193},{2,194},{3,195},{4,196},{5,197},{6,198},{7,199},{3... | collective-permute-start | bytes 1474568 | tf_op jit(solution)/shard_map/basis_plane/ppermute | solution.py:45
  33.5 12.6 %collective-permute-start.6 = (bf16[40,6144]{1,0:T(8,128)(2,1)S(1)}, bf16[40,6144]{1,0:T(8,128)(2,1)S(1)}, u32[]{:S(2)}, u32[]{:S(2)}) collective-permute-start(bf16[40,6144]{1,0:T(8,128)(2,1)S(1)} %collective-permute-done.4), channel_id=1, source_target_pairs={{0,64},{1,65},{2,66},{3,67},{4,68},{5,69},{6,70},{7,71},{32,96},{3... | collective-permute-start | bytes 1474568 | tf_op jit(solution)/shard_map/basis_plane/ppermute | solution.py:45
  33.5 21.3 %collective-permute-start.7 = (bf16[40,6144]{1,0:T(8,128)(2,1)S(1)}, bf16[40,6144]{1,0:T(8,128)(2,1)S(1)}, u32[]{:S(2)}, u32[]{:S(2)}) collective-permute-start(bf16[40,6144]{1,0:T(8,128)(2,1)S(1)} %collective-permute-done.4), channel_id=1, source_target_pairs={{0,128},{1,129},{2,130},{3,131},{4,132},{5,133},{6,134},{7,135},{3... | collective-permute-start | bytes 1474568 | tf_op jit(solution)/shard_map/basis_plane/ppermute | solution.py:45
  35.2 24.7 %collective-permute-start.8 = (bf16[160,6144]{1,0:T(8,128)(2,1)S(1)}, bf16[160,6144]{1,0:T(8,128)(2,1)S(1)}, u32[]{:S(2)}, u32[]{:S(2)}) collective-permute-start(bf16[160,6144]{1,0:T(8,128)(2,1)S(1)} %pad_maximum_fusion.u0), channel_id=1, source_target_pairs={{0,24},{1,39},{2,26},{3,1},{4,28},{5,3},{6,30},{7,5},{32,56},{33,7... | collective-permute-start | bytes 5898248 | tf_op jit(solution)/shard_map/basis_plane/ppermute | solution.py:45
  38.3 25.0 %collective-permute-start.9 = (bf16[160,6144]{1,0:T(8,128)(2,1)S(1)}, bf16[160,6144]{1,0:T(8,128)(2,1)S(1)}, u32[]{:S(2)}, u32[]{:S(2)}) collective-permute-start(bf16[160,6144]{1,0:T(8,128)(2,1)S(1)} %pad_maximum_fusion.u0), channel_id=1, source_target_pairs={{0,8},{1,3},{2,10},{3,5},{4,12},{5,7},{6,14},{7,33},{32,40},{33,35... | collective-permute-start | bytes 5898248 | tf_op jit(solution)/shard_map/basis_plane/ppermute | solution.py:45
  65.0 5.7 %collective-permute-start.12 = (bf16[4,40,384]{2,1,0:T(8,128)(2,1)S(1)}, bf16[4,40,384]{2,1,0:T(8,128)(2,1)S(1)}, u32[]{:S(2)}, u32[]{:S(2)}) collective-permute-start(bf16[4,40,384]{2,1,0:T(8,128)(2,1)S(1)} %bitcast.83), channel_id=1, source_target_pairs={{0,8},{1,3},{2,10},{3,5},{4,12},{5,7},{6,14},{7,1},{32,40},{33,35}... | collective-permute-start | bytes 368648 | tf_op jit(solution)/shard_map/projected_back/ppermute | solution.py:45
  66.7 6.8 %collective-permute-start.11 = (bf16[4,40,384]{2,1,0:T(8,128)(2,1)S(1)}, bf16[4,40,384]{2,1,0:T(8,128)(2,1)S(1)}, u32[]{:S(2)}, u32[]{:S(2)}) collective-permute-start(bf16[4,40,384]{2,1,0:T(8,128)(2,1)S(1)} %bitcast.82), channel_id=1, source_target_pairs={{0,16},{1,5},{2,18},{3,7},{4,20},{5,1},{6,22},{7,3},{32,48},{33,37... | collective-permute-start | bytes 368648 | tf_op jit(solution)/shard_map/projected_back/ppermute | solution.py:45
  67.7 6.1 %collective-permute-start.10 = (bf16[4,40,384]{2,1,0:T(8,128)(2,1)S(1)}, bf16[4,40,384]{2,1,0:T(8,128)(2,1)S(1)}, u32[]{:S(2)}, u32[]{:S(2)}) collective-permute-start(bf16[4,40,384]{2,1,0:T(8,128)(2,1)S(1)} %bitcast.81), channel_id=1, source_target_pairs={{0,24},{1,7},{2,26},{3,1},{4,28},{5,3},{6,30},{7,5},{32,56},{33,39... | collective-permute-start | bytes 368648 | tf_op jit(solution)/shard_map/projected_back/ppermute | solution.py:45
  74.2 6.3 %collective-permute-start.14 = (bf16[4,40,384]{2,1,0:T(8,128)(2,1)S(1)}, bf16[4,40,384]{2,1,0:T(8,128)(2,1)S(1)}, u32[]{:S(2)}, u32[]{:S(2)}) collective-permute-start(bf16[4,40,384]{2,1,0:T(8,128)(2,1)S(1)} %pad_maximum_fusion.5), channel_id=1, source_target_pairs={{0,4},{1,17},{2,6},{3,19},{4,0},{5,21},{6,2},{7,23},{32,36},{33,49... | collective-permute-start | bytes 368648 | tf_op jit(solution)/shard_map/projected_aside/ppermute | solution.py:45
  80.9 10.5 %collective-permute-start.16 = (bf16[4,4,40,384]{3,2,1,0:T(8,128)(2,1)S(1)}, bf16[4,4,40,384]{3,2,1,0:T(8,128)(2,1)S(1)}, u32[]{:S(2)}, u32[]{:S(2)}) collective-permute-start(bf16[4,4,40,384]{3,2,1,0:T(8,128)(2,1)S(1)} %pad_maximum_fusion.1.own_ref), channel_id=1, source_target_pairs={{0,1},{1,0},{2,3},{3,2},{4,5},{5,4},{6,7},{7,6},{32,33},{33,32},{3... | collective-permute-start | bytes 1474568 | tf_op jit(solution)/shard_map/projected_aside/ppermute | solution.py:45
  103.7 8.7 %collective-permute-start.17 = (bf16[80,640]{1,0:T(8,128)(2,1)S(1)}, bf16[80,640]{1,0:T(8,128)(2,1)S(1)}, u32[]{:S(2)}, u32[]{:S(2)}) collective-permute-start(bf16[80,640]{1,0:T(8,128)(2,1)S(1)} %get-tuple-element.24), channel_id=1, source_target_pairs={{0,32},{1,33},{2,34},{3,35},{4,36},{5,37},{6,38},{7,39},{32,0},{33... | collective-permute-start | bytes 307208 | tf_op jit(solution)/shard_map/columns_exchange/ppermute | solution.py:45
  107.7 14.3 %all-to-all-start = ((bf16[8,2,40,80]{3,2,1,0:T(8,128)(2,1)}), bf16[8,2,40,80]{3,2,1,0:T(8,128)(2,1)S(1)}, u32[]{:S(2)}, u32[]{:S(2)}) async-start(bf16[8,2,40,80]{3,2,1,0:T(8,128)(2,1)} %copy.8), calls=%async_computation | async-start | bytes 327680 | tf_op jit(solution)/shard_map/columns_exchange/all_to_all | solution.py:201
  112.5 23.1 %collective-permute-start.18 = (bf16[2,80,640]{2,1,0:T(8,128)(2,1)S(1)}, bf16[2,80,640]{2,1,0:T(8,128)(2,1)S(1)}, u32[]{:S(2)}, u32[]{:S(2)}) collective-permute-start(bf16[2,80,640]{2,1,0:T(8,128)(2,1)S(1)} %pad_maximum_fusion.2.l0), channel_id=1, source_target_pairs={{0,192},{1,193},{2,194},{3,195},{4,196},{5,197},{6,198},{7,199},{3... | collective-permute-start | bytes 614408 | tf_op jit(solution)/shard_map/points/ppermute | solution.py:45
  125.0 6.0 %collective-permute-start.24 = (bf16[40,1280]{1,0:T(8,128)(2,1)S(1)}, bf16[40,1280]{1,0:T(8,128)(2,1)S(1)}, u32[]{:S(2)}, u32[]{:S(2)}) collective-permute-start(bf16[40,1280]{1,0:T(8,128)(2,1)S(1)} %reshape.160), channel_id=1, source_target_pairs={{0,2},{1,9},{2,4},{3,11},{4,6},{5,13},{6,0},{7,15},{32,34},{33,41}... | collective-permute-start | bytes 307208 | tf_op jit(solution)/shard_map/mixed_line/ppermute | solution.py:45
  131.1 12.1 %collective-permute-start.25 = (bf16[160,1280]{1,0:T(8,128)(2,1)S(1)}, bf16[160,1280]{1,0:T(8,128)(2,1)S(1)}, u32[]{:S(2)}, u32[]{:S(2)}) collective-permute-start(bf16[160,1280]{1,0:T(8,128)(2,1)S(1)} %constant_dynamic-update-slice_fusion.m0), channel_id=1, source_target_pairs={{0,24},{1,7},{2,26},{3,1},{4,28},{5,3},{6,30},{7,5},{32,56},{33,39... | collective-permute-start | bytes 1228808 | tf_op jit(solution)/shard_map/mixed_plane/ppermute | solution.py:45
  132.7 20.7 %collective-permute-start.26 = (bf16[160,1280]{1,0:T(8,128)(2,1)S(1)}, bf16[160,1280]{1,0:T(8,128)(2,1)S(1)}, u32[]{:S(2)}, u32[]{:S(2)}) collective-permute-start(bf16[160,1280]{1,0:T(8,128)(2,1)S(1)} %constant_dynamic-update-slice_fusion.m0), channel_id=1, source_target_pairs={{0,16},{1,5},{2,18},{3,7},{4,20},{5,1},{6,22},{7,3},{32,48},{33,37... | collective-permute-start | bytes 1228808 | tf_op jit(solution)/shard_map/mixed_plane/ppermute | solution.py:45
  134.9 18.5 %collective-permute-start.27 = (bf16[160,1280]{1,0:T(8,128)(2,1)S(1)}, bf16[160,1280]{1,0:T(8,128)(2,1)S(1)}, u32[]{:S(2)}, u32[]{:S(2)}) collective-permute-start(bf16[160,1280]{1,0:T(8,128)(2,1)S(1)} %constant_dynamic-update-slice_fusion.m0), channel_id=1, source_target_pairs={{0,8},{1,3},{2,10},{3,5},{4,12},{5,7},{6,14},{7,1},{32,40},{33,35}... | collective-permute-start | bytes 1228808 | tf_op jit(solution)/shard_map/mixed_plane/ppermute | solution.py:45
  134.9 6.2 %collective-permute-start.19 = (bf16[2,80,640]{2,1,0:T(8,128)(2,1)S(1)}, bf16[2,80,640]{2,1,0:T(8,128)(2,1)S(1)}, u32[]{:S(2)}, u32[]{:S(2)}) collective-permute-start(bf16[2,80,640]{2,1,0:T(8,128)(2,1)S(1)} %pad_maximum_fusion.2.l0), channel_id=1, source_target_pairs={{0,128},{1,129},{2,130},{3,131},{4,132},{5,133},{6,134},{7,135},{3... | collective-permute-start | bytes 614408 | tf_op jit(solution)/shard_map/points/ppermute | solution.py:45
  135.6 7.6 %collective-permute-start.20 = (bf16[2,80,640]{2,1,0:T(8,128)(2,1)S(1)}, bf16[2,80,640]{2,1,0:T(8,128)(2,1)S(1)}, u32[]{:S(2)}, u32[]{:S(2)}) collective-permute-start(bf16[2,80,640]{2,1,0:T(8,128)(2,1)S(1)} %pad_maximum_fusion.2.l0), channel_id=1, source_target_pairs={{0,64},{1,65},{2,66},{3,67},{4,68},{5,69},{6,70},{7,71},{32,96},{3... | collective-permute-start | bytes 614408 | tf_op jit(solution)/shard_map/points/ppermute | solution.py:45
  (15 other events, 217.2 us)

commit v7 on v3

--- a/solution.py
+++ b/solution.py
@@ -38,6 +38,7 @@
 TWO = lambda v: 2 if v % 2 == 0 else -2
 CROSS = lambda step: pairs(lambda x, y, z, c: (x + step(x), y, z, c))
 CORE = pairs(lambda x, y, z, c: (x, y, z, 1 - c))
+HALF = pairs(lambda x, y, z, c: (x, y, z + 4, c))
 CHIPS = [[2 * chip + core for chip in range(16)] for core in range(2)]
 
 
@@ -60,11 +61,17 @@
     return lax.dynamic_slice_in_dim(jnp.concatenate([blocks, blocks], 0), (4 - start) % 4, 4, 0)
 
 
+def by_offset(values, width, axis):
+    firsts, rest, down, two, up = values
+    own, lower, upper = jnp.split(firsts, (width, 2 * width), axis)
+    return [jnp.concatenate(pair, axis) for pair in ((own, rest), (lower, down), (two,), (upper, up))]
+
+
 INTERPRET = False
 
 
-def product_kernel(left_ref, m0, m1, m2, m3, out_ref, right):
-    points, side, lanes = left_ref.shape
+def product_kernel(l0, l1, l2, l3, m0, m1, m2, m3, out_ref, right):
+    points = 8
     part = m0.shape[0]
     span = m0.shape[1] // points
     for a, m in enumerate((m0, m1, m2, m3)):
@@ -74,22 +81,24 @@
         low = span * r // 128 * 128
         high = min(-(-(span * r + span) // 128) * 128, points * span)
         at = span * r - low
-        term = jnp.dot(left_ref[r], right[:, low:high], preferred_element_type=F32)
+        left = (l0, l1, l2, l3)[r // 2]
+        term = jnp.dot(left[r % 2], right[:, low:high], preferred_element_type=F32)
         total = total + term[:, at : at + span]
     out_ref[...] = total
 
 
 def product(left, planes):
-    points, side, lanes = left.shape
+    _, side, lanes = left[0].shape
+    span = planes[0].shape[1]
     return pl.pallas_call(
         product_kernel,
-        out_shape=jax.ShapeDtypeStruct((side, planes[0].shape[1] // points), F32),
-        in_specs=[pl.BlockSpec(memory_space=pltpu.VMEM)] * 5,
+        out_shape=jax.ShapeDtypeStruct((side, span // 8), F32),
+        in_specs=[pl.BlockSpec(memory_space=pltpu.VMEM)] * 8,
         out_specs=pl.BlockSpec(memory_space=pltpu.VMEM),
-        scratch_shapes=[pltpu.VMEM((lanes, planes[0].shape[1]), BF)],
-        compiler_params=pltpu.CompilerParams(vmem_limit_bytes=32 * 1024 * 1024),
+        scratch_shapes=[pltpu.VMEM((lanes, span), BF)],
+        compiler_params=pltpu.CompilerParams(vmem_limit_bytes=12 * 1024 * 1024),
         interpret=INTERPRET,
-    )(left, *planes)
+    )(*left, *planes)
 
 
 def one_hot(spots, count):
@@ -108,25 +117,35 @@
     panel = basis.T
     width, depth = panel.shape
 
+    antisym = coupling - coupling.T
+    offset = jnp.arange(8)
+    order = (x + offset // 2) % 4 * 2 + (offset + point) % 2
+    turned = jnp.take(antisym, order, axis=1)
+    plane = along(False, True)
     with jax.named_scope("basis_line"):
-        line = jnp.concatenate(gather_line(panel, along(True, True)), 0)
+        pieces = gather_line(panel, along(True, True))
+        down, up = send(panel, plane(DOWN)), send(panel, plane(UP))
+        *pieces, down, up, turned, own_rows = lax.optimization_barrier((*pieces, down, up, turned, rows))
+        rest = jnp.concatenate(pieces[1:], 0)
+        other_rows = send(own_rows, CORE)
+        fetched = lax.select_n(x, *pieces)
+    with jax.named_scope("basis_plane"):
+        fetched, rest, other_rows = lax.optimization_barrier((send(fetched, plane(TWO)), rest, other_rows))
+        firsts = jnp.concatenate([panel, down, up], 0)
+        two = jnp.zeros((4, width, depth), BF)
+        for step, perm in ((0, None), (1, CROSS(DOWN)), (3, CROSS(UP)), (2, CROSS(TWO))):
+            piece = fetched if perm is None else send(fetched, perm)
+            two = lax.dynamic_update_index_in_dim(two, piece, (x + step) % 4, 0)
+        two = two.reshape(4 * width, depth)
+        units = firsts, rest, send(rest, plane(DOWN)), two, send(rest, plane(UP))
     with jax.named_scope("rows_pair"):
-        line, other_rows = lax.optimization_barrier((line, send(rows, CORE)))
         chip_rows = jnp.where(
             core == 0, jnp.concatenate([rows, other_rows], 0), jnp.concatenate([other_rows, rows], 0)
         )
         chip_rows = lax.optimization_barrier(chip_rows)
-    with jax.named_scope("basis_plane"):
-        plane = along(False, True)
-        fetched = lax.dynamic_index_in_dim(line.reshape(4, width, depth), x, 0, keepdims=False)
-        fetched, line = lax.optimization_barrier((send(fetched, plane(TWO)), line))
-        two = jnp.zeros((4, width, depth), BF)
-        for step, perm in ((0, None), (1, CROSS(DOWN)), (3, CROSS(UP)), (2, CROSS(TWO))):
-            piece = fetched if perm is None else send(fetched, perm)
-            two = lax.dynamic_update_index_in_dim(two, piece, (x + step) % 4, 0)
-        units = line, send(line, plane(DOWN)), two.reshape(4 * width, depth), send(line, plane(UP))
     with jax.named_scope("projected"):
-        parts = [unroll(nt(u, chip_rows).astype(BF).reshape(4, width, -1), first) for u in units]
+        parts = by_offset([nt(unit, chip_rows).astype(BF) for unit in units], width, 0)
+        parts = [unroll(part.reshape(4, width, -1), first) for part in parts]
         blocks = unroll(jnp.stack(parts), second)
         blocks = jnp.where(core == 0, blocks, blocks.transpose(1, 0, 2, 3)).reshape(16, width, -1)
     with jax.named_scope("projected_exchange"):
@@ -134,9 +153,10 @@
         own = got.transpose(1, 0, 2).reshape(width, depth)
         both = jnp.concatenate([own, send(own, CORE)], 0)
     with jax.named_scope("channel"):
-        channel = jnp.concatenate([nt(both, u).astype(BF) for u in units], 1)
+        channel = jnp.concatenate(by_offset([nt(both, unit).astype(BF) for unit in units], width, 1), 1)
     lanes = 16 * width
     with jax.named_scope("columns_exchange"):
+        left = [jnp.stack([channel, send(channel, HALF)])]
         crossed = send(channel[width:], CORE)
         block = jnp.arange(2 * lanes) // width
         dy, dz = (block // 8 - y) % 4, (block // 2 % 4 - z) % 4
@@ -146,20 +166,18 @@
         ordered += jnp.dot(crossed, one_hot(jnp.where(mine, -1, spot), lanes), preferred_element_type=F32)
         ordered = ordered.astype(BF).reshape(width, 8, 4 * width).transpose(1, 0, 2)
         chosen = lax.all_to_all(ordered, "pt", 0, 0, tiled=True)
-        chosen, channel = lax.optimization_barrier((chosen, channel))
         chosen = chosen.astype(F32)
-        antisym = coupling - coupling.T
-        mixed = jnp.einsum("qr,qin->irn", antisym, chosen, precision=lax.Precision.HIGHEST)
+        mixed = jnp.einsum("qr,qin->irn", turned, chosen, precision=lax.Precision.HIGHEST)
         mixed = mixed.astype(BF).reshape(width, -1)
         linear = jnp.einsum("q,qin->in", weights, chosen, precision=lax.Precision.HIGHEST)
+    with jax.named_scope("points"):
+        left = gather_line(left[0], CROSS)
     with jax.named_scope("mixed_line"):
         line = jnp.concatenate(gather_line(mixed, along(True, False)), 0)
-    with jax.named_scope("points"):
-        every = lax.all_to_all(jnp.broadcast_to(channel, (8,) + channel.shape), "pt", 0, 0, tiled=True)
     with jax.named_scope("mixed_plane"):
         planes = gather_line(line, along(False, False))
     with jax.named_scope("product"):
-        total = product(every, planes)
+        total = product(left, planes)
     with jax.named_scope("output"):
         return linear + total[:width] + send(total[width:], CORE)
 

time: 169 us -> 153 us (0.905)
  the two profiles are of different devices: /device:TPU:67 before, /device:TPU:1 now
where the time goes in v7:
time: 153 us; the launch traced here: 151 us
  waiting for transfers between devices  81.1 us (53%)
  starting transfers between devices  40.5 us (26%)
  matrix products  12.9 us (8%)
  other arithmetic  8.52 us (6%)
  local copies, waits for them, and re-layouts  6.79 us (4%)
    ppermute x25, waiting for transfers between devices, send(): return lax.ppermute(value, AXES, perm)  60.3 us
    ppermute x25, starting transfers between devices, send(): return lax.ppermute(value, AXES, perm)  32.4 us
    all_to_all x1, waiting for transfers between devices, shards(): lax.all_to_all(blocks, 'pan', 0, 0, axis_index_groups=CHIPS, tiled=True)  14 us
    dot_general x10, matrix products, nt(): lax.dot_general(a, b, (((1,), (1,)), ((), ())), preferred_element_type=F32)  11 us
    all_to_all x1, waiting for transfers between devices, shards(): chosen = lax.all_to_all(ordered, 'pt', 0, 0, tiled=True)  6.8 us
    all_to_all x1, starting transfers between devices, shards(): lax.all_to_all(blocks, 'pan', 0, 0, axis_index_groups=CHIPS, tiled=True)  4.23 us
    select_n x1, other arithmetic, shards(): jnp.where(core == 0, jnp.concatenate([rows, other_rows], 0), jnp.concaten...  3.97 us
    all_to_all x1, starting transfers between devices, shards(): chosen = lax.all_to_all(ordered, 'pt', 0, 0, tiled=True)  3.89 us
  transfers between devices with their start and end apart: 27, of which 18 were waited for; matrix products, arithmetic and copies ran while one was open for 12% of the time, Pallas kernels for 0%

profile of v7, /device:TPU:1, one launch (start us, length us, event | category | flops | bytes accessed | tf_op | source)
XLA Modules:
  0.0 150.9 jit_solution(11362558575693310350)
XLA Ops:
  0.0 3.6 %collective-permute-start = (bf16[40,6144]{1,0:T(8,128)(2,1)}, bf16[40,6144]{1,0:T(8,128)(2,1)S(1)}, u32[]{:S(2)}, u32[]{:S(2)}) collective-permute-start(bf16[40,6144]{1,0:T(8,128)(2,1)} %bitcast.101), channel_id=1, source_target_pairs={{0,38},{1,25},{2,0},{3,27},{4,2},{5,29},{6,4},{7,31},{32,6},{33,57... | collective-permute-start | bytes 1474568 | tf_op jit(solution)/shard_map/basis_line/ppermute | solution.py:46
  4.6 5.6 %collective-permute-start.3 = (bf16[40,6144]{1,0:T(8,128)(2,1)}, bf16[40,6144]{1,0:T(8,128)(2,1)S(1)}, u32[]{:S(2)}, u32[]{:S(2)}) collective-permute-start(bf16[40,6144]{1,0:T(8,128)(2,1)} %bitcast.104), channel_id=1, source_target_pairs={{0,24},{1,39},{2,26},{3,1},{4,28},{5,3},{6,30},{7,5},{32,56},{33,7... | collective-permute-start | bytes 1474568 | tf_op jit(solution)/shard_map/basis_line/ppermute | solution.py:46
  12.3 3.5 %collective-permute-done = bf16[40,6144]{1,0:T(8,128)(2,1)S(1)} collective-permute-done((bf16[40,6144]{1,0:T(8,128)(2,1)}, bf16[40,6144]{1,0:T(8,128)(2,1)S(1)}, u32[]{:S(2)}, u32[]{:S(2)}) %collective-permute-start) | collective-permute-done | bytes 491552 | tf_op jit(solution)/shard_map/basis_line/ppermute | solution.py:46
  15.8 3.7 %collective-permute-done.2 = bf16[40,6144]{1,0:T(8,128)(2,1)S(1)} collective-permute-done((bf16[40,6144]{1,0:T(8,128)(2,1)}, bf16[40,6144]{1,0:T(8,128)(2,1)S(1)}, u32[]{:S(2)}, u32[]{:S(2)}) %collective-permute-start.2) | collective-permute-done | bytes 491552 | tf_op jit(solution)/shard_map/basis_line/ppermute | solution.py:46
  19.5 4.6 %collective-permute-done.3 = bf16[40,6144]{1,0:T(8,128)(2,1)S(1)} collective-permute-done((bf16[40,6144]{1,0:T(8,128)(2,1)}, bf16[40,6144]{1,0:T(8,128)(2,1)S(1)}, u32[]{:S(2)}, u32[]{:S(2)}) %collective-permute-start.3) | collective-permute-done | bytes 491552 | tf_op jit(solution)/shard_map/basis_line/ppermute | solution.py:46
  24.2 3.3 %collective-permute-done.4 = bf16[40,6144]{1,0:T(8,128)(2,1)S(1)} collective-permute-done((bf16[40,6144]{1,0:T(8,128)(2,1)}, bf16[40,6144]{1,0:T(8,128)(2,1)S(1)}, u32[]{:S(2)}, u32[]{:S(2)}) %collective-permute-start.4) | collective-permute-done | bytes 491552 | tf_op jit(solution)/shard_map/basis_line/ppermute | solution.py:46
  29.1 9.9 %collective-permute-done.5 = bf16[40,6144]{1,0:T(8,128)(2,1)S(1)} collective-permute-done((bf16[40,6144]{1,0:T(8,128)(2,1)S(1)}, bf16[40,6144]{1,0:T(8,128)(2,1)S(1)}, u32[]{:S(2)}, u32[]{:S(2)}) %collective-permute-start.5) | collective-permute-done | bytes 491552 | tf_op jit(solution)/shard_map/basis_plane/ppermute | solution.py:46
  40.7 1.7 %collective-permute-start.10 = (bf16[40,6144]{1,0:T(8,128)(2,1)S(1)}, bf16[40,6144]{1,0:T(8,128)(2,1)S(1)}, u32[]{:S(2)}, u32[]{:S(2)}) collective-permute-start(bf16[40,6144]{1,0:T(8,128)(2,1)S(1)} %collective-permute-done.5), channel_id=1, source_target_pairs={{0,128},{1,129},{2,130},{3,131},{4,132},{5,133},{6,134},{7,135},{3... | collective-permute-start | bytes 1474568 | tf_op jit(solution)/shard_map/basis_plane/ppermute | solution.py:46
  42.4 2.7 %collective-permute-start.7 = (bf16[120,6144]{1,0:T(8,128)(2,1)S(1)}, bf16[120,6144]{1,0:T(8,128)(2,1)S(1)}, u32[]{:S(2)}, u32[]{:S(2)}) collective-permute-start(bf16[120,6144]{1,0:T(8,128)(2,1)S(1)} %pad_maximum_fusion.1), channel_id=1, source_target_pairs={{0,24},{1,39},{2,26},{3,1},{4,28},{5,3},{6,30},{7,5},{32,56},{33,7... | collective-permute-start | bytes 4423688 | tf_op jit(solution)/shard_map/basis_plane/ppermute | solution.py:46
  45.1 4.0 %maximum_select_fusion = bf16[384,6144]{1,0:T(8,128)(2,1)S(1)} fusion(bf16[192,6144]{1,0:T(8,128)(2,1)} %collective-permute-done.6, bf16[192,6144]{1,0:T(8,128)(2,1)S(1)} %bitcast.88, pred[]{:T(512)S(6)} %eq.78), kind=kLoop, calls=%fused_computation.1 | loop fusion | flops 21233664 | bytes 9437185 | tf_op jit(solution)/shard_map/rows_pair/jit(_where)/select_n | solution.py:142
  54.9 8.7 %collective-permute-done.10 = bf16[40,6144]{1,0:T(8,128)(2,1)S(1)} collective-permute-done((bf16[40,6144]{1,0:T(8,128)(2,1)S(1)}, bf16[40,6144]{1,0:T(8,128)(2,1)S(1)}, u32[]{:S(2)}, u32[]{:S(2)}) %collective-permute-start.10) | collective-permute-done | bytes 491552 | tf_op jit(solution)/shard_map/basis_plane/ppermute | solution.py:46
  69.9 4.2 %all-to-all-start = ((bf16[16,40,384]{2,1,0:T(8,128)(2,1)}), bf16[16,40,384]{2,1,0:T(8,128)(2,1)}, u32[]{:S(2)}, u32[]{:S(2)}) async-start(bf16[16,40,384]{2,1,0:T(8,128)(2,1)} %bitcast.89), calls=%async_computation | async-start | bytes 983040 | tf_op jit(solution)/shard_map/projected_exchange/all_to_all | solution.py:152
  74.2 14.0 %all-to-all-done = bf16[16,40,384]{2,1,0:T(8,128)(2,1)} async-done(((bf16[16,40,384]{2,1,0:T(8,128)(2,1)}), bf16[16,40,384]{2,1,0:T(8,128)(2,1)}, u32[]{:S(2)}, u32[]{:S(2)}) %all-to-all-start) | async-done | bytes 491552 | tf_op jit(solution)/shard_map/projected_exchange/all_to_all | solution.py:152
  89.3 2.8 %collective-permute-start.12 = (bf16[40,6144]{1,0:T(8,128)(2,1)S(1)}, bf16[40,6144]{1,0:T(8,128)(2,1)S(1)}, u32[]{:S(2)}, u32[]{:S(2)}) collective-permute-start(bf16[40,6144]{1,0:T(8,128)(2,1)S(1)} %bitcast.90), channel_id=1, source_target_pairs={{0,1},{1,0},{2,3},{3,2},{4,5},{5,4},{6,7},{7,6},{32,33},{33,32},{3... | collective-permute-start | bytes 1474568 | tf_op jit(solution)/shard_map/projected_exchange/ppermute | solution.py:46
  98.7 3.7 %collective-permute-start.14 = (bf16[80,640]{1,0:T(8,128)(2,1)S(1)}, bf16[80,640]{1,0:T(8,128)(2,1)S(1)}, u32[]{:S(2)}, u32[]{:S(2)}) collective-permute-start(bf16[80,640]{1,0:T(8,128)(2,1)S(1)} %concatenate.59), channel_id=1, source_target_pairs={{0,32},{1,33},{2,34},{3,35},{4,36},{5,37},{6,38},{7,39},{32,0},{33... | collective-permute-start | bytes 307208 | tf_op jit(solution)/shard_map/columns_exchange/ppermute | solution.py:46
  105.6 3.9 %all-to-all-start.1 = ((bf16[8,40,160]{2,1,0:T(8,128)(2,1)}), bf16[8,40,160]{2,1,0:T(8,128)(2,1)S(1)}, u32[]{:S(2)}, u32[]{:S(2)}) async-start(bf16[8,40,160]{2,1,0:T(8,128)(2,1)} %bitcast.84), calls=%async_computation.1 | async-start | bytes 327680 | tf_op jit(solution)/shard_map/columns_exchange/all_to_all | solution.py:168
  109.5 2.7 %collective-permute-start.15 = (bf16[2,80,640]{2,1,0:T(8,128)(2,1)S(1)}, bf16[2,80,640]{2,1,0:T(8,128)(2,1)S(1)}, u32[]{:S(2)}, u32[]{:S(2)}) collective-permute-start(bf16[2,80,640]{2,1,0:T(8,128)(2,1)S(1)} %pad_maximum_fusion.4.l0), channel_id=1, source_target_pairs={{0,192},{1,193},{2,194},{3,195},{4,196},{5,197},{6,198},{7,199},{3... | collective-permute-start | bytes 614408 | tf_op jit(solution)/shard_map/points/ppermute | solution.py:46
  112.2 6.8 %all-to-all-done.1 = bf16[8,40,160]{2,1,0:T(8,128)(2,1)S(1)} async-done(((bf16[8,40,160]{2,1,0:T(8,128)(2,1)}), bf16[8,40,160]{2,1,0:T(8,128)(2,1)S(1)}, u32[]{:S(2)}, u32[]{:S(2)}) %all-to-all-start.1) | async-done | bytes 102432 | tf_op jit(solution)/shard_map/columns_exchange/all_to_all | solution.py:168
  121.3 1.9 %collective-permute-done.18 = bf16[40,1280]{1,0:T(8,128)(2,1)S(1)} collective-permute-done((bf16[40,1280]{1,0:T(8,128)(2,1)S(1)}, bf16[40,1280]{1,0:T(8,128)(2,1)S(1)}, u32[]{:S(2)}, u32[]{:S(2)}) %collective-permute-start.18) | collective-permute-done | bytes 102432 | tf_op jit(solution)/shard_map/mixed_line/ppermute | solution.py:46
  123.1 2.3 %collective-permute-done.19 = bf16[40,1280]{1,0:T(8,128)(2,1)S(1)} collective-permute-done((bf16[40,1280]{1,0:T(8,128)(2,1)S(1)}, bf16[40,1280]{1,0:T(8,128)(2,1)S(1)}, u32[]{:S(2)}, u32[]{:S(2)}) %collective-permute-start.19) | collective-permute-done | bytes 102432 | tf_op jit(solution)/shard_map/mixed_line/ppermute | solution.py:46
  127.6 2.2 %collective-permute-start.22 = (bf16[160,1280]{1,0:T(8,128)(2,1)S(1)}, bf16[160,1280]{1,0:T(8,128)(2,1)S(1)}, u32[]{:S(2)}, u32[]{:S(2)}) collective-permute-start(bf16[160,1280]{1,0:T(8,128)(2,1)S(1)} %constant_dynamic-update-slice_fusion.2.m0), channel_id=1, source_target_pairs={{0,16},{1,5},{2,18},{3,7},{4,20},{5,1},{6,22},{7,3},{32,48},{33,37... | collective-permute-start | bytes 1228808 | tf_op jit(solution)/shard_map/mixed_plane/ppermute | solution.py:46
  130.9 5.0 %collective-permute-done.16.l2 = bf16[2,80,640]{2,1,0:T(8,128)(2,1)S(1)} collective-permute-done((bf16[2,80,640]{2,1,0:T(8,128)(2,1)S(1)}, bf16[2,80,640]{2,1,0:T(8,128)(2,1)S(1)}, u32[]{:S(2)}, u32[]{:S(2)}) %collective-permute-start.16) | collective-permute-done | bytes 204832 | tf_op jit(solution)/shard_map/points/ppermute | solution.py:46
  136.0 2.4 %collective-permute-done.17.l3 = bf16[2,80,640]{2,1,0:T(8,128)(2,1)S(1)} collective-permute-done((bf16[2,80,640]{2,1,0:T(8,128)(2,1)S(1)}, bf16[2,80,640]{2,1,0:T(8,128)(2,1)S(1)}, u32[]{:S(2)}, u32[]{:S(2)}) %collective-permute-start.17) | collective-permute-done | bytes 204832 | tf_op jit(solution)/shard_map/points/ppermute | solution.py:46
  138.4 9.9 %collective-permute-done.22.m2 = bf16[160,1280]{1,0:T(8,128)(2,1)S(1)} collective-permute-done((bf16[160,1280]{1,0:T(8,128)(2,1)S(1)}, bf16[160,1280]{1,0:T(8,128)(2,1)S(1)}, u32[]{:S(2)}, u32[]{:S(2)}) %collective-permute-start.22) | collective-permute-done | bytes 409632 | tf_op jit(solution)/shard_map/mixed_plane/ppermute | solution.py:46
  (119 shorter events, 37.4 us)
Async XLA Ops:
  0.0 15.8 %collective-permute-start = (bf16[40,6144]{1,0:T(8,128)(2,1)}, bf16[40,6144]{1,0:T(8,128)(2,1)S(1)}, u32[]{:S(2)}, u32[]{:S(2)}) collective-permute-start(bf16[40,6144]{1,0:T(8,128)(2,1)} %bitcast.101), channel_id=1, source_target_pairs={{0,38},{1,25},{2,0},{3,27},{4,2},{5,29},{6,4},{7,31},{32,6},{33,57... | collective-permute-start | bytes 1474568 | tf_op jit(solution)/shard_map/basis_line/ppermute | solution.py:46
  3.6 12.2 %collective-permute-start.1 = (bf16[40,6144]{1,0:T(8,128)(2,1)}, bf16[40,6144]{1,0:T(8,128)(2,1)S(1)}, u32[]{:S(2)}, u32[]{:S(2)}) collective-permute-start(bf16[40,6144]{1,0:T(8,128)(2,1)} %bitcast.102), channel_id=1, source_target_pairs={{0,4},{1,17},{2,38},{3,19},{4,32},{5,21},{6,2},{7,23},{32,36},{33,... | collective-permute-start | bytes 1474568 | tf_op jit(solution)/shard_map/basis_line/ppermute | solution.py:46
  3.9 15.6 %collective-permute-start.2 = (bf16[40,6144]{1,0:T(8,128)(2,1)}, bf16[40,6144]{1,0:T(8,128)(2,1)S(1)}, u32[]{:S(2)}, u32[]{:S(2)}) collective-permute-start(bf16[40,6144]{1,0:T(8,128)(2,1)} %bitcast.103), channel_id=1, source_target_pairs={{0,2},{1,9},{2,4},{3,11},{4,6},{5,13},{6,32},{7,15},{32,34},{33,41... | collective-permute-start | bytes 1474568 | tf_op jit(solution)/shard_map/basis_line/ppermute | solution.py:46
  4.6 19.6 %collective-permute-start.3 = (bf16[40,6144]{1,0:T(8,128)(2,1)}, bf16[40,6144]{1,0:T(8,128)(2,1)S(1)}, u32[]{:S(2)}, u32[]{:S(2)}) collective-permute-start(bf16[40,6144]{1,0:T(8,128)(2,1)} %bitcast.104), channel_id=1, source_target_pairs={{0,24},{1,39},{2,26},{3,1},{4,28},{5,3},{6,30},{7,5},{32,56},{33,7... | collective-permute-start | bytes 1474568 | tf_op jit(solution)/shard_map/basis_line/ppermute | solution.py:46
  10.2 17.3 %collective-permute-start.4 = (bf16[40,6144]{1,0:T(8,128)(2,1)}, bf16[40,6144]{1,0:T(8,128)(2,1)S(1)}, u32[]{:S(2)}, u32[]{:S(2)}) collective-permute-start(bf16[40,6144]{1,0:T(8,128)(2,1)} %bitcast.105), channel_id=1, source_target_pairs={{0,8},{1,3},{2,10},{3,5},{4,12},{5,7},{6,14},{7,33},{32,40},{33,35... | collective-permute-start | bytes 1474568 | tf_op jit(solution)/shard_map/basis_line/ppermute | solution.py:46
  27.5 11.6 %collective-permute-start.6 = (bf16[192,6144]{1,0:T(8,128)(2,1)}, bf16[192,6144]{1,0:T(8,128)(2,1)}, u32[]{:S(2)}, u32[]{:S(2)}) collective-permute-start(bf16[192,6144]{1,0:T(8,128)(2,1)} %bitcast.87), channel_id=1, source_target_pairs={{0,1},{1,0},{2,3},{3,2},{4,5},{5,4},{6,7},{7,6},{32,33},{33,32},{3... | collective-permute-start | bytes 7077896 | tf_op jit(solution)/shard_map/basis_line/ppermute | solution.py:46
  28.9 10.2 %collective-permute-start.5 = (bf16[40,6144]{1,0:T(8,128)(2,1)S(1)}, bf16[40,6144]{1,0:T(8,128)(2,1)S(1)}, u32[]{:S(2)}, u32[]{:S(2)}) collective-permute-start(bf16[40,6144]{1,0:T(8,128)(2,1)S(1)} %select_select_fusion), channel_id=1, source_target_pairs={{0,16},{1,5},{2,18},{3,39},{4,20},{5,33},{6,22},{7,3},{32,48},{33,... | collective-permute-start | bytes 1474568 | tf_op jit(solution)/shard_map/basis_plane/ppermute | solution.py:46
  39.0 14.5 %collective-permute-start.8 = (bf16[40,6144]{1,0:T(8,128)(2,1)S(1)}, bf16[40,6144]{1,0:T(8,128)(2,1)S(1)}, u32[]{:S(2)}, u32[]{:S(2)}) collective-permute-start(bf16[40,6144]{1,0:T(8,128)(2,1)S(1)} %collective-permute-done.5), channel_id=1, source_target_pairs={{0,192},{1,193},{2,194},{3,195},{4,196},{5,197},{6,198},{7,199},{3... | collective-permute-start | bytes 1474568 | tf_op jit(solution)/shard_map/basis_plane/ppermute | solution.py:46
  40.7 14.2 %collective-permute-start.9 = (bf16[40,6144]{1,0:T(8,128)(2,1)S(1)}, bf16[40,6144]{1,0:T(8,128)(2,1)S(1)}, u32[]{:S(2)}, u32[]{:S(2)}) collective-permute-start(bf16[40,6144]{1,0:T(8,128)(2,1)S(1)} %collective-permute-done.5), channel_id=1, source_target_pairs={{0,64},{1,65},{2,66},{3,67},{4,68},{5,69},{6,70},{7,71},{32,96},{3... | collective-permute-start | bytes 1474568 | tf_op jit(solution)/shard_map/basis_plane/ppermute | solution.py:46
  40.7 22.9 %collective-permute-start.10 = (bf16[40,6144]{1,0:T(8,128)(2,1)S(1)}, bf16[40,6144]{1,0:T(8,128)(2,1)S(1)}, u32[]{:S(2)}, u32[]{:S(2)}) collective-permute-start(bf16[40,6144]{1,0:T(8,128)(2,1)S(1)} %collective-permute-done.5), channel_id=1, source_target_pairs={{0,128},{1,129},{2,130},{3,131},{4,132},{5,133},{6,134},{7,135},{3... | collective-permute-start | bytes 1474568 | tf_op jit(solution)/shard_map/basis_plane/ppermute | solution.py:46
  42.4 23.0 %collective-permute-start.11 = (bf16[120,6144]{1,0:T(8,128)(2,1)S(1)}, bf16[120,6144]{1,0:T(8,128)(2,1)S(1)}, u32[]{:S(2)}, u32[]{:S(2)}) collective-permute-start(bf16[120,6144]{1,0:T(8,128)(2,1)S(1)} %pad_maximum_fusion.1), channel_id=1, source_target_pairs={{0,8},{1,3},{2,10},{3,5},{4,12},{5,7},{6,14},{7,33},{32,40},{33,35... | collective-permute-start | bytes 4423688 | tf_op jit(solution)/shard_map/basis_plane/ppermute | solution.py:46
  42.4 24.5 %collective-permute-start.7 = (bf16[120,6144]{1,0:T(8,128)(2,1)S(1)}, bf16[120,6144]{1,0:T(8,128)(2,1)S(1)}, u32[]{:S(2)}, u32[]{:S(2)}) collective-permute-start(bf16[120,6144]{1,0:T(8,128)(2,1)S(1)} %pad_maximum_fusion.1), channel_id=1, source_target_pairs={{0,24},{1,39},{2,26},{3,1},{4,28},{5,3},{6,30},{7,5},{32,56},{33,7... | collective-permute-start | bytes 4423688 | tf_op jit(solution)/shard_map/basis_plane/ppermute | solution.py:46
  69.9 18.3 %all-to-all-start = ((bf16[16,40,384]{2,1,0:T(8,128)(2,1)}), bf16[16,40,384]{2,1,0:T(8,128)(2,1)}, u32[]{:S(2)}, u32[]{:S(2)}) async-start(bf16[16,40,384]{2,1,0:T(8,128)(2,1)} %bitcast.89), calls=%async_computation | async-start | bytes 983040 | tf_op jit(solution)/shard_map/projected_exchange/all_to_all | solution.py:152
  89.3 4.3 %collective-permute-start.12 = (bf16[40,6144]{1,0:T(8,128)(2,1)S(1)}, bf16[40,6144]{1,0:T(8,128)(2,1)S(1)}, u32[]{:S(2)}, u32[]{:S(2)}) collective-permute-start(bf16[40,6144]{1,0:T(8,128)(2,1)S(1)} %bitcast.90), channel_id=1, source_target_pairs={{0,1},{1,0},{2,3},{3,2},{4,5},{5,4},{6,7},{7,6},{32,33},{33,32},{3... | collective-permute-start | bytes 1474568 | tf_op jit(solution)/shard_map/projected_exchange/ppermute | solution.py:46
  98.7 10.8 %collective-permute-start.14 = (bf16[80,640]{1,0:T(8,128)(2,1)S(1)}, bf16[80,640]{1,0:T(8,128)(2,1)S(1)}, u32[]{:S(2)}, u32[]{:S(2)}) collective-permute-start(bf16[80,640]{1,0:T(8,128)(2,1)S(1)} %concatenate.59), channel_id=1, source_target_pairs={{0,32},{1,33},{2,34},{3,35},{4,36},{5,37},{6,38},{7,39},{32,0},{33... | collective-permute-start | bytes 307208 | tf_op jit(solution)/shard_map/columns_exchange/ppermute | solution.py:46
  105.6 13.5 %all-to-all-start.1 = ((bf16[8,40,160]{2,1,0:T(8,128)(2,1)}), bf16[8,40,160]{2,1,0:T(8,128)(2,1)S(1)}, u32[]{:S(2)}, u32[]{:S(2)}) async-start(bf16[8,40,160]{2,1,0:T(8,128)(2,1)} %bitcast.84), calls=%async_computation.1 | async-start | bytes 327680 | tf_op jit(solution)/shard_map/columns_exchange/all_to_all | solution.py:168
  109.5 20.9 %collective-permute-start.15 = (bf16[2,80,640]{2,1,0:T(8,128)(2,1)S(1)}, bf16[2,80,640]{2,1,0:T(8,128)(2,1)S(1)}, u32[]{:S(2)}, u32[]{:S(2)}) collective-permute-start(bf16[2,80,640]{2,1,0:T(8,128)(2,1)S(1)} %pad_maximum_fusion.4.l0), channel_id=1, source_target_pairs={{0,192},{1,193},{2,194},{3,195},{4,196},{5,197},{6,198},{7,199},{3... | collective-permute-start | bytes 614408 | tf_op jit(solution)/shard_map/points/ppermute | solution.py:46
  120.3 5.2 %collective-permute-start.19 = (bf16[40,1280]{1,0:T(8,128)(2,1)S(1)}, bf16[40,1280]{1,0:T(8,128)(2,1)S(1)}, u32[]{:S(2)}, u32[]{:S(2)}) collective-permute-start(bf16[40,1280]{1,0:T(8,128)(2,1)S(1)} %reshape.267), channel_id=1, source_target_pairs={{0,4},{1,17},{2,6},{3,19},{4,0},{5,21},{6,2},{7,23},{32,36},{33,49... | collective-permute-start | bytes 307208 | tf_op jit(solution)/shard_map/mixed_line/ppermute | solution.py:46
  120.6 6.0 %collective-permute-start.20 = (bf16[40,1280]{1,0:T(8,128)(2,1)S(1)}, bf16[40,1280]{1,0:T(8,128)(2,1)S(1)}, u32[]{:S(2)}, u32[]{:S(2)}) collective-permute-start(bf16[40,1280]{1,0:T(8,128)(2,1)S(1)} %reshape.267), channel_id=1, source_target_pairs={{0,2},{1,9},{2,4},{3,11},{4,6},{5,13},{6,0},{7,15},{32,34},{33,41}... | collective-permute-start | bytes 307208 | tf_op jit(solution)/shard_map/mixed_line/ppermute | solution.py:46
  126.6 11.8 %collective-permute-start.21 = (bf16[160,1280]{1,0:T(8,128)(2,1)S(1)}, bf16[160,1280]{1,0:T(8,128)(2,1)S(1)}, u32[]{:S(2)}, u32[]{:S(2)}) collective-permute-start(bf16[160,1280]{1,0:T(8,128)(2,1)S(1)} %constant_dynamic-update-slice_fusion.2.m0), channel_id=1, source_target_pairs={{0,24},{1,7},{2,26},{3,1},{4,28},{5,3},{6,30},{7,5},{32,56},{33,39... | collective-permute-start | bytes 1228808 | tf_op jit(solution)/shard_map/mixed_plane/ppermute | solution.py:46
  127.6 20.7 %collective-permute-start.22 = (bf16[160,1280]{1,0:T(8,128)(2,1)S(1)}, bf16[160,1280]{1,0:T(8,128)(2,1)S(1)}, u32[]{:S(2)}, u32[]{:S(2)}) collective-permute-start(bf16[160,1280]{1,0:T(8,128)(2,1)S(1)} %constant_dynamic-update-slice_fusion.2.m0), channel_id=1, source_target_pairs={{0,16},{1,5},{2,18},{3,7},{4,20},{5,1},{6,22},{7,3},{32,48},{33,37... | collective-permute-start | bytes 1228808 | tf_op jit(solution)/shard_map/mixed_plane/ppermute | solution.py:46
  129.8 18.5 %collective-permute-start.23 = (bf16[160,1280]{1,0:T(8,128)(2,1)S(1)}, bf16[160,1280]{1,0:T(8,128)(2,1)S(1)}, u32[]{:S(2)}, u32[]{:S(2)}) collective-permute-start(bf16[160,1280]{1,0:T(8,128)(2,1)S(1)} %constant_dynamic-update-slice_fusion.2.m0), channel_id=1, source_target_pairs={{0,8},{1,3},{2,10},{3,5},{4,12},{5,7},{6,14},{7,1},{32,40},{33,35}... | collective-permute-start | bytes 1228808 | tf_op jit(solution)/shard_map/mixed_plane/ppermute | solution.py:46
  129.8 6.2 %collective-permute-start.16 = (bf16[2,80,640]{2,1,0:T(8,128)(2,1)S(1)}, bf16[2,80,640]{2,1,0:T(8,128)(2,1)S(1)}, u32[]{:S(2)}, u32[]{:S(2)}) collective-permute-start(bf16[2,80,640]{2,1,0:T(8,128)(2,1)S(1)} %pad_maximum_fusion.4.l0), channel_id=1, source_target_pairs={{0,128},{1,129},{2,130},{3,131},{4,132},{5,133},{6,134},{7,135},{3... | collective-permute-start | bytes 614408 | tf_op jit(solution)/shard_map/points/ppermute | solution.py:46
  130.4 8.0 %collective-permute-start.17 = (bf16[2,80,640]{2,1,0:T(8,128)(2,1)S(1)}, bf16[2,80,640]{2,1,0:T(8,128)(2,1)S(1)}, u32[]{:S(2)}, u32[]{:S(2)}) collective-permute-start(bf16[2,80,640]{2,1,0:T(8,128)(2,1)S(1)} %pad_maximum_fusion.4.l0), channel_id=1, source_target_pairs={{0,64},{1,65},{2,66},{3,67},{4,68},{5,69},{6,70},{7,71},{32,96},{3... | collective-permute-start | bytes 614408 | tf_op jit(solution)/shard_map/points/ppermute | solution.py:46
  (17 other events, 189.4 us)

commit v8 on v3

--- a/solution.py
+++ b/solution.py
@@ -38,6 +38,7 @@
 TWO = lambda v: 2 if v % 2 == 0 else -2
 CROSS = lambda step: pairs(lambda x, y, z, c: (x + step(x), y, z, c))
 CORE = pairs(lambda x, y, z, c: (x, y, z, 1 - c))
+HALF = pairs(lambda x, y, z, c: (x, y, z + 4, c))
 CHIPS = [[2 * chip + core for chip in range(16)] for core in range(2)]
 
 
@@ -63,8 +64,8 @@
 INTERPRET = False
 
 
-def product_kernel(left_ref, m0, m1, m2, m3, out_ref, right):
-    points, side, lanes = left_ref.shape
+def product_kernel(l0, l1, l2, l3, m0, m1, m2, m3, out_ref, right):
+    points = 8
     part = m0.shape[0]
     span = m0.shape[1] // points
     for a, m in enumerate((m0, m1, m2, m3)):
@@ -74,22 +75,24 @@
         low = span * r // 128 * 128
         high = min(-(-(span * r + span) // 128) * 128, points * span)
         at = span * r - low
-        term = jnp.dot(left_ref[r], right[:, low:high], preferred_element_type=F32)
+        left = (l0, l1, l2, l3)[r // 2]
+        term = jnp.dot(left[r % 2], right[:, low:high], preferred_element_type=F32)
         total = total + term[:, at : at + span]
     out_ref[...] = total
 
 
 def product(left, planes):
-    points, side, lanes = left.shape
+    _, side, lanes = left[0].shape
+    span = planes[0].shape[1]
     return pl.pallas_call(
         product_kernel,
-        out_shape=jax.ShapeDtypeStruct((side, planes[0].shape[1] // points), F32),
-        in_specs=[pl.BlockSpec(memory_space=pltpu.VMEM)] * 5,
+        out_shape=jax.ShapeDtypeStruct((side, span // 8), F32),
+        in_specs=[pl.BlockSpec(memory_space=pltpu.VMEM)] * 8,
         out_specs=pl.BlockSpec(memory_space=pltpu.VMEM),
-        scratch_shapes=[pltpu.VMEM((lanes, planes[0].shape[1]), BF)],
-        compiler_params=pltpu.CompilerParams(vmem_limit_bytes=32 * 1024 * 1024),
+        scratch_shapes=[pltpu.VMEM((lanes, span), BF)],
+        compiler_params=pltpu.CompilerParams(vmem_limit_bytes=12 * 1024 * 1024),
         interpret=INTERPRET,
-    )(left, *planes)
+    )(*left, *planes)
 
 
 def one_hot(spots, count):
@@ -108,10 +111,14 @@
     panel = basis.T
     width, depth = panel.shape
 
+    antisym = coupling - coupling.T
+    offset = jnp.arange(8)
+    order = (x + offset // 2) % 4 * 2 + (offset + point) % 2
+    turned = jnp.take(antisym, order, axis=1)
     with jax.named_scope("basis_line"):
         line = jnp.concatenate(gather_line(panel, along(True, True)), 0)
     with jax.named_scope("rows_pair"):
-        line, other_rows = lax.optimization_barrier((line, send(rows, CORE)))
+        line, other_rows, turned = lax.optimization_barrier((line, send(rows, CORE), turned))
         chip_rows = jnp.where(
             core == 0, jnp.concatenate([rows, other_rows], 0), jnp.concatenate([other_rows, rows], 0)
         )
@@ -148,18 +155,19 @@
         chosen = lax.all_to_all(ordered, "pt", 0, 0, tiled=True)
         chosen, channel = lax.optimization_barrier((chosen, channel))
         chosen = chosen.astype(F32)
-        antisym = coupling - coupling.T
-        mixed = jnp.einsum("qr,qin->irn", antisym, chosen, precision=lax.Precision.HIGHEST)
+        mixed = jnp.einsum("qr,qin->irn", turned, chosen, precision=lax.Precision.HIGHEST)
         mixed = mixed.astype(BF).reshape(width, -1)
         linear = jnp.einsum("q,qin->in", weights, chosen, precision=lax.Precision.HIGHEST)
     with jax.named_scope("mixed_line"):
         line = jnp.concatenate(gather_line(mixed, along(True, False)), 0)
+        pair = jnp.stack([channel, send(channel, HALF)])
+    with jax.named_scope("mixed_plane"):
+        line, pair = lax.optimization_barrier((line, pair))
+        planes = gather_line(line, along(False, False))
     with jax.named_scope("points"):
-        every = lax.all_to_all(jnp.broadcast_to(channel, (8,) + channel.shape), "pt", 0, 0, tiled=True)
-    with jax.named_scope("mixed_plane"):
-        planes = gather_line(line, along(False, False))
+        left = gather_line(pair, CROSS)
     with jax.named_scope("product"):
-        total = product(every, planes)
+        total = product(left, planes)
     with jax.named_scope("output"):
         return linear + total[:width] + send(total[width:], CORE)
 

time: 169 us -> 151 us (0.89)
  the two profiles are of different devices: /device:TPU:67 before, /device:TPU:65 now
where the time goes in v8:
time: 151 us; the launch traced here: 150 us
  waiting for transfers between devices  65.7 us (44%)
  starting transfers between devices  44.3 us (29%)
  blocking collectives  15.2 us (10%)
  matrix products  11.7 us (8%)
  other arithmetic  8.44 us (6%)
  local copies, waits for them, and re-layouts  3.87 us (3%)
    ppermute x23, waiting for transfers between devices, send(): return lax.ppermute(value, AXES, perm)  54.8 us
    ppermute x23, starting transfers between devices, send(): return lax.ppermute(value, AXES, perm)  36.8 us
    all_to_all x1, blocking collectives, shards(): chosen = lax.all_to_all(ordered, 'pt', 0, 0, tiled=True)  15.2 us
    all_to_all x1, waiting for transfers between devices, shards(): lax.all_to_all(blocks, 'pan', 0, 0, axis_index_groups=CHIPS, tiled=True)  10.9 us
    dot_general x8, matrix products, nt(): lax.dot_general(a, b, (((1,), (1,)), ((), ())), preferred_element_type=F32)  9.73 us
    all_to_all x1, starting transfers between devices, shards(): lax.all_to_all(blocks, 'pan', 0, 0, axis_index_groups=CHIPS, tiled=True)  7.51 us
    select_n x1, other arithmetic, shards(): jnp.where(core == 0, jnp.concatenate([rows, other_rows], 0), jnp.concaten...  4.08 us
  transfers between devices with their start and end apart: 24, of which 18 were waited for; matrix products, arithmetic and copies ran while one was open for 10% of the time, Pallas kernels for 0%

profile of v8, /device:TPU:65, one launch (start us, length us, event | category | flops | bytes accessed | tf_op | source)
XLA Modules:
  0.0 150.4 jit_solution(11936756099405396791)
XLA Ops:
  0.7 2.7 %collective-permute-start = (bf16[40,6144]{1,0:T(8,128)(2,1)}, bf16[40,6144]{1,0:T(8,128)(2,1)S(1)}, u32[]{:S(2)}, u32[]{:S(2)}) collective-permute-start(bf16[40,6144]{1,0:T(8,128)(2,1)} %bitcast.104), channel_id=1, source_target_pairs={{0,38},{1,25},{2,0},{3,27},{4,2},{5,29},{6,4},{7,31},{32,6},{33,57... | collective-permute-start | bytes 1474568 | tf_op jit(solution)/shard_map/basis_line/ppermute | solution.py:46
  6.8 8.0 %collective-permute-done = bf16[40,6144]{1,0:T(8,128)(2,1)S(1)} collective-permute-done((bf16[40,6144]{1,0:T(8,128)(2,1)}, bf16[40,6144]{1,0:T(8,128)(2,1)S(1)}, u32[]{:S(2)}, u32[]{:S(2)}) %collective-permute-start) | collective-permute-done | bytes 491552 | tf_op jit(solution)/shard_map/basis_line/ppermute | solution.py:46
  14.8 3.3 %collective-permute-done.2 = bf16[40,6144]{1,0:T(8,128)(2,1)S(1)} collective-permute-done((bf16[40,6144]{1,0:T(8,128)(2,1)}, bf16[40,6144]{1,0:T(8,128)(2,1)S(1)}, u32[]{:S(2)}, u32[]{:S(2)}) %collective-permute-start.2) | collective-permute-done | bytes 491552 | tf_op jit(solution)/shard_map/basis_line/ppermute | solution.py:46
  19.3 4.3 %collective-permute-start.4 = (bf16[40,6144]{1,0:T(8,128)(2,1)S(1)}, bf16[40,6144]{1,0:T(8,128)(2,1)S(1)}, u32[]{:S(2)}, u32[]{:S(2)}) collective-permute-start(bf16[40,6144]{1,0:T(8,128)(2,1)S(1)} %dynamic-slice_bitcast_fusion), channel_id=1, source_target_pairs={{0,16},{1,5},{2,18},{3,39},{4,20},{5,33},{6,22},{7,3},{32,48},{33,... | collective-permute-start | bytes 1474568 | tf_op jit(solution)/shard_map/basis_plane/ppermute | solution.py:46
  23.6 4.1 %maximum_select_fusion = bf16[384,6144]{1,0:T(8,128)(2,1)S(1)} fusion(bf16[192,6144]{1,0:T(8,128)(2,1)} %collective-permute-done.3, bf16[192,6144]{1,0:T(8,128)(2,1)S(1)} %bitcast.90, pred[]{:T(512)S(6)} %eq.78), kind=kLoop, calls=%fused_computation.1 | loop fusion | flops 21233664 | bytes 9437185 | tf_op jit(solution)/shard_map/rows_pair/jit(_where)/select_n | solution.py:122
  27.7 1.7 %collective-permute-done.4 = bf16[40,6144]{1,0:T(8,128)(2,1)S(1)} collective-permute-done((bf16[40,6144]{1,0:T(8,128)(2,1)S(1)}, bf16[40,6144]{1,0:T(8,128)(2,1)S(1)}, u32[]{:S(2)}, u32[]{:S(2)}) %collective-permute-start.4) | collective-permute-done | bytes 491552 | tf_op jit(solution)/shard_map/basis_plane/ppermute | solution.py:46
  29.4 2.5 %collective-permute-start.6 = (bf16[40,6144]{1,0:T(8,128)(2,1)S(1)}, bf16[40,6144]{1,0:T(8,128)(2,1)S(1)}, u32[]{:S(2)}, u32[]{:S(2)}) collective-permute-start(bf16[40,6144]{1,0:T(8,128)(2,1)S(1)} %collective-permute-done.4), channel_id=1, source_target_pairs={{0,192},{1,193},{2,194},{3,195},{4,196},{5,197},{6,198},{7,199},{3... | collective-permute-start | bytes 1474568 | tf_op jit(solution)/shard_map/basis_plane/ppermute | solution.py:46
  31.9 1.7 %collective-permute-start.8 = (bf16[40,6144]{1,0:T(8,128)(2,1)S(1)}, bf16[40,6144]{1,0:T(8,128)(2,1)S(1)}, u32[]{:S(2)}, u32[]{:S(2)}) collective-permute-start(bf16[40,6144]{1,0:T(8,128)(2,1)S(1)} %collective-permute-done.4), channel_id=1, source_target_pairs={{0,128},{1,129},{2,130},{3,131},{4,132},{5,133},{6,134},{7,135},{3... | collective-permute-start | bytes 1474568 | tf_op jit(solution)/shard_map/basis_plane/ppermute | solution.py:46
  35.3 1.7 %convolution_convert_fusion.4 = bf16[160,384]{1,0:T(8,128)(2,1)S(1)} fusion(bf16[160,6144]{1,0:T(8,128)(2,1)S(1)} %pad_maximum_fusion, bf16[384,6144]{1,0:T(8,128)(2,1)S(1)} %maximum_select_fusion), kind=kOutput, calls=%fused_computation.15 | convolution fusion | flops 755036160 | bytes 6807552 | tf_op jit(solution)/shard_map/projected/dot_general | solution.py:57
  37.1 5.2 %collective-permute-done.6 = bf16[40,6144]{1,0:T(8,128)(2,1)S(1)} collective-permute-done((bf16[40,6144]{1,0:T(8,128)(2,1)S(1)}, bf16[40,6144]{1,0:T(8,128)(2,1)S(1)}, u32[]{:S(2)}, u32[]{:S(2)}) %collective-permute-start.6) | collective-permute-done | bytes 491552 | tf_op jit(solution)/shard_map/basis_plane/ppermute | solution.py:46
  42.4 3.2 %collective-permute-done.7 = bf16[40,6144]{1,0:T(8,128)(2,1)S(1)} collective-permute-done((bf16[40,6144]{1,0:T(8,128)(2,1)S(1)}, bf16[40,6144]{1,0:T(8,128)(2,1)S(1)}, u32[]{:S(2)}, u32[]{:S(2)}) %collective-permute-start.7) | collective-permute-done | bytes 491552 | tf_op jit(solution)/shard_map/basis_plane/ppermute | solution.py:46
  45.6 8.7 %collective-permute-done.8 = bf16[40,6144]{1,0:T(8,128)(2,1)S(1)} collective-permute-done((bf16[40,6144]{1,0:T(8,128)(2,1)S(1)}, bf16[40,6144]{1,0:T(8,128)(2,1)S(1)}, u32[]{:S(2)}, u32[]{:S(2)}) %collective-permute-start.8) | collective-permute-done | bytes 491552 | tf_op jit(solution)/shard_map/basis_plane/ppermute | solution.py:46
  54.3 1.6 %convolution_convert_fusion.2 = bf16[160,384]{1,0:T(8,128)(2,1)S(1)} fusion(bf16[160,6144]{1,0:T(8,128)(2,1)S(1)} %bitcast.87, bf16[384,6144]{1,0:T(8,128)(2,1)S(1)} %maximum_select_fusion), kind=kOutput, calls=%fused_computation.13 | convolution fusion | flops 755036160 | bytes 6807552 | tf_op jit(solution)/shard_map/projected/dot_general | solution.py:57
  62.2 7.5 %all-to-all-start = ((bf16[16,40,384]{2,1,0:T(8,128)(2,1)}), bf16[16,40,384]{2,1,0:T(8,128)(2,1)S(1)}, u32[]{:S(2)}, u32[]{:S(2)}) async-start(bf16[16,40,384]{2,1,0:T(8,128)(2,1)} %bitcast.21), calls=%async_computation | async-start | bytes 983040 | tf_op jit(solution)/shard_map/projected_exchange/all_to_all | solution.py:140
  69.8 10.9 %all-to-all-done = bf16[16,40,384]{2,1,0:T(8,128)(2,1)S(1)} async-done(((bf16[16,40,384]{2,1,0:T(8,128)(2,1)}), bf16[16,40,384]{2,1,0:T(8,128)(2,1)S(1)}, u32[]{:S(2)}, u32[]{:S(2)}) %all-to-all-start) | async-done | bytes 491552 | tf_op jit(solution)/shard_map/projected_exchange/all_to_all | solution.py:140
  80.7 3.6 %collective-permute-start.10 = (bf16[40,6144]{1,0:T(8,128)(2,1)S(1)}, bf16[40,6144]{1,0:T(8,128)(2,1)S(1)}, u32[]{:S(2)}, u32[]{:S(2)}) collective-permute-start(bf16[40,6144]{1,0:T(8,128)(2,1)S(1)} %bitcast.92), channel_id=1, source_target_pairs={{0,1},{1,0},{2,3},{3,2},{4,5},{5,4},{6,7},{7,6},{32,33},{33,32},{3... | collective-permute-start | bytes 1474568 | tf_op jit(solution)/shard_map/projected_exchange/ppermute | solution.py:46
  93.0 15.2 %all_to_all.10 = bf16[8,40,160]{2,1,0:T(8,128)(2,1)S(1)} all-to-all(bf16[8,40,160]{2,1,0:T(8,128)(2,1)S(1)} %bitcast.102), channel_id=1, replica_groups=mesh['pt'=8,'pan'=32] {'pt'}, dimensions={0} | all-to-all | bytes 204800 | tf_op jit(solution)/shard_map/columns_exchange/all_to_all | solution.py:155
  111.7 4.0 %collective-permute-done.15 = bf16[80,640]{1,0:T(8,128)(2,1)S(1)} collective-permute-done((bf16[80,640]{1,0:T(8,128)(2,1)S(1)}, bf16[80,640]{1,0:T(8,128)(2,1)S(1)}, u32[]{:S(2)}, u32[]{:S(2)}) %collective-permute-start.15) | collective-permute-done | bytes 102432 | tf_op jit(solution)/shard_map/mixed_line/ppermute | solution.py:46
  117.8 3.2 %collective-permute-start.19 = (bf16[160,1280]{1,0:T(8,128)(2,1)S(1)}, bf16[160,1280]{1,0:T(8,128)(2,1)S(1)}, u32[]{:S(2)}, u32[]{:S(2)}) collective-permute-start(bf16[160,1280]{1,0:T(8,128)(2,1)S(1)} %pad_maximum_fusion.1.m0), channel_id=1, source_target_pairs={{0,24},{1,7},{2,26},{3,1},{4,28},{5,3},{6,30},{7,5},{32,56},{33,39... | collective-permute-start | bytes 1228808 | tf_op jit(solution)/shard_map/mixed_plane/ppermute | solution.py:46
  123.5 4.9 %collective-permute-done.17.l2 = bf16[2,80,640]{2,1,0:T(8,128)(2,1)S(1)} collective-permute-done((bf16[2,80,640]{2,1,0:T(8,128)(2,1)S(1)}, bf16[2,80,640]{2,1,0:T(8,128)(2,1)S(1)}, u32[]{:S(2)}, u32[]{:S(2)}) %collective-permute-start.17) | collective-permute-done | bytes 204832 | tf_op jit(solution)/shard_map/points/ppermute | solution.py:46
  128.4 2.1 %collective-permute-done.18.l3 = bf16[2,80,640]{2,1,0:T(8,128)(2,1)S(1)} collective-permute-done((bf16[2,80,640]{2,1,0:T(8,128)(2,1)S(1)}, bf16[2,80,640]{2,1,0:T(8,128)(2,1)S(1)}, u32[]{:S(2)}, u32[]{:S(2)}) %collective-permute-start.18) | collective-permute-done | bytes 204832 | tf_op jit(solution)/shard_map/points/ppermute | solution.py:46
  130.5 4.2 %collective-permute-done.19.m1 = bf16[160,1280]{1,0:T(8,128)(2,1)S(1)} collective-permute-done((bf16[160,1280]{1,0:T(8,128)(2,1)S(1)}, bf16[160,1280]{1,0:T(8,128)(2,1)S(1)}, u32[]{:S(2)}, u32[]{:S(2)}) %collective-permute-start.19) | collective-permute-done | bytes 409632 | tf_op jit(solution)/shard_map/mixed_plane/ppermute | solution.py:46
  134.7 4.4 %collective-permute-done.20.m2 = bf16[160,1280]{1,0:T(8,128)(2,1)S(1)} collective-permute-done((bf16[160,1280]{1,0:T(8,128)(2,1)S(1)}, bf16[160,1280]{1,0:T(8,128)(2,1)S(1)}, u32[]{:S(2)}, u32[]{:S(2)}) %collective-permute-start.20) | collective-permute-done | bytes 409632 | tf_op jit(solution)/shard_map/mixed_plane/ppermute | solution.py:46
  140.5 8.4 %collective-permute-start.22 = (f32[40,160]{1,0:T(8,128)S(1)}, f32[40,160]{1,0:T(8,128)S(1)}, u32[]{:S(2)}, u32[]{:S(2)}) collective-permute-start(f32[40,160]{1,0:T(8,128)S(1)} %slice.21), channel_id=1, source_target_pairs={{0,1},{1,0},{2,3},{3,2},{4,5},{5,4},{6,7},{7,6},{32,33},{33,32},{3... | collective-permute-start | bytes 76808 | tf_op jit(solution)/shard_map/output/ppermute | solution.py:46
  (93 shorter events, 32.8 us)
Async XLA Ops:
  0.0 19.3 %collective-permute-start.3 = (bf16[192,6144]{1,0:T(8,128)(2,1)}, bf16[192,6144]{1,0:T(8,128)(2,1)}, u32[]{:S(2)}, u32[]{:S(2)}) collective-permute-start(bf16[192,6144]{1,0:T(8,128)(2,1)} %bitcast.89), channel_id=1, source_target_pairs={{0,1},{1,0},{2,3},{3,2},{4,5},{5,4},{6,7},{7,6},{32,33},{33,32},{3... | collective-permute-start | bytes 7077896 | tf_op jit(solution)/shard_map/rows_pair/ppermute | solution.py:46
  0.7 14.1 %collective-permute-start = (bf16[40,6144]{1,0:T(8,128)(2,1)}, bf16[40,6144]{1,0:T(8,128)(2,1)S(1)}, u32[]{:S(2)}, u32[]{:S(2)}) collective-permute-start(bf16[40,6144]{1,0:T(8,128)(2,1)} %bitcast.104), channel_id=1, source_target_pairs={{0,38},{1,25},{2,0},{3,27},{4,2},{5,29},{6,4},{7,31},{32,6},{33,57... | collective-permute-start | bytes 1474568 | tf_op jit(solution)/shard_map/basis_line/ppermute | solution.py:46
  3.4 11.4 %collective-permute-start.1 = (bf16[40,6144]{1,0:T(8,128)(2,1)}, bf16[40,6144]{1,0:T(8,128)(2,1)S(1)}, u32[]{:S(2)}, u32[]{:S(2)}) collective-permute-start(bf16[40,6144]{1,0:T(8,128)(2,1)} %bitcast.105), channel_id=1, source_target_pairs={{0,4},{1,17},{2,38},{3,19},{4,32},{5,21},{6,2},{7,23},{32,36},{33,... | collective-permute-start | bytes 1474568 | tf_op jit(solution)/shard_map/basis_line/ppermute | solution.py:46
  3.8 14.3 %collective-permute-start.2 = (bf16[40,6144]{1,0:T(8,128)(2,1)}, bf16[40,6144]{1,0:T(8,128)(2,1)S(1)}, u32[]{:S(2)}, u32[]{:S(2)}) collective-permute-start(bf16[40,6144]{1,0:T(8,128)(2,1)} %bitcast.106), channel_id=1, source_target_pairs={{0,2},{1,9},{2,4},{3,11},{4,6},{5,13},{6,32},{7,15},{32,34},{33,41... | collective-permute-start | bytes 1474568 | tf_op jit(solution)/shard_map/basis_line/ppermute | solution.py:46
  19.3 10.1 %collective-permute-start.4 = (bf16[40,6144]{1,0:T(8,128)(2,1)S(1)}, bf16[40,6144]{1,0:T(8,128)(2,1)S(1)}, u32[]{:S(2)}, u32[]{:S(2)}) collective-permute-start(bf16[40,6144]{1,0:T(8,128)(2,1)S(1)} %dynamic-slice_bitcast_fusion), channel_id=1, source_target_pairs={{0,16},{1,5},{2,18},{3,39},{4,20},{5,33},{6,22},{7,3},{32,48},{33,... | collective-permute-start | bytes 1474568 | tf_op jit(solution)/shard_map/basis_plane/ppermute | solution.py:46
  29.4 12.9 %collective-permute-start.6 = (bf16[40,6144]{1,0:T(8,128)(2,1)S(1)}, bf16[40,6144]{1,0:T(8,128)(2,1)S(1)}, u32[]{:S(2)}, u32[]{:S(2)}) collective-permute-start(bf16[40,6144]{1,0:T(8,128)(2,1)S(1)} %collective-permute-done.4), channel_id=1, source_target_pairs={{0,192},{1,193},{2,194},{3,195},{4,196},{5,197},{6,198},{7,199},{3... | collective-permute-start | bytes 1474568 | tf_op jit(solution)/shard_map/basis_plane/ppermute | solution.py:46
  31.9 13.7 %collective-permute-start.7 = (bf16[40,6144]{1,0:T(8,128)(2,1)S(1)}, bf16[40,6144]{1,0:T(8,128)(2,1)S(1)}, u32[]{:S(2)}, u32[]{:S(2)}) collective-permute-start(bf16[40,6144]{1,0:T(8,128)(2,1)S(1)} %collective-permute-done.4), channel_id=1, source_target_pairs={{0,64},{1,65},{2,66},{3,67},{4,68},{5,69},{6,70},{7,71},{32,96},{3... | collective-permute-start | bytes 1474568 | tf_op jit(solution)/shard_map/basis_plane/ppermute | solution.py:46
  31.9 22.4 %collective-permute-start.8 = (bf16[40,6144]{1,0:T(8,128)(2,1)S(1)}, bf16[40,6144]{1,0:T(8,128)(2,1)S(1)}, u32[]{:S(2)}, u32[]{:S(2)}) collective-permute-start(bf16[40,6144]{1,0:T(8,128)(2,1)S(1)} %collective-permute-done.4), channel_id=1, source_target_pairs={{0,128},{1,129},{2,130},{3,131},{4,132},{5,133},{6,134},{7,135},{3... | collective-permute-start | bytes 1474568 | tf_op jit(solution)/shard_map/basis_plane/ppermute | solution.py:46
  33.6 23.8 %collective-permute-start.5 = (bf16[160,6144]{1,0:T(8,128)(2,1)S(1)}, bf16[160,6144]{1,0:T(8,128)(2,1)S(1)}, u32[]{:S(2)}, u32[]{:S(2)}) collective-permute-start(bf16[160,6144]{1,0:T(8,128)(2,1)S(1)} %pad_maximum_fusion), channel_id=1, source_target_pairs={{0,24},{1,39},{2,26},{3,1},{4,28},{5,3},{6,30},{7,5},{32,56},{33,7... | collective-permute-start | bytes 5898248 | tf_op jit(solution)/shard_map/basis_plane/ppermute | solution.py:46
  34.4 24.8 %collective-permute-start.9 = (bf16[160,6144]{1,0:T(8,128)(2,1)S(1)}, bf16[160,6144]{1,0:T(8,128)(2,1)S(1)}, u32[]{:S(2)}, u32[]{:S(2)}) collective-permute-start(bf16[160,6144]{1,0:T(8,128)(2,1)S(1)} %pad_maximum_fusion), channel_id=1, source_target_pairs={{0,8},{1,3},{2,10},{3,5},{4,12},{5,7},{6,14},{7,33},{32,40},{33,35... | collective-permute-start | bytes 5898248 | tf_op jit(solution)/shard_map/basis_plane/ppermute | solution.py:46
  62.2 18.5 %all-to-all-start = ((bf16[16,40,384]{2,1,0:T(8,128)(2,1)}), bf16[16,40,384]{2,1,0:T(8,128)(2,1)S(1)}, u32[]{:S(2)}, u32[]{:S(2)}) async-start(bf16[16,40,384]{2,1,0:T(8,128)(2,1)} %bitcast.21), calls=%async_computation | async-start | bytes 983040 | tf_op jit(solution)/shard_map/projected_exchange/all_to_all | solution.py:140
  80.7 5.1 %collective-permute-start.10 = (bf16[40,6144]{1,0:T(8,128)(2,1)S(1)}, bf16[40,6144]{1,0:T(8,128)(2,1)S(1)}, u32[]{:S(2)}, u32[]{:S(2)}) collective-permute-start(bf16[40,6144]{1,0:T(8,128)(2,1)S(1)} %bitcast.92), channel_id=1, source_target_pairs={{0,1},{1,0},{2,3},{3,2},{4,5},{5,4},{6,7},{7,6},{32,33},{33,32},{3... | collective-permute-start | bytes 1474568 | tf_op jit(solution)/shard_map/projected_exchange/ppermute | solution.py:46
  90.7 1.3 collective-permute-start.11
  108.2 7.5 %collective-permute-start.15 = (bf16[80,640]{1,0:T(8,128)(2,1)S(1)}, bf16[80,640]{1,0:T(8,128)(2,1)S(1)}, u32[]{:S(2)}, u32[]{:S(2)}) collective-permute-start(bf16[80,640]{1,0:T(8,128)(2,1)S(1)} %pad_maximum_fusion.3), channel_id=1, source_target_pairs={{0,32},{1,33},{2,34},{3,35},{4,36},{5,37},{6,38},{7,39},{32,0},{33... | collective-permute-start | bytes 307208 | tf_op jit(solution)/shard_map/mixed_line/ppermute | solution.py:46
  109.5 6.3 %collective-permute-start.12 = (bf16[40,1280]{1,0:T(8,128)(2,1)S(1)}, bf16[40,1280]{1,0:T(8,128)(2,1)S(1)}, u32[]{:S(2)}, u32[]{:S(2)}) collective-permute-start(bf16[40,1280]{1,0:T(8,128)(2,1)S(1)} %reshape.271), channel_id=1, source_target_pairs={{0,6},{1,25},{2,0},{3,27},{4,2},{5,29},{6,4},{7,31},{32,38},{33,57... | collective-permute-start | bytes 307208 | tf_op jit(solution)/shard_map/mixed_line/ppermute | solution.py:46
  110.4 5.3 %collective-permute-start.13 = (bf16[40,1280]{1,0:T(8,128)(2,1)S(1)}, bf16[40,1280]{1,0:T(8,128)(2,1)S(1)}, u32[]{:S(2)}, u32[]{:S(2)}) collective-permute-start(bf16[40,1280]{1,0:T(8,128)(2,1)S(1)} %reshape.271), channel_id=1, source_target_pairs={{0,4},{1,17},{2,6},{3,19},{4,0},{5,21},{6,2},{7,23},{32,36},{33,49... | collective-permute-start | bytes 307208 | tf_op jit(solution)/shard_map/mixed_line/ppermute | solution.py:46
  111.7 4.9 %collective-permute-start.14 = (bf16[40,1280]{1,0:T(8,128)(2,1)S(1)}, bf16[40,1280]{1,0:T(8,128)(2,1)S(1)}, u32[]{:S(2)}, u32[]{:S(2)}) collective-permute-start(bf16[40,1280]{1,0:T(8,128)(2,1)S(1)} %reshape.271), channel_id=1, source_target_pairs={{0,2},{1,9},{2,4},{3,11},{4,6},{5,13},{6,0},{7,15},{32,34},{33,41}... | collective-permute-start | bytes 307208 | tf_op jit(solution)/shard_map/mixed_line/ppermute | solution.py:46
  116.6 7.0 %collective-permute-start.16 = (bf16[2,80,640]{2,1,0:T(8,128)(2,1)S(1)}, bf16[2,80,640]{2,1,0:T(8,128)(2,1)S(1)}, u32[]{:S(2)}, u32[]{:S(2)}) collective-permute-start(bf16[2,80,640]{2,1,0:T(8,128)(2,1)S(1)} %pad_maximum_fusion.2.l0), channel_id=1, source_target_pairs={{0,192},{1,193},{2,194},{3,195},{4,196},{5,197},{6,198},{7,199},{3... | collective-permute-start | bytes 614408 | tf_op jit(solution)/shard_map/points/ppermute | solution.py:46
  117.8 16.8 %collective-permute-start.19 = (bf16[160,1280]{1,0:T(8,128)(2,1)S(1)}, bf16[160,1280]{1,0:T(8,128)(2,1)S(1)}, u32[]{:S(2)}, u32[]{:S(2)}) collective-permute-start(bf16[160,1280]{1,0:T(8,128)(2,1)S(1)} %pad_maximum_fusion.1.m0), channel_id=1, source_target_pairs={{0,24},{1,7},{2,26},{3,1},{4,28},{5,3},{6,30},{7,5},{32,56},{33,39... | collective-permute-start | bytes 1228808 | tf_op jit(solution)/shard_map/mixed_plane/ppermute | solution.py:46
  121.0 18.1 %collective-permute-start.20 = (bf16[160,1280]{1,0:T(8,128)(2,1)S(1)}, bf16[160,1280]{1,0:T(8,128)(2,1)S(1)}, u32[]{:S(2)}, u32[]{:S(2)}) collective-permute-start(bf16[160,1280]{1,0:T(8,128)(2,1)S(1)} %pad_maximum_fusion.1.m0), channel_id=1, source_target_pairs={{0,16},{1,5},{2,18},{3,7},{4,20},{5,1},{6,22},{7,3},{32,48},{33,37... | collective-permute-start | bytes 1228808 | tf_op jit(solution)/shard_map/mixed_plane/ppermute | solution.py:46
  121.0 18.8 %collective-permute-start.21 = (bf16[160,1280]{1,0:T(8,128)(2,1)S(1)}, bf16[160,1280]{1,0:T(8,128)(2,1)S(1)}, u32[]{:S(2)}, u32[]{:S(2)}) collective-permute-start(bf16[160,1280]{1,0:T(8,128)(2,1)S(1)} %pad_maximum_fusion.1.m0), channel_id=1, source_target_pairs={{0,8},{1,3},{2,10},{3,5},{4,12},{5,7},{6,14},{7,1},{32,40},{33,35}... | collective-permute-start | bytes 1228808 | tf_op jit(solution)/shard_map/mixed_plane/ppermute | solution.py:46
  122.2 6.2 %collective-permute-start.17 = (bf16[2,80,640]{2,1,0:T(8,128)(2,1)S(1)}, bf16[2,80,640]{2,1,0:T(8,128)(2,1)S(1)}, u32[]{:S(2)}, u32[]{:S(2)}) collective-permute-start(bf16[2,80,640]{2,1,0:T(8,128)(2,1)S(1)} %pad_maximum_fusion.2.l0), channel_id=1, source_target_pairs={{0,128},{1,129},{2,130},{3,131},{4,132},{5,133},{6,134},{7,135},{3... | collective-permute-start | bytes 614408 | tf_op jit(solution)/shard_map/points/ppermute | solution.py:46
  123.5 7.0 %collective-permute-start.18 = (bf16[2,80,640]{2,1,0:T(8,128)(2,1)S(1)}, bf16[2,80,640]{2,1,0:T(8,128)(2,1)S(1)}, u32[]{:S(2)}, u32[]{:S(2)}) collective-permute-start(bf16[2,80,640]{2,1,0:T(8,128)(2,1)S(1)} %pad_maximum_fusion.2.l0), channel_id=1, source_target_pairs={{0,64},{1,65},{2,66},{3,67},{4,68},{5,69},{6,70},{7,71},{32,96},{3... | collective-permute-start | bytes 614408 | tf_op jit(solution)/shard_map/points/ppermute | solution.py:46
  140.5 9.2 %collective-permute-start.22 = (f32[40,160]{1,0:T(8,128)S(1)}, f32[40,160]{1,0:T(8,128)S(1)}, u32[]{:S(2)}, u32[]{:S(2)}) collective-permute-start(f32[40,160]{1,0:T(8,128)S(1)} %slice.21), channel_id=1, source_target_pairs={{0,1},{1,0},{2,3},{3,2},{4,5},{5,4},{6,7},{7,6},{32,33},{33,32},{3... | collective-permute-start | bytes 76808 | tf_op jit(solution)/shard_map/output/ppermute | solution.py:46
  (8 other events, 176.0 us)

commit v9 on v8

--- a/solution.py
+++ b/solution.py
@@ -38,6 +38,12 @@
 TWO = lambda v: 2 if v % 2 == 0 else -2
 CROSS = lambda step: pairs(lambda x, y, z, c: (x + step(x), y, z, c))
 CORE = pairs(lambda x, y, z, c: (x, y, z, 1 - c))
+def far(x, y, z, c):
+    back = lambda v: v + (0, -1, TWO(v), 1)[x]
+    return (x, y + TWO(y), back(z), c) if c == 0 else (x, back(y), z + TWO(z), c)
+
+
+FAR = pairs(far)
 HALF = pairs(lambda x, y, z, c: (x, y, z + 4, c))
 CHIPS = [[2 * chip + core for chip in range(16)] for core in range(2)]
 
@@ -118,15 +124,15 @@
     with jax.named_scope("basis_line"):
         line = jnp.concatenate(gather_line(panel, along(True, True)), 0)
     with jax.named_scope("rows_pair"):
-        line, other_rows, turned = lax.optimization_barrier((line, send(rows, CORE), turned))
+        line, fetched, other_rows, turned = lax.optimization_barrier(
+            (line, send(panel, FAR), send(rows, CORE), turned)
+        )
         chip_rows = jnp.where(
             core == 0, jnp.concatenate([rows, other_rows], 0), jnp.concatenate([other_rows, rows], 0)
         )
         chip_rows = lax.optimization_barrier(chip_rows)
     with jax.named_scope("basis_plane"):
         plane = along(False, True)
-        fetched = lax.dynamic_index_in_dim(line.reshape(4, width, depth), x, 0, keepdims=False)
-        fetched, line = lax.optimization_barrier((send(fetched, plane(TWO)), line))
         two = jnp.zeros((4, width, depth), BF)
         for step, perm in ((0, None), (1, CROSS(DOWN)), (3, CROSS(UP)), (2, CROSS(TWO))):
             piece = fetched if perm is None else send(fetched, perm)
@@ -159,10 +165,11 @@
         mixed = mixed.astype(BF).reshape(width, -1)
         linear = jnp.einsum("q,qin->in", weights, chosen, precision=lax.Precision.HIGHEST)
     with jax.named_scope("mixed_line"):
-        line = jnp.concatenate(gather_line(mixed, along(True, False)), 0)
+        pieces = list(gather_line(mixed, along(True, False)))
+        channel, pieces[1] = lax.optimization_barrier((channel, pieces[1]))
         pair = jnp.stack([channel, send(channel, HALF)])
+        line = jnp.concatenate(pieces, 0)
     with jax.named_scope("mixed_plane"):
-        line, pair = lax.optimization_barrier((line, pair))
         planes = gather_line(line, along(False, False))
     with jax.named_scope("points"):
         left = gather_line(pair, CROSS)

time: 151 us -> 149 us (0.987)
  the two profiles are of different devices: /device:TPU:65 before, /device:TPU:1 now
where the time goes in v9:
time: 149 us
  waiting for transfers between devices  71.4 us (48%)
  starting transfers between devices  38.3 us (26%)
  blocking collectives  13.9 us (9%)
  matrix products  11.7 us (8%)
  other arithmetic  8.55 us (6%)
  local copies, waits for them, and re-layouts  3.87 us (3%)
    ppermute x23, waiting for transfers between devices, send(): return lax.ppermute(value, AXES, perm)  57.7 us
    ppermute x23, starting transfers between devices, send(): return lax.ppermute(value, AXES, perm)  34.7 us
    all_to_all x1, blocking collectives, shards(): chosen = lax.all_to_all(ordered, 'pt', 0, 0, tiled=True)  13.9 us
    all_to_all x1, waiting for transfers between devices, shards(): lax.all_to_all(blocks, 'pan', 0, 0, axis_index_groups=CHIPS, tiled=True)  13.8 us
    dot_general x8, matrix products, nt(): lax.dot_general(a, b, (((1,), (1,)), ((), ())), preferred_element_type=F32)  9.74 us
    select_n x1, other arithmetic, shards(): jnp.where(core == 0, jnp.concatenate([rows, other_rows], 0), jnp.concaten...  4.07 us
    all_to_all x1, starting transfers between devices, shards(): lax.all_to_all(blocks, 'pan', 0, 0, axis_index_groups=CHIPS, tiled=True)  3.57 us
  transfers between devices with their start and end apart: 24, of which 16 were waited for; matrix products, arithmetic and copies ran while one was open for 10% of the time, Pallas kernels for 0%

profile of v9, /device:TPU:1, one launch (start us, length us, event | category | flops | bytes accessed | tf_op | source)
XLA Modules:
  0.0 149.0 jit_solution(12526169336622683132)
XLA Ops:
  0.0 3.2 %collective-permute-start.4 = (bf16[192,6144]{1,0:T(8,128)(2,1)}, bf16[192,6144]{1,0:T(8,128)(2,1)}, u32[]{:S(2)}, u32[]{:S(2)}) collective-permute-start(bf16[192,6144]{1,0:T(8,128)(2,1)} %bitcast.85), channel_id=1, source_target_pairs={{0,1},{1,0},{2,3},{3,2},{4,5},{5,4},{6,7},{7,6},{32,33},{33,32},{3... | collective-permute-start | bytes 7077896 | tf_op jit(solution)/shard_map/rows_pair/ppermute | solution.py:52
  5.3 3.0 %collective-permute-start.3 = (bf16[40,6144]{1,0:T(8,128)(2,1)}, bf16[40,6144]{1,0:T(8,128)(2,1)S(1)}, u32[]{:S(2)}, u32[]{:S(2)}) collective-permute-start(bf16[40,6144]{1,0:T(8,128)(2,1)} %bitcast.103), channel_id=1, source_target_pairs={{0,16},{1,5},{2,18},{3,39},{4,20},{5,33},{6,22},{7,3},{32,48},{33,... | collective-permute-start | bytes 1474568 | tf_op jit(solution)/shard_map/rows_pair/ppermute | solution.py:52
  11.4 2.5 %collective-permute-done.1 = bf16[40,6144]{1,0:T(8,128)(2,1)S(1)} collective-permute-done((bf16[40,6144]{1,0:T(8,128)(2,1)}, bf16[40,6144]{1,0:T(8,128)(2,1)S(1)}, u32[]{:S(2)}, u32[]{:S(2)}) %collective-permute-start.1) | collective-permute-done | bytes 491552 | tf_op jit(solution)/shard_map/basis_line/ppermute | solution.py:52
  14.0 9.7 %collective-permute-done.2 = bf16[40,6144]{1,0:T(8,128)(2,1)} collective-permute-done((bf16[40,6144]{1,0:T(8,128)(2,1)}, bf16[40,6144]{1,0:T(8,128)(2,1)}, u32[]{:S(2)}, u32[]{:S(2)}) %collective-permute-start.2) | collective-permute-done | bytes 491552 | tf_op jit(solution)/shard_map/basis_line/ppermute | solution.py:52
  25.0 3.5 %collective-permute-start.6 = (bf16[40,6144]{1,0:T(8,128)(2,1)S(1)}, bf16[40,6144]{1,0:T(8,128)(2,1)S(1)}, u32[]{:S(2)}, u32[]{:S(2)}) collective-permute-start(bf16[40,6144]{1,0:T(8,128)(2,1)S(1)} %collective-permute-done.3), channel_id=1, source_target_pairs={{0,192},{1,193},{2,194},{3,195},{4,196},{5,197},{6,198},{7,199},{3... | collective-permute-start | bytes 1474568 | tf_op jit(solution)/shard_map/basis_plane/ppermute | solution.py:52
  28.5 1.7 %collective-permute-start.8 = (bf16[40,6144]{1,0:T(8,128)(2,1)S(1)}, bf16[40,6144]{1,0:T(8,128)(2,1)S(1)}, u32[]{:S(2)}, u32[]{:S(2)}) collective-permute-start(bf16[40,6144]{1,0:T(8,128)(2,1)S(1)} %collective-permute-done.3), channel_id=1, source_target_pairs={{0,128},{1,129},{2,130},{3,131},{4,132},{5,133},{6,134},{7,135},{3... | collective-permute-start | bytes 1474568 | tf_op jit(solution)/shard_map/basis_plane/ppermute | solution.py:52
  30.2 10.5 %collective-permute-start.5 = (bf16[160,6144]{1,0:T(8,128)(2,1)S(1)}, bf16[160,6144]{1,0:T(8,128)(2,1)S(1)}, u32[]{:S(2)}, u32[]{:S(2)}) collective-permute-start(bf16[160,6144]{1,0:T(8,128)(2,1)S(1)} %pad_maximum_fusion), channel_id=1, source_target_pairs={{0,24},{1,39},{2,26},{3,1},{4,28},{5,3},{6,30},{7,5},{32,56},{33,7... | collective-permute-start | bytes 5898248 | tf_op jit(solution)/shard_map/basis_plane/ppermute | solution.py:52
  40.8 4.1 %maximum_select_fusion = bf16[384,6144]{1,0:T(8,128)(2,1)S(1)} fusion(bf16[192,6144]{1,0:T(8,128)(2,1)} %collective-permute-done.4, bf16[192,6144]{1,0:T(8,128)(2,1)S(1)} %bitcast.86, pred[]{:T(512)S(6)} %eq.78), kind=kLoop, calls=%fused_computation.1 | loop fusion | flops 21233664 | bytes 9437185 | tf_op jit(solution)/shard_map/rows_pair/jit(_where)/select_n | solution.py:130
  45.1 1.7 %convolution_convert_fusion.4 = bf16[160,384]{1,0:T(8,128)(2,1)S(1)} fusion(bf16[160,6144]{1,0:T(8,128)(2,1)S(1)} %pad_maximum_fusion, bf16[384,6144]{1,0:T(8,128)(2,1)S(1)} %maximum_select_fusion), kind=kOutput, calls=%fused_computation.15 | convolution fusion | flops 755036160 | bytes 6807552 | tf_op jit(solution)/shard_map/projected/dot_general | solution.py:63
  47.1 1.6 %convolution_convert_fusion.2 = bf16[160,384]{1,0:T(8,128)(2,1)S(1)} fusion(bf16[160,6144]{1,0:T(8,128)(2,1)S(1)} %bitcast.83, bf16[384,6144]{1,0:T(8,128)(2,1)S(1)} %maximum_select_fusion), kind=kOutput, calls=%fused_computation.13 | convolution fusion | flops 755036160 | bytes 6807552 | tf_op jit(solution)/shard_map/projected/dot_general | solution.py:63
  48.7 13.6 %collective-permute-done.5 = bf16[160,6144]{1,0:T(8,128)(2,1)S(1)} collective-permute-done((bf16[160,6144]{1,0:T(8,128)(2,1)S(1)}, bf16[160,6144]{1,0:T(8,128)(2,1)S(1)}, u32[]{:S(2)}, u32[]{:S(2)}) %collective-permute-start.5) | collective-permute-done | bytes 1966112 | tf_op jit(solution)/shard_map/basis_plane/ppermute | solution.py:52
  62.4 1.6 %convolution_convert_fusion.3 = bf16[160,384]{1,0:T(8,128)(2,1)S(1)} fusion(bf16[160,6144]{1,0:T(8,128)(2,1)S(1)} %collective-permute-done.5, bf16[384,6144]{1,0:T(8,128)(2,1)S(1)} %maximum_select_fusion), kind=kOutput, calls=%fused_computation.14 | convolution fusion | flops 755036160 | bytes 6807552 | tf_op jit(solution)/shard_map/projected/dot_general | solution.py:63
  64.2 1.6 %collective-permute-done.9 = bf16[160,6144]{1,0:T(8,128)(2,1)S(1)} collective-permute-done((bf16[160,6144]{1,0:T(8,128)(2,1)S(1)}, bf16[160,6144]{1,0:T(8,128)(2,1)S(1)}, u32[]{:S(2)}, u32[]{:S(2)}) %collective-permute-start.9) | collective-permute-done | bytes 1966112 | tf_op jit(solution)/shard_map/basis_plane/ppermute | solution.py:52
  65.8 1.6 %convolution_convert_fusion.1 = bf16[160,384]{1,0:T(8,128)(2,1)S(1)} fusion(bf16[160,6144]{1,0:T(8,128)(2,1)S(1)} %collective-permute-done.9, bf16[384,6144]{1,0:T(8,128)(2,1)S(1)} %maximum_select_fusion), kind=kOutput, calls=%fused_computation.12 | convolution fusion | flops 755036160 | bytes 6807552 | tf_op jit(solution)/shard_map/projected/dot_general | solution.py:63
  68.7 3.6 %all-to-all-start = ((bf16[16,40,384]{2,1,0:T(8,128)(2,1)}), bf16[16,40,384]{2,1,0:T(8,128)(2,1)S(1)}, u32[]{:S(2)}, u32[]{:S(2)}) async-start(bf16[16,40,384]{2,1,0:T(8,128)(2,1)} %bitcast.19), calls=%async_computation | async-start | bytes 983040 | tf_op jit(solution)/shard_map/projected_exchange/all_to_all | solution.py:146
  72.4 13.8 %all-to-all-done = bf16[16,40,384]{2,1,0:T(8,128)(2,1)S(1)} async-done(((bf16[16,40,384]{2,1,0:T(8,128)(2,1)}), bf16[16,40,384]{2,1,0:T(8,128)(2,1)S(1)}, u32[]{:S(2)}, u32[]{:S(2)}) %all-to-all-start) | async-done | bytes 491552 | tf_op jit(solution)/shard_map/projected_exchange/all_to_all | solution.py:146
  86.3 2.9 %collective-permute-start.10 = (bf16[40,6144]{1,0:T(8,128)(2,1)S(1)}, bf16[40,6144]{1,0:T(8,128)(2,1)S(1)}, u32[]{:S(2)}, u32[]{:S(2)}) collective-permute-start(bf16[40,6144]{1,0:T(8,128)(2,1)S(1)} %bitcast.88), channel_id=1, source_target_pairs={{0,1},{1,0},{2,3},{3,2},{4,5},{5,4},{6,7},{7,6},{32,33},{33,32},{3... | collective-permute-start | bytes 1474568 | tf_op jit(solution)/shard_map/projected_exchange/ppermute | solution.py:52
  97.8 13.9 %all_to_all.10 = bf16[8,40,160]{2,1,0:T(8,128)(2,1)S(1)} all-to-all(bf16[8,40,160]{2,1,0:T(8,128)(2,1)S(1)} %bitcast.98), channel_id=1, replica_groups=mesh['pt'=8,'pan'=32] {'pt'}, dimensions={0} | all-to-all | bytes 204800 | tf_op jit(solution)/shard_map/columns_exchange/all_to_all | solution.py:161
  113.9 1.9 %collective-permute-done.12 = bf16[40,1280]{1,0:T(8,128)(2,1)S(1)} collective-permute-done((bf16[40,1280]{1,0:T(8,128)(2,1)S(1)}, bf16[40,1280]{1,0:T(8,128)(2,1)S(1)}, u32[]{:S(2)}, u32[]{:S(2)}) %collective-permute-start.12) | collective-permute-done | bytes 102432 | tf_op jit(solution)/shard_map/mixed_line/ppermute | solution.py:52
  118.1 5.5 %collective-permute-done.13 = bf16[80,640]{1,0:T(8,128)(2,1)S(1)} collective-permute-done((bf16[80,640]{1,0:T(8,128)(2,1)S(1)}, bf16[80,640]{1,0:T(8,128)(2,1)S(1)}, u32[]{:S(2)}, u32[]{:S(2)}) %collective-permute-start.13) | collective-permute-done | bytes 102432 | tf_op jit(solution)/shard_map/mixed_line/ppermute | solution.py:52
  124.8 2.2 %collective-permute-start.20 = (bf16[160,1280]{1,0:T(8,128)(2,1)S(1)}, bf16[160,1280]{1,0:T(8,128)(2,1)S(1)}, u32[]{:S(2)}, u32[]{:S(2)}) collective-permute-start(bf16[160,1280]{1,0:T(8,128)(2,1)S(1)} %constant_dynamic-update-slice_fusion.2.m0), channel_id=1, source_target_pairs={{0,16},{1,5},{2,18},{3,7},{4,20},{5,1},{6,22},{7,3},{32,48},{33,37... | collective-permute-start | bytes 1228808 | tf_op jit(solution)/shard_map/mixed_plane/ppermute | solution.py:52
  129.0 4.2 %collective-permute-done.15.l2 = bf16[2,80,640]{2,1,0:T(8,128)(2,1)S(1)} collective-permute-done((bf16[2,80,640]{2,1,0:T(8,128)(2,1)S(1)}, bf16[2,80,640]{2,1,0:T(8,128)(2,1)S(1)}, u32[]{:S(2)}, u32[]{:S(2)}) %collective-permute-start.15) | collective-permute-done | bytes 204832 | tf_op jit(solution)/shard_map/points/ppermute | solution.py:52
  133.2 2.1 %collective-permute-done.16.l3 = bf16[2,80,640]{2,1,0:T(8,128)(2,1)S(1)} collective-permute-done((bf16[2,80,640]{2,1,0:T(8,128)(2,1)S(1)}, bf16[2,80,640]{2,1,0:T(8,128)(2,1)S(1)}, u32[]{:S(2)}, u32[]{:S(2)}) %collective-permute-start.16) | collective-permute-done | bytes 204832 | tf_op jit(solution)/shard_map/points/ppermute | solution.py:52
  135.3 11.0 %collective-permute-done.20.m2 = bf16[160,1280]{1,0:T(8,128)(2,1)S(1)} collective-permute-done((bf16[160,1280]{1,0:T(8,128)(2,1)S(1)}, bf16[160,1280]{1,0:T(8,128)(2,1)S(1)}, u32[]{:S(2)}, u32[]{:S(2)}) %collective-permute-start.20) | collective-permute-done | bytes 409632 | tf_op jit(solution)/shard_map/mixed_plane/ppermute | solution.py:52
  (95 shorter events, 27.2 us)
Async XLA Ops:
  0.0 25.0 %collective-permute-start.4 = (bf16[192,6144]{1,0:T(8,128)(2,1)}, bf16[192,6144]{1,0:T(8,128)(2,1)}, u32[]{:S(2)}, u32[]{:S(2)}) collective-permute-start(bf16[192,6144]{1,0:T(8,128)(2,1)} %bitcast.85), channel_id=1, source_target_pairs={{0,1},{1,0},{2,3},{3,2},{4,5},{5,4},{6,7},{7,6},{32,33},{33,32},{3... | collective-permute-start | bytes 7077896 | tf_op jit(solution)/shard_map/rows_pair/ppermute | solution.py:52
  3.2 8.2 %collective-permute-start = (bf16[40,6144]{1,0:T(8,128)(2,1)}, bf16[40,6144]{1,0:T(8,128)(2,1)S(1)}, u32[]{:S(2)}, u32[]{:S(2)}) collective-permute-start(bf16[40,6144]{1,0:T(8,128)(2,1)} %bitcast.100), channel_id=1, source_target_pairs={{0,38},{1,25},{2,0},{3,27},{4,2},{5,29},{6,4},{7,31},{32,6},{33,57... | collective-permute-start | bytes 1474568 | tf_op jit(solution)/shard_map/basis_line/ppermute | solution.py:52
  4.2 9.7 %collective-permute-start.1 = (bf16[40,6144]{1,0:T(8,128)(2,1)}, bf16[40,6144]{1,0:T(8,128)(2,1)S(1)}, u32[]{:S(2)}, u32[]{:S(2)}) collective-permute-start(bf16[40,6144]{1,0:T(8,128)(2,1)} %bitcast.101), channel_id=1, source_target_pairs={{0,4},{1,17},{2,38},{3,19},{4,32},{5,21},{6,2},{7,23},{32,36},{33,... | collective-permute-start | bytes 1474568 | tf_op jit(solution)/shard_map/basis_line/ppermute | solution.py:52
  4.6 19.0 %collective-permute-start.2 = (bf16[40,6144]{1,0:T(8,128)(2,1)}, bf16[40,6144]{1,0:T(8,128)(2,1)}, u32[]{:S(2)}, u32[]{:S(2)}) collective-permute-start(bf16[40,6144]{1,0:T(8,128)(2,1)} %bitcast.102), channel_id=1, source_target_pairs={{0,2},{1,9},{2,4},{3,11},{4,6},{5,13},{6,32},{7,15},{32,34},{33,41... | collective-permute-start | bytes 1474568 | tf_op jit(solution)/shard_map/basis_line/ppermute | solution.py:52
  5.3 19.7 %collective-permute-start.3 = (bf16[40,6144]{1,0:T(8,128)(2,1)}, bf16[40,6144]{1,0:T(8,128)(2,1)S(1)}, u32[]{:S(2)}, u32[]{:S(2)}) collective-permute-start(bf16[40,6144]{1,0:T(8,128)(2,1)} %bitcast.103), channel_id=1, source_target_pairs={{0,16},{1,5},{2,18},{3,39},{4,20},{5,33},{6,22},{7,3},{32,48},{33,... | collective-permute-start | bytes 1474568 | tf_op jit(solution)/shard_map/rows_pair/ppermute | solution.py:52
  25.0 21.9 %collective-permute-start.6 = (bf16[40,6144]{1,0:T(8,128)(2,1)S(1)}, bf16[40,6144]{1,0:T(8,128)(2,1)S(1)}, u32[]{:S(2)}, u32[]{:S(2)}) collective-permute-start(bf16[40,6144]{1,0:T(8,128)(2,1)S(1)} %collective-permute-done.3), channel_id=1, source_target_pairs={{0,192},{1,193},{2,194},{3,195},{4,196},{5,197},{6,198},{7,199},{3... | collective-permute-start | bytes 1474568 | tf_op jit(solution)/shard_map/basis_plane/ppermute | solution.py:52
  28.5 18.5 %collective-permute-start.7 = (bf16[40,6144]{1,0:T(8,128)(2,1)S(1)}, bf16[40,6144]{1,0:T(8,128)(2,1)S(1)}, u32[]{:S(2)}, u32[]{:S(2)}) collective-permute-start(bf16[40,6144]{1,0:T(8,128)(2,1)S(1)} %collective-permute-done.3), channel_id=1, source_target_pairs={{0,64},{1,65},{2,66},{3,67},{4,68},{5,69},{6,70},{7,71},{32,96},{3... | collective-permute-start | bytes 1474568 | tf_op jit(solution)/shard_map/basis_plane/ppermute | solution.py:52
  28.5 18.5 %collective-permute-start.8 = (bf16[40,6144]{1,0:T(8,128)(2,1)S(1)}, bf16[40,6144]{1,0:T(8,128)(2,1)S(1)}, u32[]{:S(2)}, u32[]{:S(2)}) collective-permute-start(bf16[40,6144]{1,0:T(8,128)(2,1)S(1)} %collective-permute-done.3), channel_id=1, source_target_pairs={{0,128},{1,129},{2,130},{3,131},{4,132},{5,133},{6,134},{7,135},{3... | collective-permute-start | bytes 1474568 | tf_op jit(solution)/shard_map/basis_plane/ppermute | solution.py:52
  30.2 32.1 %collective-permute-start.5 = (bf16[160,6144]{1,0:T(8,128)(2,1)S(1)}, bf16[160,6144]{1,0:T(8,128)(2,1)S(1)}, u32[]{:S(2)}, u32[]{:S(2)}) collective-permute-start(bf16[160,6144]{1,0:T(8,128)(2,1)S(1)} %pad_maximum_fusion), channel_id=1, source_target_pairs={{0,24},{1,39},{2,26},{3,1},{4,28},{5,3},{6,30},{7,5},{32,56},{33,7... | collective-permute-start | bytes 5898248 | tf_op jit(solution)/shard_map/basis_plane/ppermute | solution.py:52
  40.8 25.0 %collective-permute-start.9 = (bf16[160,6144]{1,0:T(8,128)(2,1)S(1)}, bf16[160,6144]{1,0:T(8,128)(2,1)S(1)}, u32[]{:S(2)}, u32[]{:S(2)}) collective-permute-start(bf16[160,6144]{1,0:T(8,128)(2,1)S(1)} %pad_maximum_fusion), channel_id=1, source_target_pairs={{0,8},{1,3},{2,10},{3,5},{4,12},{5,7},{6,14},{7,33},{32,40},{33,35... | collective-permute-start | bytes 5898248 | tf_op jit(solution)/shard_map/basis_plane/ppermute | solution.py:52
  68.7 17.5 %all-to-all-start = ((bf16[16,40,384]{2,1,0:T(8,128)(2,1)}), bf16[16,40,384]{2,1,0:T(8,128)(2,1)S(1)}, u32[]{:S(2)}, u32[]{:S(2)}) async-start(bf16[16,40,384]{2,1,0:T(8,128)(2,1)} %bitcast.19), calls=%async_computation | async-start | bytes 983040 | tf_op jit(solution)/shard_map/projected_exchange/all_to_all | solution.py:146
  86.3 4.4 %collective-permute-start.10 = (bf16[40,6144]{1,0:T(8,128)(2,1)S(1)}, bf16[40,6144]{1,0:T(8,128)(2,1)S(1)}, u32[]{:S(2)}, u32[]{:S(2)}) collective-permute-start(bf16[40,6144]{1,0:T(8,128)(2,1)S(1)} %bitcast.88), channel_id=1, source_target_pairs={{0,1},{1,0},{2,3},{3,2},{4,5},{5,4},{6,7},{7,6},{32,33},{33,32},{3... | collective-permute-start | bytes 1474568 | tf_op jit(solution)/shard_map/projected_exchange/ppermute | solution.py:52
  95.5 1.3 collective-permute-start.11
  112.2 3.6 %collective-permute-start.12 = (bf16[40,1280]{1,0:T(8,128)(2,1)S(1)}, bf16[40,1280]{1,0:T(8,128)(2,1)S(1)}, u32[]{:S(2)}, u32[]{:S(2)}) collective-permute-start(bf16[40,1280]{1,0:T(8,128)(2,1)S(1)} %reshape.267), channel_id=1, source_target_pairs={{0,6},{1,25},{2,0},{3,27},{4,2},{5,29},{6,4},{7,31},{32,38},{33,57... | collective-permute-start | bytes 307208 | tf_op jit(solution)/shard_map/mixed_line/ppermute | solution.py:52
  112.9 5.2 %collective-permute-start.17 = (bf16[40,1280]{1,0:T(8,128)(2,1)S(1)}, bf16[40,1280]{1,0:T(8,128)(2,1)S(1)}, u32[]{:S(2)}, u32[]{:S(2)}) collective-permute-start(bf16[40,1280]{1,0:T(8,128)(2,1)S(1)} %reshape.267), channel_id=1, source_target_pairs={{0,4},{1,17},{2,6},{3,19},{4,0},{5,21},{6,2},{7,23},{32,36},{33,49... | collective-permute-start | bytes 307208 | tf_op jit(solution)/shard_map/mixed_line/ppermute | solution.py:52
  113.2 11.4 %collective-permute-start.18 = (bf16[40,1280]{1,0:T(8,128)(2,1)S(1)}, bf16[40,1280]{1,0:T(8,128)(2,1)S(1)}, u32[]{:S(2)}, u32[]{:S(2)}) collective-permute-start(bf16[40,1280]{1,0:T(8,128)(2,1)S(1)} %reshape.267), channel_id=1, source_target_pairs={{0,2},{1,9},{2,4},{3,11},{4,6},{5,13},{6,0},{7,15},{32,34},{33,41}... | collective-permute-start | bytes 307208 | tf_op jit(solution)/shard_map/mixed_line/ppermute | solution.py:52
  115.8 7.9 %collective-permute-start.13 = (bf16[80,640]{1,0:T(8,128)(2,1)S(1)}, bf16[80,640]{1,0:T(8,128)(2,1)S(1)}, u32[]{:S(2)}, u32[]{:S(2)}) collective-permute-start(bf16[80,640]{1,0:T(8,128)(2,1)S(1)} %pad_maximum_fusion.2), channel_id=1, source_target_pairs={{0,32},{1,33},{2,34},{3,35},{4,36},{5,37},{6,38},{7,39},{32,0},{33... | collective-permute-start | bytes 307208 | tf_op jit(solution)/shard_map/mixed_line/ppermute | solution.py:52
  123.7 5.0 %collective-permute-start.14 = (bf16[2,80,640]{2,1,0:T(8,128)(2,1)S(1)}, bf16[2,80,640]{2,1,0:T(8,128)(2,1)S(1)}, u32[]{:S(2)}, u32[]{:S(2)}) collective-permute-start(bf16[2,80,640]{2,1,0:T(8,128)(2,1)S(1)} %pad_maximum_fusion.1.l0), channel_id=1, source_target_pairs={{0,192},{1,193},{2,194},{3,195},{4,196},{5,197},{6,198},{7,199},{3... | collective-permute-start | bytes 614408 | tf_op jit(solution)/shard_map/points/ppermute | solution.py:52
  124.7 10.6 %collective-permute-start.19 = (bf16[160,1280]{1,0:T(8,128)(2,1)S(1)}, bf16[160,1280]{1,0:T(8,128)(2,1)S(1)}, u32[]{:S(2)}, u32[]{:S(2)}) collective-permute-start(bf16[160,1280]{1,0:T(8,128)(2,1)S(1)} %constant_dynamic-update-slice_fusion.2.m0), channel_id=1, source_target_pairs={{0,24},{1,7},{2,26},{3,1},{4,28},{5,3},{6,30},{7,5},{32,56},{33,39... | collective-permute-start | bytes 1228808 | tf_op jit(solution)/shard_map/mixed_plane/ppermute | solution.py:52
  124.8 21.5 %collective-permute-start.20 = (bf16[160,1280]{1,0:T(8,128)(2,1)S(1)}, bf16[160,1280]{1,0:T(8,128)(2,1)S(1)}, u32[]{:S(2)}, u32[]{:S(2)}) collective-permute-start(bf16[160,1280]{1,0:T(8,128)(2,1)S(1)} %constant_dynamic-update-slice_fusion.2.m0), channel_id=1, source_target_pairs={{0,16},{1,5},{2,18},{3,7},{4,20},{5,1},{6,22},{7,3},{32,48},{33,37... | collective-permute-start | bytes 1228808 | tf_op jit(solution)/shard_map/mixed_plane/ppermute | solution.py:52
  127.0 19.4 %collective-permute-start.21 = (bf16[160,1280]{1,0:T(8,128)(2,1)S(1)}, bf16[160,1280]{1,0:T(8,128)(2,1)S(1)}, u32[]{:S(2)}, u32[]{:S(2)}) collective-permute-start(bf16[160,1280]{1,0:T(8,128)(2,1)S(1)} %constant_dynamic-update-slice_fusion.2.m0), channel_id=1, source_target_pairs={{0,8},{1,3},{2,10},{3,5},{4,12},{5,7},{6,14},{7,1},{32,40},{33,35}... | collective-permute-start | bytes 1228808 | tf_op jit(solution)/shard_map/mixed_plane/ppermute | solution.py:52
  127.0 6.2 %collective-permute-start.15 = (bf16[2,80,640]{2,1,0:T(8,128)(2,1)S(1)}, bf16[2,80,640]{2,1,0:T(8,128)(2,1)S(1)}, u32[]{:S(2)}, u32[]{:S(2)}) collective-permute-start(bf16[2,80,640]{2,1,0:T(8,128)(2,1)S(1)} %pad_maximum_fusion.1.l0), channel_id=1, source_target_pairs={{0,128},{1,129},{2,130},{3,131},{4,132},{5,133},{6,134},{7,135},{3... | collective-permute-start | bytes 614408 | tf_op jit(solution)/shard_map/points/ppermute | solution.py:52
  128.7 6.6 %collective-permute-start.16 = (bf16[2,80,640]{2,1,0:T(8,128)(2,1)S(1)}, bf16[2,80,640]{2,1,0:T(8,128)(2,1)S(1)}, u32[]{:S(2)}, u32[]{:S(2)}) collective-permute-start(bf16[2,80,640]{2,1,0:T(8,128)(2,1)S(1)} %pad_maximum_fusion.1.l0), channel_id=1, source_target_pairs={{0,64},{1,65},{2,66},{3,67},{4,68},{5,69},{6,70},{7,71},{32,96},{3... | collective-permute-start | bytes 614408 | tf_op jit(solution)/shard_map/points/ppermute | solution.py:52
  147.1 1.3 collective-permute-start.22
  (8 other events, 187.7 us)

commit v10 on v9

--- a/solution.py
+++ b/solution.py
@@ -133,13 +133,19 @@
         chip_rows = lax.optimization_barrier(chip_rows)
     with jax.named_scope("basis_plane"):
         plane = along(False, True)
+        near = send(line, plane(DOWN)), send(line, plane(UP))
+        shared = [fetched] + [send(fetched, CROSS(step)) for step in (DOWN, TWO, UP)]
+    with jax.named_scope("projected"):
+        project = lambda unit: nt(unit, chip_rows).astype(BF)
+        near_parts = [project(unit) for unit in near]
+        *shared, near_parts[0], near_parts[1] = lax.optimization_barrier((*shared, *near_parts))
         two = jnp.zeros((4, width, depth), BF)
-        for step, perm in ((0, None), (1, CROSS(DOWN)), (3, CROSS(UP)), (2, CROSS(TWO))):
-            piece = fetched if perm is None else send(fetched, perm)
-            two = lax.dynamic_update_index_in_dim(two, piece, (x + step) % 4, 0)
-        units = line, send(line, plane(DOWN)), two.reshape(4 * width, depth), send(line, plane(UP))
-    with jax.named_scope("projected"):
-        parts = [unroll(nt(u, chip_rows).astype(BF).reshape(4, width, -1), first) for u in units]
+        for offset_x, piece in enumerate(shared):
+            two = lax.dynamic_update_index_in_dim(two, piece, (x + offset_x) % 4, 0)
+        two = two.reshape(4 * width, depth)
+        units = line, near[0], two, near[1]
+        parts = project(line), near_parts[0], project(two), near_parts[1]
+        parts = [unroll(part.reshape(4, width, -1), first) for part in parts]
         blocks = unroll(jnp.stack(parts), second)
         blocks = jnp.where(core == 0, blocks, blocks.transpose(1, 0, 2, 3)).reshape(16, width, -1)
     with jax.named_scope("projected_exchange"):

time: 149 us -> 154 us (1.034)
  blocking collectives: 13.9 us -> 21.5 us
  waiting for transfers between devices: 71.4 us -> 64 us
  matrix products: 11.7 us -> 17.9 us
  local copies, waits for them, and re-layouts: 3.87 us -> 2.33 us
    ppermute x23, waiting for transfers between devices: 57.7 us -> 49.2 us  [send(): return lax.ppermute(value, AXES, perm)]
    all_to_all x1, blocking collectives: 13.9 us -> 21.5 us  [shards(): chosen = lax.all_to_all(ordered, 'pt', 0, 0, tiled=True)]
    dot_general x8, matrix products: 9.74 us -> 16 us  [nt(): lax.dot_general(a, b, (((1,), (1,)), ((), ())), preferred_element_type=F32)]
    unnamed x21 -> x11, local copies, waits for them, and re-layouts: 2.37 us -> 0.82 us
  transfers between devices with their start and end apart: 24 -> 24, of which waited for: 16 -> 14; matrix products, arithmetic and copies ran while one was open for 10% -> 12% of each run, Pallas kernels for 0% -> 0%
where the time goes in v10:
time: 154 us
  waiting for transfers between devices  64 us (42%)
  starting transfers between devices  37.3 us (24%)
  blocking collectives  21.5 us (14%)
  matrix products  17.9 us (12%)
  other arithmetic  9.55 us (6%)
  local copies, waits for them, and re-layouts  2.33 us (2%)
    ppermute x23, waiting for transfers between devices, send(): return lax.ppermute(value, AXES, perm)  49.2 us
    ppermute x23, starting transfers between devices, send(): return lax.ppermute(value, AXES, perm)  33.8 us
    all_to_all x1, blocking collectives, shards(): chosen = lax.all_to_all(ordered, 'pt', 0, 0, tiled=True)  21.5 us
    dot_general x8, matrix products, nt(): lax.dot_general(a, b, (((1,), (1,)), ((), ())), preferred_element_type=F32)  16 us
    all_to_all x1, waiting for transfers between devices, shards(): lax.all_to_all(blocks, 'pan', 0, 0, axis_index_groups=CHIPS, tiled=True)  14.7 us
    select_n x1, other arithmetic, shards(): jnp.where(core == 0, jnp.concatenate([rows, other_rows], 0), jnp.concaten...  5 us
    all_to_all x1, starting transfers between devices, shards(): lax.all_to_all(blocks, 'pan', 0, 0, axis_index_groups=CHIPS, tiled=True)  3.57 us
  transfers between devices with their start and end apart: 24, of which 14 were waited for; matrix products, arithmetic and copies ran while one was open for 12% of the time, Pallas kernels for 0%

profile of v10, /device:TPU:1, one launch (start us, length us, event | category | flops | bytes accessed | tf_op | source)
XLA Modules:
  0.0 153.7 jit_solution(7468170720117707072)
XLA Ops:
  0.0 3.2 %collective-permute-start.4 = (bf16[192,6144]{1,0:T(8,128)(2,1)}, bf16[192,6144]{1,0:T(8,128)(2,1)}, u32[]{:S(2)}, u32[]{:S(2)}) collective-permute-start(bf16[192,6144]{1,0:T(8,128)(2,1)} %bitcast.85), channel_id=1, source_target_pairs={{0,1},{1,0},{2,3},{3,2},{4,5},{5,4},{6,7},{7,6},{32,33},{33,32},{3... | collective-permute-start | bytes 7077896 | tf_op jit(solution)/shard_map/rows_pair/ppermute | solution.py:52
  5.3 3.0 %collective-permute-start.3 = (bf16[40,6144]{1,0:T(8,128)(2,1)}, bf16[40,6144]{1,0:T(8,128)(2,1)S(1)}, u32[]{:S(2)}, u32[]{:S(2)}) collective-permute-start(bf16[40,6144]{1,0:T(8,128)(2,1)} %bitcast.103), channel_id=1, source_target_pairs={{0,16},{1,5},{2,18},{3,39},{4,20},{5,33},{6,22},{7,3},{32,48},{33,... | collective-permute-start | bytes 1474568 | tf_op jit(solution)/shard_map/rows_pair/ppermute | solution.py:52
  11.4 2.5 %collective-permute-done.1 = bf16[40,6144]{1,0:T(8,128)(2,1)S(1)} collective-permute-done((bf16[40,6144]{1,0:T(8,128)(2,1)}, bf16[40,6144]{1,0:T(8,128)(2,1)S(1)}, u32[]{:S(2)}, u32[]{:S(2)}) %collective-permute-start.1) | collective-permute-done | bytes 491552 | tf_op jit(solution)/shard_map/basis_line/ppermute | solution.py:52
  14.0 9.7 %collective-permute-done.2 = bf16[40,6144]{1,0:T(8,128)(2,1)} collective-permute-done((bf16[40,6144]{1,0:T(8,128)(2,1)}, bf16[40,6144]{1,0:T(8,128)(2,1)}, u32[]{:S(2)}, u32[]{:S(2)}) %collective-permute-start.2) | collective-permute-done | bytes 491552 | tf_op jit(solution)/shard_map/basis_line/ppermute | solution.py:52
  25.1 2.4 %collective-permute-start.9 = (bf16[160,6144]{1,0:T(8,128)(2,1)S(1)}, bf16[160,6144]{1,0:T(8,128)(2,1)}, u32[]{:S(2)}, u32[]{:S(2)}) collective-permute-start(bf16[160,6144]{1,0:T(8,128)(2,1)S(1)} %pad_maximum_fusion), channel_id=1, source_target_pairs={{0,8},{1,3},{2,10},{3,5},{4,12},{5,7},{6,14},{7,33},{32,40},{33,35... | collective-permute-start | bytes 5898248 | tf_op jit(solution)/shard_map/basis_plane/ppermute | solution.py:52
  27.5 4.0 %collective-permute-start.8 = (bf16[160,6144]{1,0:T(8,128)(2,1)S(1)}, bf16[160,6144]{1,0:T(8,128)(2,1)}, u32[]{:S(2)}, u32[]{:S(2)}) collective-permute-start(bf16[160,6144]{1,0:T(8,128)(2,1)S(1)} %pad_maximum_fusion), channel_id=1, source_target_pairs={{0,24},{1,39},{2,26},{3,1},{4,28},{5,3},{6,30},{7,5},{32,56},{33,7... | collective-permute-start | bytes 5898248 | tf_op jit(solution)/shard_map/basis_plane/ppermute | solution.py:52
  31.5 2.5 %collective-permute-start.5 = (bf16[40,6144]{1,0:T(8,128)(2,1)S(1)}, bf16[40,6144]{1,0:T(8,128)(2,1)S(1)}, u32[]{:S(2)}, u32[]{:S(2)}) collective-permute-start(bf16[40,6144]{1,0:T(8,128)(2,1)S(1)} %collective-permute-done.3), channel_id=1, source_target_pairs={{0,192},{1,193},{2,194},{3,195},{4,196},{5,197},{6,198},{7,199},{3... | collective-permute-start | bytes 1474568 | tf_op jit(solution)/shard_map/basis_plane/ppermute | solution.py:52
  34.0 5.5 %collective-permute-start.6 = (bf16[40,6144]{1,0:T(8,128)(2,1)S(1)}, bf16[40,6144]{1,0:T(8,128)(2,1)S(1)}, u32[]{:S(2)}, u32[]{:S(2)}) collective-permute-start(bf16[40,6144]{1,0:T(8,128)(2,1)S(1)} %collective-permute-done.3), channel_id=1, source_target_pairs={{0,128},{1,129},{2,130},{3,131},{4,132},{5,133},{6,134},{7,135},{3... | collective-permute-start | bytes 1474568 | tf_op jit(solution)/shard_map/basis_plane/ppermute | solution.py:52
  40.4 5.0 %maximum_select_fusion = bf16[384,6144]{1,0:T(8,128)(2,1)S(1)} fusion(bf16[192,6144]{1,0:T(8,128)(2,1)} %collective-permute-done.4, bf16[192,6144]{1,0:T(8,128)(2,1)} %bitcast.86, pred[]{:T(512)S(6)} %eq.78), kind=kLoop, calls=%fused_computation.1 | loop fusion | flops 21233664 | bytes 9437185 | tf_op jit(solution)/shard_map/rows_pair/jit(_where)/select_n | solution.py:130
  47.1 6.7 %collective-permute-done.9 = bf16[160,6144]{1,0:T(8,128)(2,1)} collective-permute-done((bf16[160,6144]{1,0:T(8,128)(2,1)S(1)}, bf16[160,6144]{1,0:T(8,128)(2,1)}, u32[]{:S(2)}, u32[]{:S(2)}) %collective-permute-start.9) | collective-permute-done | bytes 1966112 | tf_op jit(solution)/shard_map/basis_plane/ppermute | solution.py:52
  53.8 3.2 %convolution_convert_fusion.2 = bf16[160,384]{1,0:T(8,128)(2,1)S(1)} fusion(bf16[160,6144]{1,0:T(8,128)(2,1)} %collective-permute-done.9, bf16[384,6144]{1,0:T(8,128)(2,1)S(1)} %maximum_select_fusion), kind=kOutput, calls=%fused_computation.13 | convolution fusion | flops 755036160 | bytes 6807552 | tf_op jit(solution)/shard_map/projected/dot_general | solution.py:63
  57.1 3.2 %convolution_convert_fusion.3 = bf16[160,384]{1,0:T(8,128)(2,1)S(1)} fusion(bf16[160,6144]{1,0:T(8,128)(2,1)} %collective-permute-done.8, bf16[384,6144]{1,0:T(8,128)(2,1)S(1)} %maximum_select_fusion), kind=kOutput, calls=%fused_computation.14 | convolution fusion | flops 755036160 | bytes 6807552 | tf_op jit(solution)/shard_map/projected/dot_general | solution.py:63
  63.9 3.6 %all-to-all-start = ((bf16[16,40,384]{2,1,0:T(8,128)(2,1)}), bf16[16,40,384]{2,1,0:T(8,128)(2,1)S(1)}, u32[]{:S(2)}, u32[]{:S(2)}) async-start(bf16[16,40,384]{2,1,0:T(8,128)(2,1)} %bitcast.19), calls=%async_computation | async-start | bytes 983040 | tf_op jit(solution)/shard_map/projected_exchange/all_to_all | solution.py:152
  67.5 14.7 %all-to-all-done = bf16[16,40,384]{2,1,0:T(8,128)(2,1)S(1)} async-done(((bf16[16,40,384]{2,1,0:T(8,128)(2,1)}), bf16[16,40,384]{2,1,0:T(8,128)(2,1)S(1)}, u32[]{:S(2)}, u32[]{:S(2)}) %all-to-all-start) | async-done | bytes 491552 | tf_op jit(solution)/shard_map/projected_exchange/all_to_all | solution.py:152
  82.3 2.0 %collective-permute-start.10 = (bf16[40,6144]{1,0:T(8,128)(2,1)S(1)}, bf16[40,6144]{1,0:T(8,128)(2,1)S(1)}, u32[]{:S(2)}, u32[]{:S(2)}) collective-permute-start(bf16[40,6144]{1,0:T(8,128)(2,1)S(1)} %bitcast.88), channel_id=1, source_target_pairs={{0,1},{1,0},{2,3},{3,2},{4,5},{5,4},{6,7},{7,6},{32,33},{33,32},{3... | collective-permute-start | bytes 1474568 | tf_op jit(solution)/shard_map/projected_exchange/ppermute | solution.py:52
  87.4 2.3 %convolution_convert_fusion.7 = bf16[80,160]{1,0:T(8,128)(2,1)S(1)} fusion(bf16[80,6144]{1,0:T(8,128)(2,1)S(1)} %constant_dynamic-update-slice_fusion, bf16[160,6144]{1,0:T(8,128)(2,1)} %collective-permute-done.8), kind=kOutput, calls=%fused_computation.19 | convolution fusion | flops 157299200 | bytes 2974720 | tf_op jit(solution)/shard_map/channel/dot_general | solution.py:63
  89.7 2.3 %convolution_convert_fusion.5 = bf16[80,160]{1,0:T(8,128)(2,1)S(1)} fusion(bf16[80,6144]{1,0:T(8,128)(2,1)S(1)} %constant_dynamic-update-slice_fusion, bf16[160,6144]{1,0:T(8,128)(2,1)} %collective-permute-done.9), kind=kOutput, calls=%fused_computation.17 | convolution fusion | flops 157299200 | bytes 2974720 | tf_op jit(solution)/shard_map/channel/dot_general | solution.py:63
  94.5 21.5 %all_to_all.10 = bf16[8,40,160]{2,1,0:T(8,128)(2,1)S(1)} all-to-all(bf16[8,40,160]{2,1,0:T(8,128)(2,1)S(1)} %bitcast.98), channel_id=1, replica_groups=mesh['pt'=8,'pan'=32] {'pt'}, dimensions={0} | all-to-all | bytes 204800 | tf_op jit(solution)/shard_map/columns_exchange/all_to_all | solution.py:167
  118.2 1.9 %collective-permute-done.12 = bf16[40,1280]{1,0:T(8,128)(2,1)S(1)} collective-permute-done((bf16[40,1280]{1,0:T(8,128)(2,1)S(1)}, bf16[40,1280]{1,0:T(8,128)(2,1)S(1)}, u32[]{:S(2)}, u32[]{:S(2)}) %collective-permute-start.12) | collective-permute-done | bytes 102432 | tf_op jit(solution)/shard_map/mixed_line/ppermute | solution.py:52
  122.4 5.4 %collective-permute-done.13 = bf16[80,640]{1,0:T(8,128)(2,1)S(1)} collective-permute-done((bf16[80,640]{1,0:T(8,128)(2,1)S(1)}, bf16[80,640]{1,0:T(8,128)(2,1)S(1)}, u32[]{:S(2)}, u32[]{:S(2)}) %collective-permute-start.13) | collective-permute-done | bytes 102432 | tf_op jit(solution)/shard_map/mixed_line/ppermute | solution.py:52
  129.1 2.4 %collective-permute-start.20 = (bf16[160,1280]{1,0:T(8,128)(2,1)S(1)}, bf16[160,1280]{1,0:T(8,128)(2,1)S(1)}, u32[]{:S(2)}, u32[]{:S(2)}) collective-permute-start(bf16[160,1280]{1,0:T(8,128)(2,1)S(1)} %constant_dynamic-update-slice_fusion.2.m0), channel_id=1, source_target_pairs={{0,16},{1,5},{2,18},{3,7},{4,20},{5,1},{6,22},{7,3},{32,48},{33,37... | collective-permute-start | bytes 1228808 | tf_op jit(solution)/shard_map/mixed_plane/ppermute | solution.py:52
  133.1 4.7 %collective-permute-done.15.l2 = bf16[2,80,640]{2,1,0:T(8,128)(2,1)S(1)} collective-permute-done((bf16[2,80,640]{2,1,0:T(8,128)(2,1)S(1)}, bf16[2,80,640]{2,1,0:T(8,128)(2,1)S(1)}, u32[]{:S(2)}, u32[]{:S(2)}) %collective-permute-start.15) | collective-permute-done | bytes 204832 | tf_op jit(solution)/shard_map/points/ppermute | solution.py:52
  137.8 2.4 %collective-permute-done.16.l3 = bf16[2,80,640]{2,1,0:T(8,128)(2,1)S(1)} collective-permute-done((bf16[2,80,640]{2,1,0:T(8,128)(2,1)S(1)}, bf16[2,80,640]{2,1,0:T(8,128)(2,1)S(1)}, u32[]{:S(2)}, u32[]{:S(2)}) %collective-permute-start.16) | collective-permute-done | bytes 204832 | tf_op jit(solution)/shard_map/points/ppermute | solution.py:52
  140.2 10.8 %collective-permute-done.20.m2 = bf16[160,1280]{1,0:T(8,128)(2,1)S(1)} collective-permute-done((bf16[160,1280]{1,0:T(8,128)(2,1)S(1)}, bf16[160,1280]{1,0:T(8,128)(2,1)S(1)}, u32[]{:S(2)}, u32[]{:S(2)}) %collective-permute-start.20) | collective-permute-done | bytes 409632 | tf_op jit(solution)/shard_map/mixed_plane/ppermute | solution.py:52
  (85 shorter events, 28.3 us)
Async XLA Ops:
  0.0 25.1 %collective-permute-start.4 = (bf16[192,6144]{1,0:T(8,128)(2,1)}, bf16[192,6144]{1,0:T(8,128)(2,1)}, u32[]{:S(2)}, u32[]{:S(2)}) collective-permute-start(bf16[192,6144]{1,0:T(8,128)(2,1)} %bitcast.85), channel_id=1, source_target_pairs={{0,1},{1,0},{2,3},{3,2},{4,5},{5,4},{6,7},{7,6},{32,33},{33,32},{3... | collective-permute-start | bytes 7077896 | tf_op jit(solution)/shard_map/rows_pair/ppermute | solution.py:52
  3.2 8.2 %collective-permute-start = (bf16[40,6144]{1,0:T(8,128)(2,1)}, bf16[40,6144]{1,0:T(8,128)(2,1)S(1)}, u32[]{:S(2)}, u32[]{:S(2)}) collective-permute-start(bf16[40,6144]{1,0:T(8,128)(2,1)} %bitcast.100), channel_id=1, source_target_pairs={{0,38},{1,25},{2,0},{3,27},{4,2},{5,29},{6,4},{7,31},{32,6},{33,57... | collective-permute-start | bytes 1474568 | tf_op jit(solution)/shard_map/basis_line/ppermute | solution.py:52
  4.2 9.7 %collective-permute-start.1 = (bf16[40,6144]{1,0:T(8,128)(2,1)}, bf16[40,6144]{1,0:T(8,128)(2,1)S(1)}, u32[]{:S(2)}, u32[]{:S(2)}) collective-permute-start(bf16[40,6144]{1,0:T(8,128)(2,1)} %bitcast.101), channel_id=1, source_target_pairs={{0,4},{1,17},{2,38},{3,19},{4,32},{5,21},{6,2},{7,23},{32,36},{33,... | collective-permute-start | bytes 1474568 | tf_op jit(solution)/shard_map/basis_line/ppermute | solution.py:52
  4.6 19.0 %collective-permute-start.2 = (bf16[40,6144]{1,0:T(8,128)(2,1)}, bf16[40,6144]{1,0:T(8,128)(2,1)}, u32[]{:S(2)}, u32[]{:S(2)}) collective-permute-start(bf16[40,6144]{1,0:T(8,128)(2,1)} %bitcast.102), channel_id=1, source_target_pairs={{0,2},{1,9},{2,4},{3,11},{4,6},{5,13},{6,32},{7,15},{32,34},{33,41... | collective-permute-start | bytes 1474568 | tf_op jit(solution)/shard_map/basis_line/ppermute | solution.py:52
  5.3 19.8 %collective-permute-start.3 = (bf16[40,6144]{1,0:T(8,128)(2,1)}, bf16[40,6144]{1,0:T(8,128)(2,1)S(1)}, u32[]{:S(2)}, u32[]{:S(2)}) collective-permute-start(bf16[40,6144]{1,0:T(8,128)(2,1)} %bitcast.103), channel_id=1, source_target_pairs={{0,16},{1,5},{2,18},{3,39},{4,20},{5,33},{6,22},{7,3},{32,48},{33,... | collective-permute-start | bytes 1474568 | tf_op jit(solution)/shard_map/rows_pair/ppermute | solution.py:52
  25.1 28.7 %collective-permute-start.9 = (bf16[160,6144]{1,0:T(8,128)(2,1)S(1)}, bf16[160,6144]{1,0:T(8,128)(2,1)}, u32[]{:S(2)}, u32[]{:S(2)}) collective-permute-start(bf16[160,6144]{1,0:T(8,128)(2,1)S(1)} %pad_maximum_fusion), channel_id=1, source_target_pairs={{0,8},{1,3},{2,10},{3,5},{4,12},{5,7},{6,14},{7,33},{32,40},{33,35... | collective-permute-start | bytes 5898248 | tf_op jit(solution)/shard_map/basis_plane/ppermute | solution.py:52
  27.5 29.6 %collective-permute-start.8 = (bf16[160,6144]{1,0:T(8,128)(2,1)S(1)}, bf16[160,6144]{1,0:T(8,128)(2,1)}, u32[]{:S(2)}, u32[]{:S(2)}) collective-permute-start(bf16[160,6144]{1,0:T(8,128)(2,1)S(1)} %pad_maximum_fusion), channel_id=1, source_target_pairs={{0,24},{1,39},{2,26},{3,1},{4,28},{5,3},{6,30},{7,5},{32,56},{33,7... | collective-permute-start | bytes 5898248 | tf_op jit(solution)/shard_map/basis_plane/ppermute | solution.py:52
  31.5 28.8 %collective-permute-start.5 = (bf16[40,6144]{1,0:T(8,128)(2,1)S(1)}, bf16[40,6144]{1,0:T(8,128)(2,1)S(1)}, u32[]{:S(2)}, u32[]{:S(2)}) collective-permute-start(bf16[40,6144]{1,0:T(8,128)(2,1)S(1)} %collective-permute-done.3), channel_id=1, source_target_pairs={{0,192},{1,193},{2,194},{3,195},{4,196},{5,197},{6,198},{7,199},{3... | collective-permute-start | bytes 1474568 | tf_op jit(solution)/shard_map/basis_plane/ppermute | solution.py:52
  34.0 26.3 %collective-permute-start.6 = (bf16[40,6144]{1,0:T(8,128)(2,1)S(1)}, bf16[40,6144]{1,0:T(8,128)(2,1)S(1)}, u32[]{:S(2)}, u32[]{:S(2)}) collective-permute-start(bf16[40,6144]{1,0:T(8,128)(2,1)S(1)} %collective-permute-done.3), channel_id=1, source_target_pairs={{0,128},{1,129},{2,130},{3,131},{4,132},{5,133},{6,134},{7,135},{3... | collective-permute-start | bytes 1474568 | tf_op jit(solution)/shard_map/basis_plane/ppermute | solution.py:52
  39.5 20.8 %collective-permute-start.7 = (bf16[40,6144]{1,0:T(8,128)(2,1)S(1)}, bf16[40,6144]{1,0:T(8,128)(2,1)S(1)}, u32[]{:S(2)}, u32[]{:S(2)}) collective-permute-start(bf16[40,6144]{1,0:T(8,128)(2,1)S(1)} %collective-permute-done.3), channel_id=1, source_target_pairs={{0,64},{1,65},{2,66},{3,67},{4,68},{5,69},{6,70},{7,71},{32,96},{3... | collective-permute-start | bytes 1474568 | tf_op jit(solution)/shard_map/basis_plane/ppermute | solution.py:52
  63.9 18.4 %all-to-all-start = ((bf16[16,40,384]{2,1,0:T(8,128)(2,1)}), bf16[16,40,384]{2,1,0:T(8,128)(2,1)S(1)}, u32[]{:S(2)}, u32[]{:S(2)}) async-start(bf16[16,40,384]{2,1,0:T(8,128)(2,1)} %bitcast.19), calls=%async_computation | async-start | bytes 983040 | tf_op jit(solution)/shard_map/projected_exchange/all_to_all | solution.py:152
  82.3 3.5 %collective-permute-start.10 = (bf16[40,6144]{1,0:T(8,128)(2,1)S(1)}, bf16[40,6144]{1,0:T(8,128)(2,1)S(1)}, u32[]{:S(2)}, u32[]{:S(2)}) collective-permute-start(bf16[40,6144]{1,0:T(8,128)(2,1)S(1)} %bitcast.88), channel_id=1, source_target_pairs={{0,1},{1,0},{2,3},{3,2},{4,5},{5,4},{6,7},{7,6},{32,33},{33,32},{3... | collective-permute-start | bytes 1474568 | tf_op jit(solution)/shard_map/projected_exchange/ppermute | solution.py:52
  92.2 1.3 collective-permute-start.11
  116.5 3.6 %collective-permute-start.12 = (bf16[40,1280]{1,0:T(8,128)(2,1)S(1)}, bf16[40,1280]{1,0:T(8,128)(2,1)S(1)}, u32[]{:S(2)}, u32[]{:S(2)}) collective-permute-start(bf16[40,1280]{1,0:T(8,128)(2,1)S(1)} %reshape.267), channel_id=1, source_target_pairs={{0,6},{1,25},{2,0},{3,27},{4,2},{5,29},{6,4},{7,31},{32,38},{33,57... | collective-permute-start | bytes 307208 | tf_op jit(solution)/shard_map/mixed_line/ppermute | solution.py:52
  117.2 5.2 %collective-permute-start.17 = (bf16[40,1280]{1,0:T(8,128)(2,1)S(1)}, bf16[40,1280]{1,0:T(8,128)(2,1)S(1)}, u32[]{:S(2)}, u32[]{:S(2)}) collective-permute-start(bf16[40,1280]{1,0:T(8,128)(2,1)S(1)} %reshape.267), channel_id=1, source_target_pairs={{0,4},{1,17},{2,6},{3,19},{4,0},{5,21},{6,2},{7,23},{32,36},{33,49... | collective-permute-start | bytes 307208 | tf_op jit(solution)/shard_map/mixed_line/ppermute | solution.py:52
  117.5 11.2 %collective-permute-start.18 = (bf16[40,1280]{1,0:T(8,128)(2,1)S(1)}, bf16[40,1280]{1,0:T(8,128)(2,1)S(1)}, u32[]{:S(2)}, u32[]{:S(2)}) collective-permute-start(bf16[40,1280]{1,0:T(8,128)(2,1)S(1)} %reshape.267), channel_id=1, source_target_pairs={{0,2},{1,9},{2,4},{3,11},{4,6},{5,13},{6,0},{7,15},{32,34},{33,41}... | collective-permute-start | bytes 307208 | tf_op jit(solution)/shard_map/mixed_line/ppermute | solution.py:52
  120.1 7.8 %collective-permute-start.13 = (bf16[80,640]{1,0:T(8,128)(2,1)S(1)}, bf16[80,640]{1,0:T(8,128)(2,1)S(1)}, u32[]{:S(2)}, u32[]{:S(2)}) collective-permute-start(bf16[80,640]{1,0:T(8,128)(2,1)S(1)} %pad_maximum_fusion.2), channel_id=1, source_target_pairs={{0,32},{1,33},{2,34},{3,35},{4,36},{5,37},{6,38},{7,39},{32,0},{33... | collective-permute-start | bytes 307208 | tf_op jit(solution)/shard_map/mixed_line/ppermute | solution.py:52
  127.8 4.8 %collective-permute-start.14 = (bf16[2,80,640]{2,1,0:T(8,128)(2,1)S(1)}, bf16[2,80,640]{2,1,0:T(8,128)(2,1)S(1)}, u32[]{:S(2)}, u32[]{:S(2)}) collective-permute-start(bf16[2,80,640]{2,1,0:T(8,128)(2,1)S(1)} %pad_maximum_fusion.1.l0), channel_id=1, source_target_pairs={{0,192},{1,193},{2,194},{3,195},{4,196},{5,197},{6,198},{7,199},{3... | collective-permute-start | bytes 614408 | tf_op jit(solution)/shard_map/points/ppermute | solution.py:52
  128.7 11.5 %collective-permute-start.19 = (bf16[160,1280]{1,0:T(8,128)(2,1)S(1)}, bf16[160,1280]{1,0:T(8,128)(2,1)S(1)}, u32[]{:S(2)}, u32[]{:S(2)}) collective-permute-start(bf16[160,1280]{1,0:T(8,128)(2,1)S(1)} %constant_dynamic-update-slice_fusion.2.m0), channel_id=1, source_target_pairs={{0,24},{1,7},{2,26},{3,1},{4,28},{5,3},{6,30},{7,5},{32,56},{33,39... | collective-permute-start | bytes 1228808 | tf_op jit(solution)/shard_map/mixed_plane/ppermute | solution.py:52
  129.1 21.9 %collective-permute-start.20 = (bf16[160,1280]{1,0:T(8,128)(2,1)S(1)}, bf16[160,1280]{1,0:T(8,128)(2,1)S(1)}, u32[]{:S(2)}, u32[]{:S(2)}) collective-permute-start(bf16[160,1280]{1,0:T(8,128)(2,1)S(1)} %constant_dynamic-update-slice_fusion.2.m0), channel_id=1, source_target_pairs={{0,16},{1,5},{2,18},{3,7},{4,20},{5,1},{6,22},{7,3},{32,48},{33,37... | collective-permute-start | bytes 1228808 | tf_op jit(solution)/shard_map/mixed_plane/ppermute | solution.py:52
  131.6 19.4 %collective-permute-start.21 = (bf16[160,1280]{1,0:T(8,128)(2,1)S(1)}, bf16[160,1280]{1,0:T(8,128)(2,1)S(1)}, u32[]{:S(2)}, u32[]{:S(2)}) collective-permute-start(bf16[160,1280]{1,0:T(8,128)(2,1)S(1)} %constant_dynamic-update-slice_fusion.2.m0), channel_id=1, source_target_pairs={{0,8},{1,3},{2,10},{3,5},{4,12},{5,7},{6,14},{7,1},{32,40},{33,35}... | collective-permute-start | bytes 1228808 | tf_op jit(solution)/shard_map/mixed_plane/ppermute | solution.py:52
  131.6 6.2 %collective-permute-start.15 = (bf16[2,80,640]{2,1,0:T(8,128)(2,1)S(1)}, bf16[2,80,640]{2,1,0:T(8,128)(2,1)S(1)}, u32[]{:S(2)}, u32[]{:S(2)}) collective-permute-start(bf16[2,80,640]{2,1,0:T(8,128)(2,1)S(1)} %pad_maximum_fusion.1.l0), channel_id=1, source_target_pairs={{0,128},{1,129},{2,130},{3,131},{4,132},{5,133},{6,134},{7,135},{3... | collective-permute-start | bytes 614408 | tf_op jit(solution)/shard_map/points/ppermute | solution.py:52
  132.6 7.6 %collective-permute-start.16 = (bf16[2,80,640]{2,1,0:T(8,128)(2,1)S(1)}, bf16[2,80,640]{2,1,0:T(8,128)(2,1)S(1)}, u32[]{:S(2)}, u32[]{:S(2)}) collective-permute-start(bf16[2,80,640]{2,1,0:T(8,128)(2,1)S(1)} %pad_maximum_fusion.1.l0), channel_id=1, source_target_pairs={{0,64},{1,65},{2,66},{3,67},{4,68},{5,69},{6,70},{7,71},{32,96},{3... | collective-permute-start | bytes 614408 | tf_op jit(solution)/shard_map/points/ppermute | solution.py:52
  151.7 1.3 collective-permute-start.22
  (3 other events, 155.8 us)
